TPU v7x, 256 devices: a whole 4x4x8 slice. The times are simulated.
256 devices in a mesh: gx: 8 (over y, core), gy: 32 (over z, x).
Axes of the slice: x: 4, y: 4, z: 8, core: 2. Of those that a mesh axis runs over, the one named last changes fastest.
Arguments:
- mesh_element_matrix: bfloat16 [262144, 256], P(('gx', 'gy')), may hold values from -12 to 12
- occupied_element_tally: int32 [256], P(('gx', 'gy')), may hold values from 1 to 1024, as said below
- transfer_assignment: int32 [256, 8], P(('gx', 'gy')), may hold values from -1 to 31, as said below
- adjoint_output: bfloat16 [131072, 256], P(('gx', 'gy')), may hold values from -6 to 6
- normalizer_factor: float32 [256], replicated, may hold values from 0.5 to 1.5
- entrance_matrix: bfloat16 [256, 512], replicated, may hold values from -0.375 to 0.375
- portion_matrix: bfloat16 [32, 64], replicated, may hold values from -80 to 80
- softness_matrix: bfloat16 [32], replicated, may hold values from -0.59765625 to 0.59765625
- default_softness: float32 [8], replicated, may hold values from 0.3 to 1.2
- request_matrix: float32 [32, 32], replicated, may hold values from -10 to 10
- lookup_matrix: float32 [32, 32], replicated, may hold values from -10 to 10
- content_matrix: float32 [32, 32], replicated, may hold values from -1 to 1
- exit_matrix: bfloat16 [256, 256], replicated, may hold values from -0.375 to 0.375
Outputs:
- result_bal: bfloat16 [131072, 256], P(('gx', 'gy'))
- cell_grad: bfloat16 [262144, 256], P(('gx', 'gy'))
- grad_in: float32 [256, 512], replicated
- grad_out: float32 [256, 256], replicated
- grad_slice: float32 [32, 64], replicated
Inputs may be any that keep to these rules, and one draw needn't show every extreme that they name: `occupied_element_tally`: every device holds at least one live cell in its first rows; in every gx row some device is full. transfer_assignment[p, s] is -1 exactly when block s of device p has no live row; otherwise it is a gy index in the gx row of p. No device sends more than 1 block to one device, none receives more than 4 blocks, and both bounds are reached in every draw.
All inputs are finite; a program needn't handle non-finite values.
Results may differ from a plain program's by a relative error of at most 0.015.
The roundings to bfloat16 on the way count: a program that leaves them out, or rounds other values in their place, can miss the bound.
Values may be sent and summed in bfloat16 or wider, within the bound.
No kernel may reach another device: no remote copies, remote signals or barrier semaphores. Data moves between devices by JAX's collectives and lax.ppermute only.
A program may use at most 64 MiB of HBM per device.

v0:
```python
import math

import jax
import jax.numpy as jnp
from jax import lax
from jax.sharding import PartitionSpec as P

C = 256
FOCUS_GROUPS = 8
GROUP_PARTITIONS = 64
GROUP_WIDTH = 32
BLK = 128
SIN = 8
SOUT = 4


norm_eps = 1e-05
slice_eps = 1e-05


def layer_norm(cells_rows, normalizer_factor):
    cells_f32 = cells_rows.astype(jnp.float32)
    row_mean = jnp.mean(cells_f32, axis=-1, keepdims=True)
    centered = cells_f32 - row_mean
    variance = jnp.mean(centered * centered, axis=-1, keepdims=True)
    inv_std = lax.rsqrt(variance + norm_eps)
    unit_rows = centered * inv_std
    standardized = (unit_rows * normalizer_factor[None, :]).astype(jnp.bfloat16)
    return (cells_f32, unit_rows, inv_std, standardized)


def portion_coefficients(
    standardized,
    entry_alive_flags,
    entrance_matrix,
    portion_matrix,
    softness_matrix,
    default_softness,
):
    entry_accumulated = standardized.shape[0]
    mapped_elements = jnp.dot(
        standardized, entrance_matrix, preferred_element_type=jnp.float32
    ).astype(jnp.bfloat16)
    mesh_entries = mapped_elements[:, :C].reshape(entry_accumulated, FOCUS_GROUPS, GROUP_WIDTH)
    interior_entries = mapped_elements[:, C:].reshape(entry_accumulated * FOCUS_GROUPS, GROUP_WIDTH)
    portion_affinity = jnp.dot(
        interior_entries, portion_matrix, preferred_element_type=jnp.float32
    ).reshape(entry_accumulated, FOCUS_GROUPS, GROUP_PARTITIONS)
    softness_presquash = jnp.dot(
        interior_entries, softness_matrix, preferred_element_type=jnp.float32
    ).reshape(entry_accumulated, FOCUS_GROUPS)
    group_softness = default_softness[None, :] + jax.nn.softplus(softness_presquash)
    rescaled_affinity = portion_affinity / group_softness[:, :, None]
    portion_chance = jax.nn.softmax(rescaled_affinity, axis=-1)
    portion_lowprecision = (portion_chance * entry_alive_flags[:, None, None]).astype(jnp.bfloat16)
    return (
        mesh_entries,
        interior_entries,
        softness_presquash,
        group_softness,
        rescaled_affinity,
        portion_chance,
        portion_lowprecision,
    )


def token_forward(numerator, denominator, request_matrix, lookup_matrix, content_matrix):
    upper_value = lax.Precision.HIGHEST
    slice_tokens = numerator / (denominator[:, :, None] + slice_eps)
    query_rows = jnp.einsum("woy,yu->wou", slice_tokens, request_matrix, precision=upper_value)
    projected_keys = jnp.einsum("woy,yu->wou", slice_tokens, lookup_matrix, precision=upper_value)
    projected_values = jnp.einsum(
        "woy,yu->wou", slice_tokens, content_matrix, precision=upper_value
    )
    scores = jnp.einsum(
        "hme,hne->hmn", query_rows, projected_keys, precision=upper_value
    ) * GROUP_WIDTH ** (-0.5)
    attention = jax.nn.softmax(scores, axis=-1)
    mixed = jnp.einsum("hmn,hne->hme", attention, projected_values, precision=upper_value)
    return (
        slice_tokens,
        query_rows,
        projected_keys,
        projected_values,
        attention,
        mixed.astype(jnp.bfloat16),
    )


def token_backward(
    tok_grad_sum, token_state, denominator, request_matrix, lookup_matrix, content_matrix
):
    upper_value = lax.Precision.HIGHEST
    slice_tokens, query_rows, projected_keys, projected_values, attention, mixed_half_float = (
        token_state
    )
    grad_att = jnp.einsum("hme,hne->hmn", tok_grad_sum, projected_values, precision=upper_value)
    value_gradient = jnp.einsum("hmn,hme->hne", attention, tok_grad_sum, precision=upper_value)
    grad_scores = (
        attention
        * (grad_att - jnp.sum(attention * grad_att, axis=-1, keepdims=True))
        * GROUP_WIDTH ** (-0.5)
    )
    query_gradient = jnp.einsum("hmn,hne->hme", grad_scores, projected_keys, precision=upper_value)
    key_gradient = jnp.einsum("hmn,hme->hne", grad_scores, query_rows, precision=upper_value)
    token_gradient = jnp.einsum(
        "fgs,js->fgj", query_gradient, request_matrix, precision=upper_value
    )
    token_gradient = token_gradient + jnp.einsum(
        "fgs,js->fgj", key_gradient, lookup_matrix, precision=upper_value
    )
    token_gradient = token_gradient + jnp.einsum(
        "fgs,js->fgj", value_gradient, content_matrix, precision=upper_value
    )
    inverse = 1.0 / (denominator + slice_eps)
    numerator_gradient = (token_gradient * inverse[:, :, None]).astype(jnp.bfloat16)
    denominator_gradient = -jnp.sum(token_gradient * slice_tokens, axis=-1) * inverse
    return (numerator_gradient, denominator_gradient)


def forward_rows(cells_rows, entry_alive_flags, weights_all):
    (
        normalizer_factor,
        entrance_matrix,
        portion_matrix,
        softness_matrix,
        default_softness,
        request_matrix,
        lookup_matrix,
        content_matrix,
        exit_matrix,
    ) = weights_all
    entry_accumulated = cells_rows.shape[0]
    cells_f32, unit_rows, inv_std, standardized = layer_norm(cells_rows, normalizer_factor)
    assignment_chance = portion_coefficients(
        standardized,
        entry_alive_flags,
        entrance_matrix,
        portion_matrix,
        softness_matrix,
        default_softness,
    )
    mesh_entries = assignment_chance[0]
    portion_lowprecision = assignment_chance[6]
    numerator_partial = jnp.einsum(
        "ajq,ajs->jqs", portion_lowprecision, mesh_entries, preferred_element_type=jnp.float32
    )
    denom_part = jnp.sum(portion_lowprecision, axis=0, dtype=jnp.float32)
    numerator, denominator = lax.psum((numerator_partial, denom_part), ("gx", "gy"))
    token_state = token_forward(
        numerator, denominator, request_matrix, lookup_matrix, content_matrix
    )
    deslice_f32 = jnp.einsum(
        "ngx,gxw->ngw", portion_lowprecision, token_state[5], preferred_element_type=jnp.float32
    )
    deslice_bf = deslice_f32.astype(jnp.bfloat16).reshape(entry_accumulated, C)
    branch_out = jnp.dot(deslice_bf, exit_matrix, preferred_element_type=jnp.float32)
    result_rows = (entry_alive_flags[:, None] * (cells_f32 + branch_out)).astype(jnp.bfloat16)
    saved = (
        unit_rows,
        inv_std,
        standardized,
        assignment_chance,
        denominator,
        token_state,
        deslice_bf,
    )
    return (result_rows, saved)


def backward_rows(cot_rows, entry_alive_flags, saved, weights_all, grad_scale):
    (
        normalizer_factor,
        entrance_matrix,
        portion_matrix,
        softness_matrix,
        default_softness,
        request_matrix,
        lookup_matrix,
        content_matrix,
        exit_matrix,
    ) = weights_all
    unit_rows, inv_std, standardized, assignment_chance, denominator, token_state, deslice_bf = (
        saved
    )
    (
        mesh_entries,
        interior_entries,
        softness_presquash,
        group_softness,
        rescaled_affinity,
        portion_chance,
        portion_lowprecision,
    ) = assignment_chance
    mixed_half_float = token_state[5]
    entry_accumulated = cot_rows.shape[0]
    contract_rows = (((0,), (0,)), ((), ()))
    contract_cols = (((1,), (1,)), ((), ()))
    masked_cot = jnp.where(entry_alive_flags[:, None] > 0, cot_rows, jnp.zeros_like(cot_rows))
    out_grad_part = lax.dot_general(
        deslice_bf, masked_cot, contract_rows, preferred_element_type=jnp.float32
    )
    unslice_gradient = lax.dot_general(
        masked_cot, exit_matrix, contract_cols, preferred_element_type=jnp.float32
    )
    unslice_gradient = unslice_gradient.astype(jnp.bfloat16).reshape(
        entry_accumulated, FOCUS_GROUPS, GROUP_WIDTH
    )
    token_gradient_partial = jnp.einsum(
        "ajq,ajs->jqs", portion_lowprecision, unslice_gradient, preferred_element_type=jnp.float32
    )
    probability_gradient_first = jnp.einsum(
        "bco,cfo->bcf", unslice_gradient, mixed_half_float, preferred_element_type=jnp.float32
    )
    tok_grad_sum, out_grad_sum = lax.psum((token_gradient_partial, out_grad_part), ("gx", "gy"))
    numerator_gradient, denominator_gradient = token_backward(
        tok_grad_sum, token_state, denominator, request_matrix, lookup_matrix, content_matrix
    )
    probability_gradient = (
        probability_gradient_first
        + jnp.einsum(
            "bco,cfo->bcf", mesh_entries, numerator_gradient, preferred_element_type=jnp.float32
        )
        + denominator_gradient[None, :, :]
    )
    probability_gradient = probability_gradient * entry_alive_flags[:, None, None]
    feature_gradient = jnp.einsum(
        "ngx,gxw->ngw", portion_lowprecision, numerator_gradient, preferred_element_type=jnp.float32
    )
    rescaled_adjoint = portion_chance * (
        probability_gradient
        - jnp.sum(portion_chance * probability_gradient, axis=-1, keepdims=True)
    )
    affinity_adjoint = (
        (rescaled_adjoint / group_softness[:, :, None])
        .astype(jnp.bfloat16)
        .reshape(entry_accumulated * FOCUS_GROUPS, GROUP_PARTITIONS)
    )
    softness_adjoint = (
        -jnp.sum(rescaled_adjoint * rescaled_affinity, axis=-1)
        / group_softness
        * jax.nn.sigmoid(softness_presquash)
    )
    adjoint_between = lax.dot_general(
        affinity_adjoint, portion_matrix, contract_cols, preferred_element_type=jnp.float32
    )
    adjoint_between = (
        adjoint_between
        + softness_adjoint.reshape(entry_accumulated * FOCUS_GROUPS, 1)
        * softness_matrix.astype(jnp.float32)[None, :]
    )
    slice_grad_part = lax.dot_general(
        interior_entries, affinity_adjoint, contract_rows, preferred_element_type=jnp.float32
    )
    grad_proj = jnp.concatenate(
        [
            feature_gradient.reshape(entry_accumulated, C),
            adjoint_between.reshape(entry_accumulated, C),
        ],
        axis=1,
    ).astype(jnp.bfloat16)
    in_grad_part = lax.dot_general(
        standardized, grad_proj, contract_rows, preferred_element_type=jnp.float32
    )
    grad_normed = lax.dot_general(
        grad_proj, entrance_matrix, contract_cols, preferred_element_type=jnp.float32
    )
    grad_unit = grad_normed * normalizer_factor[None, :]
    grad_norm_in = inv_std * (
        grad_unit
        - jnp.mean(grad_unit, axis=-1, keepdims=True)
        - unit_rows * jnp.mean(grad_unit * unit_rows, axis=-1, keepdims=True)
    )
    cell_grad = (masked_cot.astype(jnp.float32) + grad_norm_in).astype(jnp.bfloat16)
    in_grad_sum, slice_grad_sum = lax.psum((in_grad_part, slice_grad_part), ("gx", "gy"))
    return (
        cell_grad,
        in_grad_sum * grad_scale,
        out_grad_sum * grad_scale,
        slice_grad_sum * grad_scale,
    )


def pick_blocks(blocks, chosen_rows):
    return jnp.take(blocks, chosen_rows, axis=0, mode="fill", fill_value=0)


def arrival_maps(arrived_rows, send_slots):
    arrived_live = (arrived_rows > 0).astype(jnp.int32)
    arrival_slot = jnp.cumsum(arrived_live) - 1
    home_slot = jnp.where(arrived_live > 0, arrival_slot, SOUT)
    slot_index = jnp.arange(SOUT, dtype=jnp.int32)
    slot_match = home_slot[None, :] == slot_index[:, None]
    spot_index = jnp.arange(send_slots, dtype=jnp.int32)
    arrival_pick = jnp.sum(jnp.where(slot_match, spot_index[None, :], 0), axis=1)
    arrival_pick = arrival_pick + jnp.where(jnp.any(slot_match, axis=1), 0, send_slots)
    return (home_slot, arrival_pick)


def shards(
    mesh_element_matrix,
    occupied_element_tally,
    transfer_assignment,
    adjoint_output,
    normalizer_factor,
    entrance_matrix,
    portion_matrix,
    softness_matrix,
    default_softness,
    request_matrix,
    lookup_matrix,
    content_matrix,
    exit_matrix,
):
    weights_all = (
        normalizer_factor,
        entrance_matrix,
        portion_matrix,
        softness_matrix,
        default_softness,
        request_matrix,
        lookup_matrix,
        content_matrix,
        exit_matrix,
    )
    gy_count = lax.axis_size("gy")
    per_peer = (SIN + gy_count - 1) // gy_count
    send_slots = gy_count * per_peer
    live_count = occupied_element_tally[0]
    target_gy = transfer_assignment[0]
    block_index = jnp.arange(SIN, dtype=jnp.int32)
    block_alive = target_gy >= 0
    earlier_same = (target_gy[:, None] == target_gy[None, :]) & (
        block_index[None, :] < block_index[:, None]
    )
    block_rank = jnp.sum(earlier_same.astype(jnp.int32), axis=1)
    send_spot = jnp.where(block_alive, target_gy * per_peer + block_rank, send_slots)
    spot_index = jnp.arange(send_slots, dtype=jnp.int32)
    spot_match = send_spot[None, :] == spot_index[:, None]
    source_block = jnp.sum(jnp.where(spot_match, block_index[None, :], 0), axis=1)
    source_block = source_block + jnp.where(jnp.any(spot_match, axis=1), 0, SIN)
    block_rows = jnp.clip(live_count - block_index * BLK, 0, BLK)
    send_rows = jnp.take(block_rows, source_block, mode="fill", fill_value=0)
    rows_in = SIN * BLK
    in_mask = (jnp.arange(rows_in, dtype=jnp.int32) < live_count).astype(jnp.float32)
    grad_scale = 1.0 / math.sqrt(lax.axis_size("gx") * gy_count * rows_in)
    result_rows, saved = forward_rows(mesh_element_matrix, in_mask, weights_all)
    result_send = pick_blocks(result_rows.reshape(SIN, BLK, C), source_block)
    result_recv, arrived_rows = (
        lax.all_to_all(result_send, "gy", split_axis=0, concat_axis=0, tiled=True),
        lax.all_to_all(send_rows, "gy", split_axis=0, concat_axis=0, tiled=True),
    )
    home_slot, arrival_pick = arrival_maps(arrived_rows, send_slots)
    result_bal = pick_blocks(result_recv, arrival_pick).reshape(SOUT * BLK, C)
    cot_back = pick_blocks(adjoint_output.reshape(SOUT, BLK, C), home_slot)
    cot_home = lax.all_to_all(cot_back, "gy", split_axis=0, concat_axis=0, tiled=True)
    cot_rows = pick_blocks(cot_home, send_spot).reshape(rows_in, C)
    cell_grad, grad_in, grad_out, grad_slice = backward_rows(
        cot_rows, in_mask, saved, weights_all, grad_scale
    )
    return (result_bal, cell_grad, grad_in, grad_out, grad_slice)


def solution(mesh):
    placed = (
        P(("gx", "gy"), None),
        P(("gx", "gy")),
        P(("gx", "gy"), None),
        P(("gx", "gy"), None),
        P(),
        P(),
        P(),
        P(),
        P(),
        P(),
        P(),
        P(),
        P(),
    )
    return jax.shard_map(
        shards,
        mesh=mesh,
        in_specs=placed,
        out_specs=(P(("gx", "gy"), None), P(("gx", "gy"), None), P(), P(), P()),
        check_vma=False,
    )
```

profile of v0, /device:TPU:2, one launch (start us, length us, event | category | flops | bytes accessed | tf_op | source)
XLA Modules:
  0.0 725.5 jit_solution(6871990733664742684)
XLA Ops:
  7.2 0.9 convert_reduce_fusion.2
  8.1 0.7 fusion.54
  9.8 0.7 gather_fusion
  10.6 0.7 copy.66
  11.3 11.6 %all-to-all-start = ((s32[32,1,1]{2,1,0:T(1,128)}), s32[32,1,1]{2,1,0:T(1,128)S(1)}, u32[]{:S(2)}, u32[]{:S(2)}) async-start(s32[32,1,1]{2,1,0:T(1,128)} %copy.66), calls=%async_computation | async-start | bytes 32768 | tf_op jit(solution)/shard_map/all_to_all | solution.py:351
  22.9 1.3 convert_reduce_fusion.1
  24.1 1.4 fusion.20
  25.6 1.9 convolution_convert_fusion
  27.5 0.9 fusion.73
  28.4 2.8 fusion.56
  31.9 2.9 copy.83
  34.7 1.9 reshape.389
  37.5 0.7 gather_fusion.3
  38.2 1.6 broadcast_select_fusion
  39.8 10.0 %all-to-all-start.2 = ((bf16[32,128,256]{2,1,0:T(8,128)(2,1)}), bf16[32,128,256]{2,1,0:T(8,128)(2,1)}, u32[]{:S(2)}, u32[]{:S(2)}) async-start(bf16[32,128,256]{2,1,0:T(8,128)(2,1)} %broadcast_select_fusion), calls=%async_computation.2 | async-start | bytes 4194304 | tf_op jit(solution)/shard_map/all_to_all | solution.py:356
  50.6 2.9 fusion.74
  53.6 0.6 copy-done.12
  54.5 86.7 %psum.43 = f32[8,64]{1,0:T(8,128)S(1)} all-reduce(f32[8,64]{1,0:T(8,128)S(1)} %get-tuple-element.13), channel_id=1, replica_groups=mesh['gx'=8,'gy'=32] {'gx','gy'}, use_global_device_ids=true, to_apply=%region_12.13 | all-reduce | flops 512 | bytes 4096 | tf_op jit(solution)/shard_map/psum | solution.py:149
  142.4 0.7 fusion.58
  143.7 0.7 compare_and_fusion.1
  144.4 1.2 compare_and_fusion.2
  145.6 0.6 broadcast_bitcast_fusion
  146.2 2.1 fusion.76
  148.3 0.8 fusion.53
  149.1 0.8 select_reduce_fusion.1
  149.9 0.6 pad_clamp_fusion.2
  151.1 3.1 gather_fusion.4
  154.2 1.4 fusion.23
  156.0 0.8 copy-done.3
  156.7 1.1 fusion.77
  157.8 2.1 select_select_fusion
  159.9 246.6 %all-reduce.7.cloned.1.call-done = (f32[8,64,32]{1,2,0:T(8,128)}, f32[8,64,32]{1,2,0:T(8,128)}) async-done(((f32[8,64,32]{1,2,0:T(8,128)}, f32[8,64,32]{1,2,0:T(8,128)}), (f32[8,64,32]{1,2,0:T(8,128)}, f32[8,64,32]{1,2,0:T(8,128)})) %all-reduce.7.cloned.1.call-update) | async-done | bytes 131088 | tf_op jit(solution)/shard_map/psum | solution.py:149
  406.5 1.2 fusion.43
  407.8 1.2 fusion.47
  409.0 1.2 fusion.40
  410.2 0.6 fusion.75
  411.5 0.6 multiply_reduce_fusion.1
  413.6 1.8 fusion.78
  415.4 1.1 convolution_convert_fusion.3
  417.3 0.6 broadcast_divide_fusion.2
  417.9 1.1 convolution_convert_fusion.1
  419.0 2.1 copy.80
  421.1 1.6 fusion.8
  422.7 2.2 gather_fusion.1
  424.9 3.2 broadcast_select_fusion.1
  428.1 8.8 %all-to-all-start.1 = ((bf16[32,128,256]{2,1,0:T(8,128)(2,1)}), bf16[32,128,256]{2,1,0:T(8,128)(2,1)}, u32[]{:S(2)}, u32[]{:S(2)}) async-start(bf16[32,128,256]{2,1,0:T(8,128)(2,1)} %broadcast_select_fusion.1), calls=%async_computation.1 | async-start | bytes 4194304 | tf_op jit(solution)/shard_map/all_to_all | solution.py:350
  437.3 2.2 add_multiply_fusion
  439.6 0.7 multiply_reduce_fusion
  440.9 1.7 copy.77
  442.6 0.8 fusion.2
  443.5 1.7 copy.79
  445.2 3.1 reshape.388
  448.4 2.8 fusion.22
  451.2 1.0 fusion.79
  452.3 2.3 fusion.3
  454.6 77.3 %psum.47 = f32[32,64]{1,0:T(8,128)S(1)} all-reduce(f32[32,64]{1,0:T(8,128)S(1)} %fusion.3), channel_id=1, replica_groups=mesh['gx'=8,'gy'=32] {'gx','gy'}, use_global_device_ids=true, to_apply=%region_24.25 | all-reduce | flops 2048 | bytes 16384 | tf_op jit(solution)/shard_map/psum | solution.py:275
  531.8 0.6 broadcast_multiply_fusion.2
  532.4 1.9 fusion.72
  534.3 2.2 fusion.19
  536.6 175.5 %all-reduce.5.cloned.1.call-done = (f32[256,512]{1,0:T(8,128)}, f32[256,256]{1,0:T(8,128)}) async-done(((f32[256,512]{1,0:T(8,128)}, f32[256,256]{1,0:T(8,128)}), (f32[256,512]{1,0:T(8,128)}, f32[256,256]{1,0:T(8,128)})) %all-reduce.5.cloned.1.call-update) | async-done | bytes 786448 | tf_op jit(solution)/shard_map/psum | solution.py:275
  712.0 1.7 broadcast_multiply_fusion.1
  713.7 1.9 broadcast_multiply_fusion
  715.6 2.3 gather_fusion.2
  717.9 0.8 bitcast_select_fusion.1
  (132 shorter events, 9.6 us)
Async XLA Ops:
  7.2 30.4 %copy-start = (bf16[512,256]{1,0:T(8,128)(2,1)S(1)}, bf16[512,256]{1,0:T(8,128)(2,1)}, u32[]{:S(2)}) copy-start(bf16[512,256]{1,0:T(8,128)(2,1)} %param.16) | copy-start | bytes 786436
  8.1 0.8 copy-start.41
  8.8 19.5 %copy-start.37 = (pred[32]{0:T(512)(128)(4,1)}, pred[32]{0:T(512)(128)(4,1)S(1)}, u32[]{:S(2)}) copy-start(pred[32]{0:T(512)(128)(4,1)S(1)} %fusion.50) | copy-start | bytes 100
  8.9 19.4 %copy-start.38 = (s32[32]{0:T(128)}, s32[32]{0:T(128)S(1)}, u32[]{:S(2)}) copy-start(s32[32]{0:T(128)S(1)} %select_reduce_fusion) | copy-start | bytes 388
  9.2 19.2 %copy-start.27 = (s32[1024]{0:T(1024)}, s32[1024]{0:T(1024)S(1)}, u32[]{:S(2)}) copy-start(s32[1024]{0:T(1024)S(1)} %pad_clamp_fusion.3) | copy-start | bytes 12292
  11.3 25.4 %all-to-all-start = ((s32[32,1,1]{2,1,0:T(1,128)}), s32[32,1,1]{2,1,0:T(1,128)S(1)}, u32[]{:S(2)}, u32[]{:S(2)}) async-start(s32[32,1,1]{2,1,0:T(1,128)} %copy.66), calls=%async_computation | async-start | bytes 32768 | tf_op jit(solution)/shard_map/all_to_all | solution.py:351
  25.6 2.8 copy-start.32
  25.6 5.6 copy-start.18
  34.7 15.2 %copy-start.10 = (f32[1,1024,8]{1,2,0:T(8,128)}, f32[1,1024,8]{1,2,0:T(8,128)S(1)}, u32[]{:S(2)}) copy-start(f32[1,1024,8]{1,2,0:T(8,128)S(1)} %copy.83) | copy-start | bytes 98308
  39.8 10.0 %copy-start.30 = (f32[8]{0:T(128)S(1)}, f32[8]{0:T(128)}, u32[]{:S(2)}) copy-start(f32[8]{0:T(128)} %param.21) | copy-start | bytes 100
  39.8 10.1 %copy-start.25 = (bf16[32,64]{1,0:T(8,128)(2,1)S(1)}, bf16[32,64]{1,0:T(8,128)(2,1)}, u32[]{:S(2)}) copy-start(bf16[32,64]{1,0:T(8,128)(2,1)} %param.19) | copy-start | bytes 12292
  39.8 111.3 %all-to-all-start.2 = ((bf16[32,128,256]{2,1,0:T(8,128)(2,1)}), bf16[32,128,256]{2,1,0:T(8,128)(2,1)}, u32[]{:S(2)}, u32[]{:S(2)}) async-start(bf16[32,128,256]{2,1,0:T(8,128)(2,1)} %broadcast_select_fusion), calls=%async_computation.2 | async-start | bytes 4194304 | tf_op jit(solution)/shard_map/all_to_all | solution.py:356
  49.8 356.7 %all-reduce.7.cloned.1.call-start = ((), (), s32[]{:S(2)}) async-start(), calls=%async_computation.4 | async-start | bytes 524288 | tf_op jit(solution)/shard_map/psum | solution.py:149
  50.0 0.6 copy-start.16
  50.6 3.0 copy-start.7
  53.6 0.6 copy-start.12
  54.5 101.1 %copy-start.14 = (bf16[256,256]{1,0:T(8,128)(2,1)S(1)}, bf16[256,256]{1,0:T(8,128)(2,1)}, u32[]{:S(2)}) copy-start(bf16[256,256]{1,0:T(8,128)(2,1)} %param.25) | copy-start | bytes 393220
  144.4 1.2 copy-start.36
  155.9 0.8 copy-start.3
  155.9 250.6 %copy-start.21 = (f32[32,32]{1,0:T(8,128)S(1)}, f32[32,32]{1,0:T(8,128)}, u32[]{:S(2)}) copy-start(f32[32,32]{1,0:T(8,128)} %param.23) | copy-start | bytes 12292
  156.0 251.8 %copy-start.20 = (f32[32,32]{1,0:T(8,128)S(1)}, f32[32,32]{1,0:T(8,128)}, u32[]{:S(2)}) copy-start(f32[32,32]{1,0:T(8,128)} %param.22) | copy-start | bytes 12292
  156.0 253.0 %copy-start.22 = (f32[32,32]{1,0:T(8,128)S(1)}, f32[32,32]{1,0:T(8,128)}, u32[]{:S(2)}) copy-start(f32[32,32]{1,0:T(8,128)} %param.24) | copy-start | bytes 12292
  406.5 4.4 copy-start.39
  411.5 2.1 copy-start.4
  413.6 3.4 copy-start.15
  413.6 3.4 copy-start.23
  422.7 2.2 copy-start.35
  428.1 9.1 %copy-start.5 = (bf16[1024,256]{0,1:T(8,128)(2,1)S(1)}, bf16[1024,256]{0,1:T(8,128)(2,1)}, u32[]{:S(2)}) copy-start(bf16[1024,256]{0,1:T(8,128)(2,1)} %get-tuple-element.19) | copy-start | bytes 1572868
  428.1 9.1 %copy-start.24 = (f32[8,64]{1,0:T(8,128)S(1)}, f32[8,64]{1,0:T(8,128)}, u32[]{:S(2)}) copy-start(f32[8,64]{1,0:T(8,128)} %get-tuple-element.22) | copy-start | bytes 6148
  428.1 287.5 %all-to-all-start.1 = ((bf16[32,128,256]{2,1,0:T(8,128)(2,1)}), bf16[32,128,256]{2,1,0:T(8,128)(2,1)}, u32[]{:S(2)}, u32[]{:S(2)}) async-start(bf16[32,128,256]{2,1,0:T(8,128)(2,1)} %broadcast_select_fusion.1), calls=%async_computation.1 | async-start | bytes 4194304 | tf_op jit(solution)/shard_map/all_to_all | solution.py:350
  437.0 275.1 %all-reduce.5.cloned.1.call-start = ((), (), s32[]{:S(2)}) async-start(), calls=%async_computation.3 | async-start | bytes 1572864 | tf_op jit(solution)/shard_map/psum | solution.py:275
  437.2 2.3 copy-start.8
  437.3 2.3 copy-start.13
  437.3 2.3 copy-start.17
  439.5 0.8 copy-start.11
  439.6 0.8 copy-start.31
  440.4 2.2 copy-start.26
  440.4 2.2 copy-start.33
  443.4 4.9 copy-start.2
  443.4 4.9 copy-start.19
  443.5 4.9 copy-start.40
  448.4 2.9 copy-start.6
  448.4 2.9 copy-start.9
  532.4 1.9 copy-start.1
  532.4 1.9 copy-start.28
  532.4 1.9 copy-start.29
  534.3 183.5 %copy-start.34 = (pred[512]{0:T(512)(128)(4,1)S(1)}, pred[512]{0:T(512)(128)(4,1)}, u32[]{:S(2)}) copy-start(pred[512]{0:T(512)(128)(4,1)} %broadcast_bitcast_fusion.1) | copy-start | bytes 1540
Sparse Core Ops, SparseCore 0:
  157.9 248.5 all-reduce.6
  452.4 259.5 all-reduce.4
where the time goes:
time: 727 us; the launch traced here: 726 us
  waiting for transfers between devices  422 us (58%)
  blocking collectives  164 us (23%)
  matrix products  33 us (5%)
  other arithmetic  32.5 us (4%)
  starting transfers between devices  30.7 us (4%)
  local copies, waits for them, and re-layouts  27.7 us (4%)
  between operations  15.5 us (2%)
    psum x1, waiting for transfers between devices, forward_rows(): lax.psum((numerator_partial, denom_part), ('gx', 'gy'))  247 us
    psum x1, waiting for transfers between devices, backward_rows(): lax.psum((in_grad_part, slice_grad_part), ('gx', 'gy'))  175 us
    psum x1, blocking collectives, forward_rows(): lax.psum((numerator_partial, denom_part), ('gx', 'gy'))  86.7 us
    psum x1, blocking collectives, backward_rows(): lax.psum((in_grad_part, slice_grad_part), ('gx', 'gy'))  77.3 us
  transfers between devices with their start and end apart: 5, of which 2 were waited for; matrix products, arithmetic and copies ran while one was open for 8% of the time, Pallas kernels for 0%

commit v1 on v0

v1 whole, which is shorter than its diff:
```python
import math

import jax
import jax.numpy as jnp
from jax import lax
from jax.experimental import pallas as pl
from jax.experimental.pallas import tpu as pltpu
from jax.sharding import Mesh, PartitionSpec as P

C = 256
HEADS = 8
SLICES = 64
WIDTH = 32
BLK = 128
SIN = 8
SOUT = 4
GX = 8
GY = 32
PIECE = BLK // GY
ROWS = GY * SOUT * PIECE
HOME = GY * SIN * PIECE
SEND = (SIN + SOUT) * PIECE
GROUP = 4 * SEND
META = 16
TOKEN_ROWS = 40
MIX_ROWS = 48
GRAD_ROWS = 56

norm_eps = 1e-05
slice_eps = 1e-05

F32 = jnp.float32
BF16 = jnp.bfloat16
HI = lax.Precision.HIGHEST
NN = (((1,), (0,)), ((), ()))
NT = (((1,), (1,)), ((), ()))
TN = (((0,), (0,)), ((), ()))


def mm(a, b, dims=NN, precision=None):
    return lax.dot_general(a, b, dims, precision=precision, preferred_element_type=F32)


def iota(shape, dim):
    return lax.broadcasted_iota(jnp.int32, shape, dim)


def call(body, outs, *args, scalars=0, scratch=(), flops=0, vmem=40):
    vm = pl.BlockSpec(memory_space=pltpu.VMEM)
    sm = pl.BlockSpec(memory_space=pltpu.SMEM)
    single = not isinstance(outs, (list, tuple))
    listed = [outs] if single else list(outs)
    moved = sum(math.prod(a.shape) * a.dtype.itemsize for a in list(args) + listed)
    res = pl.pallas_call(
        body,
        out_shape=listed,
        in_specs=[sm] * scalars + [vm] * (len(args) - scalars),
        out_specs=[vm] * len(listed),
        scratch_shapes=list(scratch),
        compiler_params=pltpu.CompilerParams(vmem_limit_bytes=vmem * 2**20),
        cost_estimate=pl.CostEstimate(flops=flops, bytes_accessed=moved, transcendentals=0),
    )(*args)
    return res[0] if single else res


def sds(shape, dtype):
    return jax.ShapeDtypeStruct(shape, dtype)


def column(row):
    n = row.shape[1]
    return jnp.sum(jnp.where(iota((n, n), 0) == iota((n, n), 1), row, 0.0), axis=1, keepdims=True)


def piece_order(back):
    sent = iota((GROUP, GROUP), 1 if back else 0)
    kept = iota((GROUP, GROUP), 0 if back else 1)
    part = (
        (sent >= SEND).astype(jnp.int32)
        + (sent >= 2 * SEND).astype(jnp.int32)
        + (sent >= 3 * SEND).astype(jnp.int32)
    )
    within = sent - part * SEND
    source = (within >> 2) * 16 + part * PIECE + (within & 3)
    return (source == kept).astype(F32).astype(BF16)


def pack_kernel(tally, plan, cells, cot, out):
    order = piece_order(False)
    for j in range(8):
        at = 16 * j
        rows = [cells[s * BLK + at : s * BLK + at + 16, :] for s in range(SIN)]
        rows += [cot[t * BLK + at : t * BLK + at + 16, :] for t in range(SOUT)]
        moved = mm(order, jnp.concatenate(rows, axis=0)).astype(BF16)
        for a in range(4):
            out[4 * j + a, 0:SEND, :] = moved[a * SEND : (a + 1) * SEND]
    block = iota((META, C), 1) >> 2
    target = jnp.zeros((META, C), jnp.int32)
    for s in range(SIN):
        target = jnp.where(block == s, plan[0, s], target)
    held = jnp.clip(tally[0] - block * BLK, 0, BLK)
    meta = jnp.where(iota((META, C), 0) < 8, target, held).astype(F32).astype(BF16)
    for j in range(GY):
        out[j, SEND : SEND + META, :] = meta


def unpack_kernel(recv, result, cell_grad):
    order = piece_order(True)
    for j in range(8):
        at = 16 * j
        rows = jnp.concatenate([recv[4 * j + a] for a in range(4)], axis=0)
        moved = mm(order, rows).astype(BF16)
        for s in range(SIN):
            cell_grad[s * BLK + at : s * BLK + at + 16, :] = moved[s * 16 : s * 16 + 16]
        for t in range(SOUT):
            u = SIN + t
            result[t * BLK + at : t * BLK + at + 16, :] = moved[u * 16 : u * 16 + 16]


def forward_kernel(
    spot, recv, gain, entrance, portion, softness, base, exit_w,
    token, pick, xt_out, normed_out, proj_out, prob_out, scaled_out, slice_out,
    uns_out, cot_out, rows_out, heads_out, spread_out,
):
    mine = spot[0]
    cells = recv[:, 0 : SIN * PIECE, :].reshape(HOME, C)
    cot = recv[:, SIN * PIECE : SEND, :].reshape(ROWS, C)
    meta = recv[:, SEND : SEND + META, 0:128].astype(F32)
    target = jnp.max(meta[:, 0:8, :], axis=1)
    held = jnp.max(meta[:, 8:16, :], axis=1)

    lane = iota((GY, 128), 1)
    lane_f = lane.astype(F32)
    hits = [(target[:, 4 * s : 4 * s + 1] == lane_f).astype(F32) for s in range(SIN)]
    taken = hits[0]
    for s in range(1, SIN):
        taken = taken + hits[s]
    before = (iota((GY, GY), 1) < iota((GY, GY), 0)).astype(F32).astype(BF16)
    place = mm(before, taken.astype(BF16)) + lane_f * SOUT + 1.0
    dest = jnp.zeros((GY, 128), F32)
    for s in range(SIN):
        found = jnp.sum(hits[s] * place, axis=1, keepdims=True)
        dest = jnp.where((lane >> 2) == s, found, dest)
    row_in_block = (mine * PIECE + (lane & 3)).astype(F32)
    dest = jnp.where(row_in_block < held, dest, 0.0) - 1.0
    repeat = ((iota((HOME, GY), 0) >> 5) == iota((HOME, GY), 1)).astype(F32).astype(BF16)
    wide = mm(repeat, dest.astype(BF16))
    own = iota((HOME, 128), 1) == (iota((HOME, 128), 0) & 31)
    dest_col = jnp.sum(jnp.where(own, wide, 0.0), axis=1, keepdims=True)
    k_col = (iota((HOME, 1), 0) & 3).astype(F32)
    spot_col = (dest_col * 4.0 + k_col).astype(jnp.int32)
    pick[...] = (spot_col == iota((HOME, ROWS), 1)).astype(F32).astype(BF16)
    live = mm(jnp.ones((8, HOME), BF16), pick[...])[0:1, :]

    xt = mm(cells, pick[...], TN)
    xt_out[...] = xt.astype(BF16)
    mean = jnp.sum(xt, axis=0, keepdims=True) * (1.0 / C)
    centered = xt - mean
    var = jnp.sum(centered * centered, axis=0, keepdims=True) * (1.0 / C)
    inv = lax.rsqrt(var + norm_eps)
    gain_col = column(gain[...])
    normed = (centered * inv * gain_col).astype(BF16)
    normed_out[...] = normed
    proj_out[...] = mm(entrance[...], normed, TN).astype(BF16)
    rows_out[0:1, :] = live
    rows_out[1:2, :] = mean
    rows_out[2:3, :] = inv

    tall = ((iota((C, WIDTH), 0) & 31) == iota((C, WIDTH), 1)).astype(F32).astype(BF16)
    broad = ((iota((SLICES, 512), 1) & 63) == iota((SLICES, 512), 0)).astype(F32).astype(BF16)
    spread = mm(mm(tall, portion[...]).astype(BF16), broad)
    same = (iota((C, 512), 0) >> 5) == (iota((C, 512), 1) >> 6)
    spread_out[...] = jnp.where(same, spread, 0.0).astype(BF16)
    soft_row = mm(softness[...], tall, NT)
    soft_same = (iota((HEADS, C), 1) >> 5) == iota((HEADS, C), 0)
    soft_spread = jnp.where(soft_same, soft_row, 0.0).astype(BF16)

    mid = proj_out[C : 2 * C, :]
    presq = mm(soft_spread, mid)
    softplus = jnp.maximum(presq, 0.0) + jnp.log1p(jnp.exp(-jnp.abs(presq)))
    inv_temp = 1.0 / (column(base[...]) + softplus)
    heads_out[0:8, :] = inv_temp
    heads_out[8:16, :] = presq
    scaled_out[...] = mm(spread_out[...], mid, TN)

    back = mm(exit_w[...], cot, NT) * live
    uns_out[...] = back.astype(BF16)
    eye = (iota((C, C), 0) == iota((C, C), 1)).astype(F32).astype(BF16)
    cot_out[...] = (mm(eye, cot, NT) * live).astype(BF16)

    for h in range(HEADS):
        at = h * SLICES
        scaled = scaled_out[at : at + SLICES, :] * inv_temp[h : h + 1, :]
        scaled_out[at : at + SLICES, :] = scaled
        top = jnp.max(scaled, axis=0, keepdims=True)
        e = jnp.exp(scaled - top)
        prob = e * (1.0 / jnp.sum(e, axis=0, keepdims=True))
        prob_out[at : at + SLICES, :] = prob
        half = (prob * live).astype(BF16)
        slice_out[at : at + SLICES, :] = half
        left = jnp.concatenate(
            [
                proj_out[h * WIDTH : (h + 1) * WIDTH, :],
                uns_out[h * WIDTH : (h + 1) * WIDTH, :],
                jnp.ones((16, ROWS), BF16),
            ],
            axis=0,
        )
        sums = mm(left, half, NT)
        token[h, 0:WIDTH, 0:SLICES] = sums[0:WIDTH]
        token[h, 0:WIDTH, SLICES:128] = sums[WIDTH : 2 * WIDTH]
        token[h, WIDTH:TOKEN_ROWS, 0:SLICES] = sums[2 * WIDTH : 2 * WIDTH + 8]
        token[h, WIDTH:TOKEN_ROWS, SLICES:128] = jnp.zeros((8, SLICES), F32)


def spread_kernel(recv, out):
    n = recv.shape[0]
    total = recv[0].astype(F32)
    for i in range(1, n):
        total = total + recv[i].astype(F32)
    total = total.astype(out.dtype)
    for i in range(out.shape[0]):
        out[i] = total


def spread_sum(recv, copies, dtype):
    return call(spread_kernel, sds((copies,) + recv.shape[1:], dtype), recv)


def token_kernel(recv, request, lookup, content, out):
    total = recv[0].astype(F32)
    for i in range(1, GY):
        total = total + recv[i].astype(F32)
    inverse = 1.0 / (total[WIDTH : WIDTH + 1, 0:SLICES] + slice_eps)
    tok = total[0:WIDTH, 0:SLICES] * inverse
    cot = total[0:WIDTH, SLICES:128]
    scale = WIDTH ** (-0.5)
    q = mm(request[...], tok, TN, HI)
    k = mm(lookup[...], tok, TN, HI)
    v = mm(content[...], tok, TN, HI)
    scores = mm(k, q, TN, HI) * scale
    e = jnp.exp(scores - jnp.max(scores, axis=0, keepdims=True))
    att = e / jnp.sum(e, axis=0, keepdims=True)
    mixed = mm(v, att, NN, HI)
    g_att = mm(v, cot, TN, HI)
    g_v = mm(cot, att, NT, HI)
    g_s = att * (g_att - jnp.sum(att * g_att, axis=0, keepdims=True)) * scale
    g_q = mm(k, g_s, NN, HI)
    g_k = mm(q, g_s, NT, HI)
    g_tok = mm(request[...], g_q, NN, HI)
    g_tok = g_tok + mm(lookup[...], g_k, NN, HI)
    g_tok = g_tok + mm(content[...], g_v, NN, HI)
    g_num = g_tok * inverse
    g_den = -jnp.sum(g_tok * tok, axis=0, keepdims=True) * inverse
    g_den_hi = g_den.astype(BF16).astype(F32)
    g_den_lo = g_den - g_den_hi
    main = jnp.concatenate([mixed, g_num], axis=1).astype(BF16)
    tail = jnp.concatenate([g_den_hi, g_den_lo], axis=1)
    tail = jnp.broadcast_to(tail, (16, 128)).astype(BF16)
    for i in range(GX):
        out[i, 0:WIDTH, :] = main
        out[i, WIDTH:MIX_ROWS, :] = tail


def backward_kernel(
    mix, gain, entrance, softness, exit_w,
    pick, xt_in, normed_in, proj_in, prob_in, scaled_in, slice_in,
    uns_in, cot_in, rows_in, heads_in, spread_in,
    send, grads, weave, stack, gprob, affs, gproj,
):
    live = rows_in[0:1, :]
    mean = rows_in[1:2, :]
    inv = rows_in[2:3, :]
    weave[...] = jnp.zeros_like(weave)
    lane = iota((WIDTH, 128), 1)
    lane16 = iota((16, 128), 1)
    sub16 = iota((16, 128), 0)
    for h in range(HEADS):
        block = mix[h].astype(F32)
        turned = pltpu.roll(block, SLICES, 1)
        low = h % 2 == 0
        left, right = (block, turned) if low else (turned, block)
        here = (lane < SLICES) if low else (lane >= SLICES)
        at = (h // 2) * 128
        weave[h * WIDTH : (h + 1) * WIDTH, at : at + 128] = jnp.where(
            here, left[0:WIDTH], 0.0
        ).astype(BF16)
        weave[C + h * WIDTH : C + (h + 1) * WIDTH, at : at + 128] = jnp.where(
            here, right[0:WIDTH], 0.0
        ).astype(BF16)
    for g in range(HEADS // 2):
        even = mix[2 * g, WIDTH:MIX_ROWS, :].astype(F32)
        odd = mix[2 * g + 1, WIDTH:MIX_ROWS, :].astype(F32)
        upper = jnp.where(lane16 < SLICES, even, pltpu.roll(odd, SLICES, 1))
        lower = jnp.where(lane16 < SLICES, pltpu.roll(even, SLICES, 1), odd)
        both = jnp.where(sub16 == 0, upper, jnp.where(sub16 == 1, lower, 0.0))
        weave[2 * C : 2 * C + 16, g * 128 : (g + 1) * 128] = both.astype(BF16)
    stack[0:C, :] = uns_in[...]
    stack[C : 2 * C, :] = proj_in[0:C, :]
    stack[2 * C : 2 * C + 16, :] = jnp.ones((16, ROWS), BF16)

    rows = mm(weave[0 : 2 * C, :], slice_in[...])
    deslice = rows[0:C].astype(BF16)
    gproj[0:C, :] = rows[C : 2 * C].astype(BF16)
    gprob[...] = mm(weave[...], stack[...], TN)
    branch = mm(exit_w[...], deslice, TN)
    xt = xt_in[...].astype(F32)
    result = (live * (xt + branch)).astype(BF16)
    eye = (iota((ROWS, ROWS), 0) == iota((ROWS, ROWS), 1)).astype(F32).astype(BF16)
    result_rows = mm(eye, result, NT).astype(BF16)
    for q in range(GY):
        send[q, SIN * PIECE : SEND, :] = result_rows[q * 16 : (q + 1) * 16]
    out_grad = mm(deslice, cot_in[...], NT)
    for b in range(2):
        grads[(4 + b) * C : (5 + b) * C, :] = out_grad[:, b * 128 : (b + 1) * 128].astype(
            grads.dtype
        )

    softs = []
    for h in range(HEADS):
        at = h * SLICES
        inv_temp = heads_in[h : h + 1, :]
        presq = heads_in[8 + h : 9 + h, :]
        prob = prob_in[at : at + SLICES, :]
        gp = gprob[at : at + SLICES, :] * live
        adj = prob * (gp - jnp.sum(prob * gp, axis=0, keepdims=True))
        affs[at : at + SLICES, :] = (adj * inv_temp).astype(BF16)
        pulled = jnp.sum(adj * scaled_in[at : at + SLICES, :], axis=0, keepdims=True)
        softs.append(-pulled * inv_temp * (1.0 / (1.0 + jnp.exp(-presq))))
    between = mm(spread_in[...], affs[...])
    soft_col = column(softness[...].astype(F32))
    slice_grad = jnp.zeros((WIDTH, SLICES), F32)
    for h in range(HEADS):
        at = h * WIDTH
        part = between[at : at + WIDTH] + soft_col * softs[h]
        gproj[C + at : C + at + WIDTH, :] = part.astype(BF16)
        slice_grad = slice_grad + mm(
            proj_in[C + at : C + at + WIDTH, :], affs[h * SLICES : (h + 1) * SLICES, :], NT
        )
    in_grad = mm(normed_in[...], gproj[...], NT)
    for b in range(4):
        grads[b * C : (b + 1) * C, :] = in_grad[:, b * 128 : (b + 1) * 128].astype(grads.dtype)
    tail = jnp.concatenate([slice_grad, jnp.zeros((WIDTH, SLICES), F32)], axis=1)
    grads[6 * C : 6 * C + WIDTH, :] = tail.astype(grads.dtype)
    grads[6 * C + WIDTH :, :] = jnp.zeros((GY * GRAD_ROWS - 6 * C - WIDTH, 128), grads.dtype)

    g_unit = mm(entrance[...], gproj[...]) * column(gain[...])
    unit = (xt - mean) * inv
    m1 = jnp.sum(g_unit, axis=0, keepdims=True) * (1.0 / C)
    m2 = jnp.sum(g_unit * unit, axis=0, keepdims=True) * (1.0 / C)
    cell = cot_in[...].astype(F32) + inv * (g_unit - m1 - unit * m2)
    cell_rows = mm(pick[...], cell.astype(BF16), NT).astype(BF16)
    for q in range(GY):
        send[q, 0 : SIN * PIECE, :] = cell_rows[q * 32 : (q + 1) * 32]


def weight_kernel(scale, recv, grad_in, grad_out, grad_slice):
    def part(b):
        return recv[b * C : (b + 1) * C, :].astype(F32) * scale

    for b in range(4):
        grad_in[:, b * 128 : (b + 1) * 128] = part(b)
    for b in range(2):
        grad_out[:, b * 128 : (b + 1) * 128] = part(4 + b)
    grad_slice[...] = recv[6 * C : 6 * C + WIDTH, 0:SLICES].astype(F32) * scale


def shards(
    cells, tally, plan, cot, gain, entrance, portion, softness, base,
    request, lookup, content, exit_w,
):
    gain = gain.reshape(1, C)
    softness = softness.reshape(1, WIDTH)
    base = base.reshape(1, HEADS)
    scale = 1.0 / math.sqrt(GX * GY * SIN * BLK)

    def swap(x, axes):
        return lax.all_to_all(x, axes, 0, 0, tiled=True)

    sent = call(
        pack_kernel, sds((GY, SEND + META, C), BF16), tally, plan, cells, cot, scalars=2
    )
    recv = swap(sent, ("z", "x"))
    spot = (lax.axis_index("z") * 4 + lax.axis_index("x")).astype(jnp.int32).reshape(1)
    state = call(
        forward_kernel,
        [
            sds((HEADS, TOKEN_ROWS, 128), F32),
            sds((HOME, ROWS), BF16),
            sds((C, ROWS), BF16),
            sds((C, ROWS), BF16),
            sds((2 * C, ROWS), BF16),
            sds((512, ROWS), F32),
            sds((512, ROWS), F32),
            sds((512, ROWS), BF16),
            sds((C, ROWS), BF16),
            sds((C, ROWS), BF16),
            sds((8, ROWS), F32),
            sds((16, ROWS), F32),
            sds((C, 512), BF16),
        ],
        spot, recv, gain, entrance, portion, softness, base, exit_w,
        scalars=1,
    )
    token, saved = state[0], state[1:]
    token = swap(token, ("y", "core"))
    token = swap(spread_sum(token, GY, BF16), ("z", "x"))
    mix = call(
        token_kernel, sds((GX, MIX_ROWS, 128), BF16), token, request, lookup, content
    )
    mix = swap(mix, ("y", "core"))
    send, grads = call(
        backward_kernel,
        [sds((GY, SEND, C), BF16), sds((GY * GRAD_ROWS, 128), BF16)],
        mix, gain, entrance, softness, exit_w, *saved,
        scratch=[
            pltpu.VMEM((2 * C + 16, 512), BF16),
            pltpu.VMEM((2 * C + 16, ROWS), BF16),
            pltpu.VMEM((512, ROWS), F32),
            pltpu.VMEM((512, ROWS), BF16),
            pltpu.VMEM((2 * C, ROWS), BF16),
        ],
    )
    home = swap(send, ("z", "x"))
    grads = swap(grads.reshape(GY, GRAD_ROWS, 128), ("y", "core", "x"))
    grads = swap(spread_sum(grads, 8, BF16), ("z",))
    grads = swap(spread_sum(grads, GY, BF16), ("y", "core", "x"))
    result, cell_grad = call(
        unpack_kernel, [sds((SOUT * BLK, C), BF16), sds((SIN * BLK, C), BF16)], home
    )
    grad_in, grad_out, grad_slice = call(
        lambda *refs: weight_kernel(scale, *refs),
        [sds((C, 2 * C), F32), sds((C, C), F32), sds((WIDTH, SLICES), F32)],
        grads.reshape(GY * GRAD_ROWS, 128),
    )
    return result, cell_grad, grad_in, grad_out, grad_slice


def solution(mesh):
    grid = Mesh(mesh.devices.reshape(4, 2, 8, 4), ("y", "core", "z", "x"))
    whole = ("y", "core", "z", "x")
    placed = (P(whole, None), P(whole), P(whole, None), P(whole, None)) + (P(),) * 9
    return jax.shard_map(
        shards,
        mesh=grid,
        in_specs=placed,
        out_specs=(P(whole, None), P(whole, None), P(), P(), P()),
        check_vma=False,
    )
```

time: 727 us -> 162 us (0.22)
  waiting for transfers between devices: 422 us -> 50.2 us
  blocking collectives: 164 us -> 76.9 us
  matrix products: 33 us -> 0 us
  other arithmetic: 32.5 us -> 0 us
  local copies, waits for them, and re-layouts: 27.7 us -> 2.68 us
  between operations: 15.5 us -> 1.42 us
  starting transfers between devices: 30.7 us -> 17.9 us
  Pallas kernels: 0 us -> 12 us
    psum x2 -> x0, waiting for transfers between devices: 422 us -> none  [the longest x1 247 us: forward_rows(): lax.psum((numerator_partial, denom_part), ('gx', 'gy'))]
    psum x2 -> x0, blocking collectives: 164 us -> none  [the longest x1 86.7 us: forward_rows(): lax.psum((numerator_partial, denom_part), ('gx', 'gy'))]
    all_to_all x0 -> x6, blocking collectives: none -> 76.9 us  [swap(): return lax.all_to_all(x, axes, 0, 0, tiled=True)]
    all_to_all x3 -> x2, waiting for transfers between devices: 0.01 us -> 50.2 us  [swap(): return lax.all_to_all(x, axes, 0, 0, tiled=True)]
    dot_general x28 -> x0, matrix products: 33 us -> none  [the longest x1 2.85 us: backward_rows(): lax.dot_general(standardized, grad_proj, contract_rows, preferred_element...]
    all_to_all x3 -> x2, starting transfers between devices: 30.4 us -> 17.9 us  [swap(): return lax.all_to_all(x, axes, 0, 0, tiled=True)]
    pallas_call x0 -> x9, Pallas kernels: none -> 12 us  [call(): pl.pallas_call(body, out_shape=listed, in_specs=[sm] * scalars + [vm] * (...]
    select_n x10 -> x0, other arithmetic: 10 us -> none  [the longest x6 6.43 us: pick_blocks(): return jnp.take(blocks, chosen_rows, axis=0, mode='fill', fill_value=0)]
  transfers between devices with their start and end apart: 5 -> 2, of which waited for: 2 -> 2; matrix products, arithmetic and copies ran while one was open for 8% -> 0% of each run, Pallas kernels for 0% -> 1%
where the time goes in v1:
time: 162 us; the launch traced here: 161 us
  blocking collectives  76.9 us (47%)
  waiting for transfers between devices  50.2 us (31%)
  starting transfers between devices  17.9 us (11%)
  Pallas kernels  12 us (7%)
  local copies, waits for them, and re-layouts  2.68 us (2%)
    all_to_all x6, blocking collectives, swap(): return lax.all_to_all(x, axes, 0, 0, tiled=True)  76.9 us
    all_to_all x2, waiting for transfers between devices, swap(): return lax.all_to_all(x, axes, 0, 0, tiled=True)  50.2 us
    all_to_all x2, starting transfers between devices, swap(): return lax.all_to_all(x, axes, 0, 0, tiled=True)  17.9 us
    pallas_call x9, Pallas kernels, call(): pl.pallas_call(body, out_shape=listed, in_specs=[sm] * scalars + [vm] * (...  12 us
  transfers between devices with their start and end apart: 2, of which 2 were waited for; matrix products, arithmetic and copies ran while one was open for 0% of the time, Pallas kernels for 1%

profile of v1, /device:TPU:2, one launch (start us, length us, event | category | flops | bytes accessed | tf_op | source)
XLA Modules:
  0.0 161.1 jit_solution(15857291514787547671)
XLA Ops:
  0.6 0.0 copy-start.10
  1.3 0.0 copy-done.10
  1.3 0.0 copy-start.1
  1.3 1.0 copy-done.1
  2.4 0.0 copy-start.3
  2.4 0.9 copy-done.3
  3.3 1.9 %shard_map.164 = bf16[32,64,256]{2,1,0:T(8,128)(2,1)} custom-call(s32[1]{0:T(128)S(6)} %copy.18.tally, s32[1,8]{1,0:T(1,128)S(1)} %copy-done.10, bf16[1024,256]{1,0:T(8,128)(2,1)S(1)} %copy-done.1, bf16[512,256]{1,0:T(8,128)(2,1)S(1)} %copy-done.3), custom_call_target="tpu_custom_call" | custom-call | bytes 1835044 | tf_op jit(solution)/shard_map/pallas_call | solution.py:54
  5.2 0.0 copy-start
  5.2 0.0 copy-start.2
  5.2 0.0 copy-start.11
  5.2 11.7 %all-to-all-start = ((bf16[32,64,256]{2,1,0:T(8,128)(2,1)}), bf16[32,64,256]{2,1,0:T(8,128)(2,1)S(1)}, u32[]{:S(2)}, u32[]{:S(2)}) async-start(bf16[32,64,256]{2,1,0:T(8,128)(2,1)} %shard_map.164), calls=%async_computation | async-start | bytes 2097152 | tf_op jit(solution)/shard_map/all_to_all | solution.py:378
  17.0 0.0 copy-start.7
  17.0 28.0 %all-to-all-done.recv = bf16[32,64,256]{2,1,0:T(8,128)(2,1)S(1)} async-done(((bf16[32,64,256]{2,1,0:T(8,128)(2,1)}), bf16[32,64,256]{2,1,0:T(8,128)(2,1)S(1)}, u32[]{:S(2)}, u32[]{:S(2)}) %all-to-all-start) | async-done | bytes 1048608 | tf_op jit(solution)/shard_map/all_to_all | solution.py:378
  45.0 0.0 copy-start.8
  45.0 0.0 copy-start.9
  45.0 0.0 copy-done
  45.0 0.0 copy-done.2
  45.0 0.0 copy-done.11
  45.0 0.0 copy-done.7
  45.1 0.6 copy-done.8
  45.7 0.0 copy-done.9
  45.7 3.2 %shard_map.165 = (f32[8,40,128]{2,1,0:T(8,128)S(1)}, bf16[1024,512]{1,0:T(8,128)(2,1)S(1)}, bf16[256,512]{1,0:T(8,128)(2,1)S(1)}, bf16[256,512]{1,0:T(8,128)(2,1...) custom-call(s32[1]{0:T(128)} %bitcast.spot, ...), custom_call_target="tpu_custom_call" | custom-call | bytes 7165028 | tf_op jit(solution)/shard_map/pallas_call | solution.py:54
  48.9 10.8 %all_to_all.40.recv = f32[8,40,128]{2,1,0:T(8,128)S(1)} all-to-all(f32[8,40,128]{2,1,0:T(8,128)S(1)} %get-tuple-element.25), channel_id=1, replica_groups=mesh['y'=4,'core'=2,'z'=8,'x'=4] {'y','core'}, dimensions={0} | all-to-all | bytes 327680 | tf_op jit(solution)/shard_map/all_to_all | solution.py:378
  59.7 0.0 copy-start.4
  59.7 0.0 copy-start.5
  59.7 0.0 copy-start.6
  59.7 17.9 %all_to_all.41.recv = bf16[32,40,128]{2,1,0:T(8,128)(2,1)S(1)} all-to-all(bf16[32,40,128]{2,1,0:T(8,128)(2,1)S(1)} %shard_map.166), channel_id=1, replica_groups=mesh['y'=4,'core'=2,'z'=8,'x'=4] {'z','x'}, dimensions={0} | all-to-all | bytes 655360 | tf_op jit(solution)/shard_map/all_to_all | solution.py:378
  77.6 0.0 copy-done.4
  77.6 0.0 copy-done.5
  77.6 0.0 copy-done.6
  77.6 1.2 shard_map.167
  78.8 8.2 %all_to_all.42.mix = bf16[8,48,128]{2,1,0:T(8,128)(2,1)S(1)} all-to-all(bf16[8,48,128]{2,1,0:T(8,128)(2,1)S(1)} %shard_map.167), channel_id=1, replica_groups=mesh['y'=4,'core'=2,'z'=8,'x'=4] {'y','core'}, dimensions={0} | all-to-all | bytes 196608 | tf_op jit(solution)/shard_map/all_to_all | solution.py:378
  87.0 3.4 %shard_map.168 = (bf16[32,48,256]{2,1,0:T(8,128)(2,1)}, bf16[1792,128]{1,0:T(8,128)(2,1)S(1)}) custom-call(bf16[8,48,128]{2,1,0:T(8,128)(2,1)S(1)} %all_to_all.42.mix, f32[1,256]{1,0:T(1,128)S(1)} %bitcast.9, bf16[256,512]{1,0:T(8,128)(2,1)S(1)} %copy-done, bf16[1,32]{1,0:T(2,128)(2,1)S(1)} %bitcast.11, bf16[256,256]{1,0:T(8,128)(2,1)S(1)} %copy-done.2, ...), custom_call_target="tpu_custom_call" | custom-call | bytes 7291968 | tf_op jit(solution)/shard_map/pallas_call | solution.py:54
  90.4 13.9 %all_to_all.43.recv = bf16[32,56,128]{2,1,0:T(8,128)(2,1)S(1)} all-to-all(bf16[32,56,128]{2,1,0:T(8,128)(2,1)S(1)} %bitcast.7), channel_id=1, replica_groups=mesh['y'=4,'core'=2,'z'=8,'x'=4] {'y','core','x'}, dimensions={0} | all-to-all | bytes 917504 | tf_op jit(solution)/shard_map/all_to_all | solution.py:378
  104.3 0.1 shard_map.170
  104.4 12.4 %all_to_all.44.recv = bf16[8,56,128]{2,1,0:T(8,128)(2,1)S(1)} all-to-all(bf16[8,56,128]{2,1,0:T(8,128)(2,1)S(1)} %shard_map.170), channel_id=1, replica_groups=mesh['y'=4,'core'=2,'z'=8,'x'=4] {'z'}, dimensions={0} | all-to-all | bytes 229376 | tf_op jit(solution)/shard_map/all_to_all | solution.py:378
  116.8 13.8 %all_to_all.45 = bf16[32,56,128]{2,1,0:T(8,128)(2,1)S(1)} all-to-all(bf16[32,56,128]{2,1,0:T(8,128)(2,1)S(1)} %shard_map.171), channel_id=1, replica_groups=mesh['y'=4,'core'=2,'z'=8,'x'=4] {'y','core','x'}, dimensions={0} | all-to-all | bytes 917504 | tf_op jit(solution)/shard_map/all_to_all | solution.py:378
  130.6 6.2 %all-to-all-start.4 = ((bf16[32,48,256]{2,1,0:T(8,128)(2,1)}), bf16[32,48,256]{2,1,0:T(8,128)(2,1)S(1)}, u32[]{:S(2)}, u32[]{:S(2)}) async-start(bf16[32,48,256]{2,1,0:T(8,128)(2,1)} %get-tuple-element.38), calls=%async_computation.4 | async-start | bytes 1572864 | tf_op jit(solution)/shard_map/all_to_all | solution.py:378
  136.8 0.9 shard_map.172
  137.7 22.2 %all-to-all-done.4.recv = bf16[32,48,256]{2,1,0:T(8,128)(2,1)S(1)} async-done(((bf16[32,48,256]{2,1,0:T(8,128)(2,1)}), bf16[32,48,256]{2,1,0:T(8,128)(2,1)S(1)}, u32[]{:S(2)}, u32[]{:S(2)}) %all-to-all-start.4) | async-done | bytes 786464 | tf_op jit(solution)/shard_map/all_to_all | solution.py:378
  159.9 1.2 shard_map.169
  (2 shorter events, 0.1 us)
Async XLA Ops:
  0.6 0.7 copy-start.10
  1.3 1.0 copy-start.1
  2.4 0.9 copy-start.3
  5.2 39.8 %copy-start = (bf16[256,512]{1,0:T(8,128)(2,1)S(1)}, bf16[256,512]{1,0:T(8,128)(2,1)}, u32[]{:S(2)}) copy-start(bf16[256,512]{1,0:T(8,128)(2,1)} %entrance.3) | copy-start | bytes 786436
  5.2 39.8 %copy-start.2 = (bf16[256,256]{1,0:T(8,128)(2,1)S(1)}, bf16[256,256]{1,0:T(8,128)(2,1)}, u32[]{:S(2)}) copy-start(bf16[256,256]{1,0:T(8,128)(2,1)} %exit_w.3) | copy-start | bytes 393220
  5.2 39.8 %copy-start.11 = (f32[8]{0:T(128)S(1)}, f32[8]{0:T(128)}, u32[]{:S(2)}) copy-start(f32[8]{0:T(128)} %param.21) | copy-start | bytes 100
  5.2 39.8 %all-to-all-start = ((bf16[32,64,256]{2,1,0:T(8,128)(2,1)}), bf16[32,64,256]{2,1,0:T(8,128)(2,1)S(1)}, u32[]{:S(2)}, u32[]{:S(2)}) async-start(bf16[32,64,256]{2,1,0:T(8,128)(2,1)} %shard_map.164), calls=%async_computation | async-start | bytes 2097152 | tf_op jit(solution)/shard_map/all_to_all | solution.py:378
  17.0 28.1 %copy-start.7 = (bf16[32,64]{1,0:T(8,128)(2,1)S(1)}, bf16[32,64]{1,0:T(8,128)(2,1)}, u32[]{:S(2)}) copy-start(bf16[32,64]{1,0:T(8,128)(2,1)} %portion.1) | copy-start | bytes 12292
  45.0 0.7 copy-start.8
  45.0 0.7 copy-start.9
  59.7 17.9 %copy-start.4 = (f32[32,32]{1,0:T(8,128)S(1)}, f32[32,32]{1,0:T(8,128)}, u32[]{:S(2)}) copy-start(f32[32,32]{1,0:T(8,128)} %request.1) | copy-start | bytes 12292
  59.7 17.9 %copy-start.5 = (f32[32,32]{1,0:T(8,128)S(1)}, f32[32,32]{1,0:T(8,128)}, u32[]{:S(2)}) copy-start(f32[32,32]{1,0:T(8,128)} %lookup.1) | copy-start | bytes 12292
  59.7 17.9 %copy-start.6 = (f32[32,32]{1,0:T(8,128)S(1)}, f32[32,32]{1,0:T(8,128)}, u32[]{:S(2)}) copy-start(f32[32,32]{1,0:T(8,128)} %content.1) | copy-start | bytes 12292
  130.6 29.3 %all-to-all-start.4 = ((bf16[32,48,256]{2,1,0:T(8,128)(2,1)}), bf16[32,48,256]{2,1,0:T(8,128)(2,1)S(1)}, u32[]{:S(2)}, u32[]{:S(2)}) async-start(bf16[32,48,256]{2,1,0:T(8,128)(2,1)} %get-tuple-element.38), calls=%async_computation.4 | async-start | bytes 1572864 | tf_op jit(solution)/shard_map/all_to_all | solution.py:378

commit v2 on v1

--- a/solution.py
+++ b/solution.py
@@ -21,7 +21,8 @@
 HOME = GY * SIN * PIECE
 SEND = (SIN + SOUT) * PIECE
 GROUP = 4 * SEND
-META = 16
+META = 8
+TALL = 2 * SEND + META
 TOKEN_ROWS = 40
 MIX_ROWS = 48
 GRAD_ROWS = 56
@@ -93,15 +94,17 @@
         rows += [cot[t * BLK + at : t * BLK + at + 16, :] for t in range(SOUT)]
         moved = mm(order, jnp.concatenate(rows, axis=0)).astype(BF16)
         for a in range(4):
-            out[4 * j + a, 0:SEND, :] = moved[a * SEND : (a + 1) * SEND]
-    block = iota((META, C), 1) >> 2
-    target = jnp.zeros((META, C), jnp.int32)
+            part = moved[a * SEND : (a + 1) * SEND]
+            out[4 * j + a, 0:SEND, :] = part[:, 0:128]
+            out[4 * j + a, SEND : 2 * SEND, :] = part[:, 128:C]
+    block = iota((META, 128), 1) >> 2
+    target = jnp.zeros((META, 128), jnp.int32)
     for s in range(SIN):
         target = jnp.where(block == s, plan[0, s], target)
     held = jnp.clip(tally[0] - block * BLK, 0, BLK)
-    meta = jnp.where(iota((META, C), 0) < 8, target, held).astype(F32).astype(BF16)
+    meta = jnp.where(iota((META, 128), 0) < 4, target, held).astype(F32).astype(BF16)
     for j in range(GY):
-        out[j, SEND : SEND + META, :] = meta
+        out[j, 2 * SEND : TALL, :] = meta
 
 
 def unpack_kernel(recv, result, cell_grad):
@@ -123,11 +126,16 @@
     uns_out, cot_out, rows_out, heads_out, spread_out,
 ):
     mine = spot[0]
-    cells = recv[:, 0 : SIN * PIECE, :].reshape(HOME, C)
-    cot = recv[:, SIN * PIECE : SEND, :].reshape(ROWS, C)
-    meta = recv[:, SEND : SEND + META, 0:128].astype(F32)
-    target = jnp.max(meta[:, 0:8, :], axis=1)
-    held = jnp.max(meta[:, 8:16, :], axis=1)
+    cells = jnp.concatenate(
+        [recv[:, a : a + SIN * PIECE, :].reshape(HOME, 128) for a in (0, SEND)], axis=1
+    )
+    cot = jnp.concatenate(
+        [recv[:, a + SIN * PIECE : a + SEND, :].reshape(ROWS, 128) for a in (0, SEND)], axis=1
+    )
+    meta = recv[:, 2 * SEND : TALL, :].astype(F32)
+    upper = iota((GY, META, 128), 1) < 4
+    target = jnp.max(jnp.where(upper, meta, -1.0), axis=1)
+    held = jnp.max(jnp.where(upper, 0.0, meta), axis=1)
 
     lane = iota((GY, 128), 1)
     lane_f = lane.astype(F32)
@@ -207,10 +215,9 @@
             axis=0,
         )
         sums = mm(left, half, NT)
-        token[h, 0:WIDTH, 0:SLICES] = sums[0:WIDTH]
-        token[h, 0:WIDTH, SLICES:128] = sums[WIDTH : 2 * WIDTH]
-        token[h, WIDTH:TOKEN_ROWS, 0:SLICES] = sums[2 * WIDTH : 2 * WIDTH + 8]
-        token[h, WIDTH:TOKEN_ROWS, SLICES:128] = jnp.zeros((8, SLICES), F32)
+        main = jnp.concatenate([sums[0:WIDTH], sums[WIDTH : 2 * WIDTH]], axis=1)
+        count = jnp.concatenate([sums[2 * WIDTH : 2 * WIDTH + 8]] * 2, axis=1)
+        token[h] = jnp.concatenate([main, count], axis=0).astype(BF16)
 
 
 def spread_kernel(recv, out):
@@ -354,15 +361,23 @@
         send[q, 0 : SIN * PIECE, :] = cell_rows[q * 32 : (q + 1) * 32]
 
 
-def weight_kernel(scale, recv, grad_in, grad_out, grad_slice):
+def weight_kernel(scale, at, r0, r1, r2, r3, grad_in, grad_out, grad_slice, flat):
+    y, core, x = at[0], at[1], at[2]
+    for dy, recv in enumerate((r0, r1, r2, r3)):
+        for dx in range(4):
+            for dc in range(2):
+                index = (((y - dy) & 3) * 2 + (core ^ dc)) * 4 + ((x - dx) & 3)
+                start = pl.multiple_of(index * GRAD_ROWS, 8)
+                flat[pl.ds(start, GRAD_ROWS), :] = recv[dx * 2 + dc].astype(F32) * scale
+
     def part(b):
-        return recv[b * C : (b + 1) * C, :].astype(F32) * scale
+        return flat[b * C : (b + 1) * C, :]
 
     for b in range(4):
         grad_in[:, b * 128 : (b + 1) * 128] = part(b)
     for b in range(2):
         grad_out[:, b * 128 : (b + 1) * 128] = part(4 + b)
-    grad_slice[...] = recv[6 * C : 6 * C + WIDTH, 0:SLICES].astype(F32) * scale
+    grad_slice[...] = flat[6 * C : 6 * C + WIDTH, 0:SLICES]
 
 
 def shards(
@@ -377,15 +392,18 @@
     def swap(x, axes):
         return lax.all_to_all(x, axes, 0, 0, tiled=True)
 
+    def shifted(x, axis, n, d):
+        return lax.ppermute(x, axis, [(i, (i + d) % n) for i in range(n)])
+
     sent = call(
-        pack_kernel, sds((GY, SEND + META, C), BF16), tally, plan, cells, cot, scalars=2
+        pack_kernel, sds((GY, TALL, 128), BF16), tally, plan, cells, cot, scalars=2
     )
     recv = swap(sent, ("z", "x"))
     spot = (lax.axis_index("z") * 4 + lax.axis_index("x")).astype(jnp.int32).reshape(1)
     state = call(
         forward_kernel,
         [
-            sds((HEADS, TOKEN_ROWS, 128), F32),
+            sds((HEADS, TOKEN_ROWS, 128), BF16),
             sds((HOME, ROWS), BF16),
             sds((C, ROWS), BF16),
             sds((C, ROWS), BF16),
@@ -421,17 +439,24 @@
             pltpu.VMEM((2 * C, ROWS), BF16),
         ],
     )
-    home = swap(send, ("z", "x"))
     grads = swap(grads.reshape(GY, GRAD_ROWS, 128), ("y", "core", "x"))
     grads = swap(spread_sum(grads, 8, BF16), ("z",))
-    grads = swap(spread_sum(grads, GY, BF16), ("y", "core", "x"))
+    grads = spread_sum(grads, 1, BF16)
+    send, grads = lax.optimization_barrier((send, grads))
+    home = swap(send, ("z", "x"))
+    grads = jnp.concatenate([grads, shifted(grads, "core", 2, 1)], axis=0)
+    grads = jnp.concatenate([grads] + [shifted(grads, "x", 4, d) for d in (1, 2, 3)], axis=0)
+    gathered = [grads] + [shifted(grads, "y", 4, d) for d in (1, 2, 3)]
+    at = jnp.stack([lax.axis_index(a) for a in ("y", "core", "x")]).astype(jnp.int32)
     result, cell_grad = call(
         unpack_kernel, [sds((SOUT * BLK, C), BF16), sds((SIN * BLK, C), BF16)], home
     )
     grad_in, grad_out, grad_slice = call(
         lambda *refs: weight_kernel(scale, *refs),
         [sds((C, 2 * C), F32), sds((C, C), F32), sds((WIDTH, SLICES), F32)],
-        grads.reshape(GY * GRAD_ROWS, 128),
+        at, *gathered,
+        scalars=1,
+        scratch=[pltpu.VMEM((GY * GRAD_ROWS, 128), F32)],
     )
     return result, cell_grad, grad_in, grad_out, grad_slice
 

time: 162 us -> 141 us (0.87)
  blocking collectives: 76.9 us -> 62.5 us
  waiting for transfers between devices: 50.2 us -> 36.7 us
  starting transfers between devices: 17.9 us -> 24.5 us
    all_to_all x2, waiting for transfers between devices: 50.2 us -> 24.4 us  [swap(): return lax.all_to_all(x, axes, 0, 0, tiled=True)]
    all_to_all x6 -> x5, blocking collectives: 76.9 us -> 62.5 us  [swap(): return lax.all_to_all(x, axes, 0, 0, tiled=True)]
    ppermute x0 -> x7, waiting for transfers between devices: none -> 12.3 us  [shifted(): return lax.ppermute(x, axis, [(i, (i + d) % n) for i in range(n)])]
    ppermute x0 -> x7, starting transfers between devices: none -> 7.29 us  [shifted(): return lax.ppermute(x, axis, [(i, (i + d) % n) for i in range(n)])]
  transfers between devices with their start and end apart: 2 -> 9, of which waited for: 2 -> 8; matrix products, arithmetic and copies ran while one was open for 0% -> 0% of each run, Pallas kernels for 1% -> 1%
where the time goes in v2:
time: 141 us; the launch traced here: 140 us
  blocking collectives  62.5 us (44%)
  waiting for transfers between devices  36.7 us (26%)
  starting transfers between devices  24.5 us (17%)
  Pallas kernels  12.5 us (9%)
  local copies, waits for them, and re-layouts  2.72 us (2%)
  between operations  1.45 us (1%)
    all_to_all x5, blocking collectives, swap(): return lax.all_to_all(x, axes, 0, 0, tiled=True)  62.5 us
    all_to_all x2, waiting for transfers between devices, swap(): return lax.all_to_all(x, axes, 0, 0, tiled=True)  24.4 us
    all_to_all x2, starting transfers between devices, swap(): return lax.all_to_all(x, axes, 0, 0, tiled=True)  17.2 us
    pallas_call x9, Pallas kernels, call(): pl.pallas_call(body, out_shape=listed, in_specs=[sm] * scalars + [vm] * (...  12.5 us
    ppermute x7, waiting for transfers between devices, shifted(): return lax.ppermute(x, axis, [(i, (i + d) % n) for i in range(n)])  12.3 us
    ppermute x7, starting transfers between devices, shifted(): return lax.ppermute(x, axis, [(i, (i + d) % n) for i in range(n)])  7.29 us
  transfers between devices with their start and end apart: 9, of which 8 were waited for; matrix products, arithmetic and copies ran while one was open for 0% of the time, Pallas kernels for 1%

profile of v2, /device:TPU:2, one launch (start us, length us, event | category | flops | bytes accessed | tf_op | source)
XLA Modules:
  0.0 140.4 jit_solution(8235570746603623012)
XLA Ops:
  0.6 0.0 copy-start.10
  1.3 0.0 copy-done.10
  1.3 0.0 copy-start.1
  1.3 1.0 copy-done.1
  2.4 0.0 copy-start.3
  2.4 0.9 copy-done.3
  3.3 1.8 %shard_map.164 = bf16[32,104,128]{2,1,0:T(8,128)(2,1)} custom-call(s32[1]{0:T(128)S(6)} %copy.23.tally, s32[1,8]{1,0:T(1,128)S(1)} %copy-done.10, bf16[1024,256]{1,0:T(8,128)(2,1)S(1)} %copy-done.1, bf16[512,256]{1,0:T(8,128)(2,1)S(1)} %copy-done.3), custom_call_target="tpu_custom_call" | custom-call | bytes 1638436 | tf_op jit(solution)/shard_map/pallas_call | solution.py:55
  5.1 0.0 copy-start
  5.1 0.0 copy-start.2
  5.1 0.0 copy-start.11
  5.1 11.7 %all-to-all-start = ((bf16[32,104,128]{2,1,0:T(8,128)(2,1)}), bf16[32,104,128]{2,1,0:T(8,128)(2,1)S(1)}, u32[]{:S(2)}, u32[]{:S(2)}) async-start(bf16[32,104,128]{2,1,0:T(8,128)(2,1)} %shard_map.164), calls=%async_computation | async-start | bytes 1703936 | tf_op jit(solution)/shard_map/all_to_all | solution.py:393
  16.9 0.0 copy-start.7
  16.9 23.8 %all-to-all-done.recv = bf16[32,104,128]{2,1,0:T(8,128)(2,1)S(1)} async-done(((bf16[32,104,128]{2,1,0:T(8,128)(2,1)}), bf16[32,104,128]{2,1,0:T(8,128)(2,1)S(1)}, u32[]{:S(2)}, u32[]{:S(2)}) %all-to-all-start) | async-done | bytes 852000 | tf_op jit(solution)/shard_map/all_to_all | solution.py:393
  40.7 0.0 copy-start.8
  40.7 0.0 copy-start.9
  40.7 0.0 copy-done
  40.7 0.0 copy-done.2
  40.7 0.0 copy-done.11
  40.8 0.0 copy-done.7
  40.8 0.6 copy-done.8
  41.4 0.0 copy-done.9
  41.4 3.2 %shard_map.165 = (bf16[8,40,128]{2,1,0:T(8,128)(2,1)S(1)}, bf16[1024,512]{1,0:T(8,128)(2,1)S(1)}, bf16[256,512]{1,0:T(8,128)(2,1)S(1)}, bf16[256,512]{1,0:T(8,12...) custom-call(s32[1]{0:T(128)} %bitcast.spot, ...), custom_call_target="tpu_custom_call" | custom-call | bytes 6886500 | tf_op jit(solution)/shard_map/pallas_call | solution.py:55
  44.6 10.0 %all_to_all.35.recv = bf16[8,40,128]{2,1,0:T(8,128)(2,1)S(1)} all-to-all(bf16[8,40,128]{2,1,0:T(8,128)(2,1)S(1)} %get-tuple-element.27), channel_id=1, replica_groups=mesh['y'=4,'core'=2,'z'=8,'x'=4] {'y','core'}, dimensions={0} | all-to-all | bytes 163840 | tf_op jit(solution)/shard_map/all_to_all | solution.py:393
  54.7 0.0 copy-start.4
  54.7 0.0 copy-start.5
  54.7 0.0 copy-start.6
  54.7 18.0 %all_to_all.36.recv = bf16[32,40,128]{2,1,0:T(8,128)(2,1)S(1)} all-to-all(bf16[32,40,128]{2,1,0:T(8,128)(2,1)S(1)} %shard_map.166), channel_id=1, replica_groups=mesh['y'=4,'core'=2,'z'=8,'x'=4] {'z','x'}, dimensions={0} | all-to-all | bytes 655360 | tf_op jit(solution)/shard_map/all_to_all | solution.py:393
  72.7 0.0 copy-done.4
  72.7 0.0 copy-done.5
  72.7 0.0 copy-done.6
  72.7 1.2 shard_map.167
  73.9 8.2 %all_to_all.37.mix = bf16[8,48,128]{2,1,0:T(8,128)(2,1)S(1)} all-to-all(bf16[8,48,128]{2,1,0:T(8,128)(2,1)S(1)} %shard_map.167), channel_id=1, replica_groups=mesh['y'=4,'core'=2,'z'=8,'x'=4] {'y','core'}, dimensions={0} | all-to-all | bytes 196608 | tf_op jit(solution)/shard_map/all_to_all | solution.py:393
  82.0 3.4 %shard_map.168 = (bf16[32,48,256]{2,1,0:T(8,128)(2,1)}, bf16[1792,128]{1,0:T(8,128)(2,1)S(1)}) custom-call(bf16[8,48,128]{2,1,0:T(8,128)(2,1)S(1)} %all_to_all.37.mix, f32[1,256]{1,0:T(1,128)S(1)} %bitcast.10, bf16[256,512]{1,0:T(8,128)(2,1)S(1)} %copy-done, bf16[1,32]{1,0:T(2,128)(2,1)S(1)} %bitcast.12, bf16[256,256]{1,0:T(8,128)(2,1)S(1)} %copy-done.2, ...), custom_call_target="tpu_custom_call" | custom-call | bytes 7291968 | tf_op jit(solution)/shard_map/pallas_call | solution.py:55
  85.5 13.9 %all_to_all.38.recv = bf16[32,56,128]{2,1,0:T(8,128)(2,1)S(1)} all-to-all(bf16[32,56,128]{2,1,0:T(8,128)(2,1)S(1)} %bitcast.8), channel_id=1, replica_groups=mesh['y'=4,'core'=2,'z'=8,'x'=4] {'y','core','x'}, dimensions={0} | all-to-all | bytes 917504 | tf_op jit(solution)/shard_map/all_to_all | solution.py:393
  99.4 0.1 shard_map.169
  99.5 12.4 %all_to_all.39.recv = bf16[8,56,128]{2,1,0:T(8,128)(2,1)S(1)} all-to-all(bf16[8,56,128]{2,1,0:T(8,128)(2,1)S(1)} %shard_map.169), channel_id=1, replica_groups=mesh['y'=4,'core'=2,'z'=8,'x'=4] {'z'}, dimensions={0} | all-to-all | bytes 229376 | tf_op jit(solution)/shard_map/all_to_all | solution.py:393
  111.9 5.5 %all-to-all-start.6 = ((bf16[32,48,256]{2,1,0:T(8,128)(2,1)}), bf16[32,48,256]{2,1,0:T(8,128)(2,1)S(1)}, u32[]{:S(2)}, u32[]{:S(2)}) async-start(bf16[32,48,256]{2,1,0:T(8,128)(2,1)} %get-tuple-element.42), calls=%async_computation.6 | async-start | bytes 1572864 | tf_op jit(solution)/shard_map/all_to_all | solution.py:393
  117.3 0.1 collective-permute-start
  117.5 1.2 collective-permute-done
  118.6 1.5 %collective-permute-start.1 = (bf16[2,56,128]{2,1,0:T(8,128)(2,1)S(1)}, bf16[2,56,128]{2,1,0:T(8,128)(2,1)S(1)}, u32[]{:S(2)}, u32[]{:S(2)}) collective-permute-start(bf16[2,56,128]{2,1,0:T(8,128)(2,1)S(1)} %get-tuple-element.49), channel_id=1, source_target_pairs={{0,1},{1,2},{2,3},{3,0},{4,5},{5,6},{6,7},{7,4},{8,9},{9,10},{10,1... | collective-permute-start | bytes 86024 | tf_op jit(solution)/shard_map/ppermute | solution.py:396
  120.2 0.6 collective-permute-start.3
  120.7 2.1 %collective-permute-start.2 = (bf16[2,56,128]{2,1,0:T(8,128)(2,1)S(1)}, bf16[2,56,128]{2,1,0:T(8,128)(2,1)S(1)}, u32[]{:S(2)}, u32[]{:S(2)}) collective-permute-start(bf16[2,56,128]{2,1,0:T(8,128)(2,1)S(1)} %get-tuple-element.49), channel_id=1, source_target_pairs={{0,2},{1,3},{2,0},{3,1},{4,6},{5,7},{6,4},{7,5},{8,10},{9,11},{10,... | collective-permute-start | bytes 86024 | tf_op jit(solution)/shard_map/ppermute | solution.py:396
  122.8 0.4 collective-permute-done.1
  123.2 4.8 %collective-permute-done.2 = bf16[2,56,128]{2,1,0:T(8,128)(2,1)S(1)} collective-permute-done((bf16[2,56,128]{2,1,0:T(8,128)(2,1)S(1)}, bf16[2,56,128]{2,1,0:T(8,128)(2,1)S(1)}, u32[]{:S(2)}, u32[]{:S(2)}) %collective-permute-start.2) | collective-permute-done | bytes 28704 | tf_op jit(solution)/shard_map/ppermute | solution.py:396
  128.0 0.0 collective-permute-done.3
  128.0 1.2 collective-permute-start.6
  129.2 1.8 %collective-permute-start.5 = (bf16[8,56,128]{2,1,0:T(8,128)(2,1)S(1)}, bf16[8,56,128]{2,1,0:T(8,128)(2,1)S(1)}, u32[]{:S(2)}, u32[]{:S(2)}) collective-permute-start(bf16[8,56,128]{2,1,0:T(8,128)(2,1)S(1)} %constant_dynamic-update-slice_fusion.2.refs_1_), channel_id=1, source_target_pairs={{0,128},{64,192},{128,0},{192,64},{1,129},{65,193},{129,1},{193,65... | collective-permute-start | bytes 344072 | tf_op jit(solution)/shard_map/ppermute | solution.py:396
  131.0 0.0 collective-permute-start.4
  131.0 0.1 pad_add_fusion.refs_0_
  131.1 1.8 %collective-permute-done.6.refs_4_ = bf16[8,56,128]{2,1,0:T(8,128)(2,1)S(1)} collective-permute-done((bf16[8,56,128]{2,1,0:T(8,128)(2,1)S(1)}, bf16[8,56,128]{2,1,0:T(8,128)(2,1)S(1)}, u32[]{:S(2)}, u32[]{:S(2)}) %collective-permute-start.6) | collective-permute-done | bytes 114720 | tf_op jit(solution)/shard_map/ppermute | solution.py:396
  132.9 2.7 %collective-permute-done.5.refs_3_ = bf16[8,56,128]{2,1,0:T(8,128)(2,1)S(1)} collective-permute-done((bf16[8,56,128]{2,1,0:T(8,128)(2,1)S(1)}, bf16[8,56,128]{2,1,0:T(8,128)(2,1)S(1)}, u32[]{:S(2)}, u32[]{:S(2)}) %collective-permute-start.5) | collective-permute-done | bytes 114720 | tf_op jit(solution)/shard_map/ppermute | solution.py:396
  135.5 1.5 %collective-permute-done.4.refs_2_ = bf16[8,56,128]{2,1,0:T(8,128)(2,1)S(1)} collective-permute-done((bf16[8,56,128]{2,1,0:T(8,128)(2,1)S(1)}, bf16[8,56,128]{2,1,0:T(8,128)(2,1)S(1)}, u32[]{:S(2)}, u32[]{:S(2)}) %collective-permute-start.4) | collective-permute-done | bytes 114720 | tf_op jit(solution)/shard_map/ppermute | solution.py:396
  137.0 1.5 %shard_map.172 = (f32[256,512]{1,0:T(8,128)}, f32[256,256]{1,0:T(8,128)}, f32[32,64]{1,0:T(8,128)}) custom-call(s32[3]{0:T(128)S(1)} %pad_add_fusion.refs_0_, bf16[8,56,128]{2,1,0:T(8,128)(2,1)S(1)} %constant_dynamic-update-slice_fusion.2.refs_1_, bf16[8,56,128]{2,1,0:T(8,128)(2,1)S(1)} %collective-permute-done.4.refs_2_, ...), custom_call_target="tpu_custom_call" | custom-call | bytes 1253388 | tf_op jit(solution)/shard_map/pallas_call | solution.py:55
  138.6 0.6 all-to-all-done.6.recv
  139.1 1.2 shard_map.171
  (7 shorter events, 0.1 us)
Async XLA Ops:
  0.6 0.7 copy-start.10
  1.3 1.0 copy-start.1
  2.4 0.9 copy-start.3
  5.1 35.6 %copy-start = (bf16[256,512]{1,0:T(8,128)(2,1)S(1)}, bf16[256,512]{1,0:T(8,128)(2,1)}, u32[]{:S(2)}) copy-start(bf16[256,512]{1,0:T(8,128)(2,1)} %entrance.3) | copy-start | bytes 786436
  5.1 35.6 %copy-start.2 = (bf16[256,256]{1,0:T(8,128)(2,1)S(1)}, bf16[256,256]{1,0:T(8,128)(2,1)}, u32[]{:S(2)}) copy-start(bf16[256,256]{1,0:T(8,128)(2,1)} %exit_w.3) | copy-start | bytes 393220
  5.1 35.6 %copy-start.11 = (f32[8]{0:T(128)S(1)}, f32[8]{0:T(128)}, u32[]{:S(2)}) copy-start(f32[8]{0:T(128)} %param.21) | copy-start | bytes 100
  5.1 35.6 %all-to-all-start = ((bf16[32,104,128]{2,1,0:T(8,128)(2,1)}), bf16[32,104,128]{2,1,0:T(8,128)(2,1)S(1)}, u32[]{:S(2)}, u32[]{:S(2)}) async-start(bf16[32,104,128]{2,1,0:T(8,128)(2,1)} %shard_map.164), calls=%async_computation | async-start | bytes 1703936 | tf_op jit(solution)/shard_map/all_to_all | solution.py:393
  16.9 23.9 %copy-start.7 = (bf16[32,64]{1,0:T(8,128)(2,1)S(1)}, bf16[32,64]{1,0:T(8,128)(2,1)}, u32[]{:S(2)}) copy-start(bf16[32,64]{1,0:T(8,128)(2,1)} %portion.1) | copy-start | bytes 12292
  40.7 0.7 copy-start.8
  40.7 0.7 copy-start.9
  54.7 18.0 %copy-start.4 = (f32[32,32]{1,0:T(8,128)S(1)}, f32[32,32]{1,0:T(8,128)}, u32[]{:S(2)}) copy-start(f32[32,32]{1,0:T(8,128)} %request.1) | copy-start | bytes 12292
  54.7 18.0 %copy-start.5 = (f32[32,32]{1,0:T(8,128)S(1)}, f32[32,32]{1,0:T(8,128)}, u32[]{:S(2)}) copy-start(f32[32,32]{1,0:T(8,128)} %lookup.1) | copy-start | bytes 12292
  54.7 18.0 %copy-start.6 = (f32[32,32]{1,0:T(8,128)S(1)}, f32[32,32]{1,0:T(8,128)}, u32[]{:S(2)}) copy-start(f32[32,32]{1,0:T(8,128)} %content.1) | copy-start | bytes 12292
  111.9 27.3 %all-to-all-start.6 = ((bf16[32,48,256]{2,1,0:T(8,128)(2,1)}), bf16[32,48,256]{2,1,0:T(8,128)(2,1)S(1)}, u32[]{:S(2)}, u32[]{:S(2)}) async-start(bf16[32,48,256]{2,1,0:T(8,128)(2,1)} %get-tuple-element.42), calls=%async_computation.6 | async-start | bytes 1572864 | tf_op jit(solution)/shard_map/all_to_all | solution.py:393
  117.3 1.3 collective-permute-start
  118.6 4.5 %collective-permute-start.1 = (bf16[2,56,128]{2,1,0:T(8,128)(2,1)S(1)}, bf16[2,56,128]{2,1,0:T(8,128)(2,1)S(1)}, u32[]{:S(2)}, u32[]{:S(2)}) collective-permute-start(bf16[2,56,128]{2,1,0:T(8,128)(2,1)S(1)} %get-tuple-element.49), channel_id=1, source_target_pairs={{0,1},{1,2},{2,3},{3,0},{4,5},{5,6},{6,7},{7,4},{8,9},{9,10},{10,1... | collective-permute-start | bytes 86024 | tf_op jit(solution)/shard_map/ppermute | solution.py:396
  120.2 7.8 %collective-permute-start.3 = (bf16[2,56,128]{2,1,0:T(8,128)(2,1)S(1)}, bf16[2,56,128]{2,1,0:T(8,128)(2,1)S(1)}, u32[]{:S(2)}, u32[]{:S(2)}) collective-permute-start(bf16[2,56,128]{2,1,0:T(8,128)(2,1)S(1)} %get-tuple-element.49), channel_id=1, source_target_pairs={{0,3},{1,0},{2,1},{3,2},{4,7},{5,4},{6,5},{7,6},{8,11},{9,8},{10,9... | collective-permute-start | bytes 86024 | tf_op jit(solution)/shard_map/ppermute | solution.py:396
  120.7 7.3 %collective-permute-start.2 = (bf16[2,56,128]{2,1,0:T(8,128)(2,1)S(1)}, bf16[2,56,128]{2,1,0:T(8,128)(2,1)S(1)}, u32[]{:S(2)}, u32[]{:S(2)}) collective-permute-start(bf16[2,56,128]{2,1,0:T(8,128)(2,1)S(1)} %get-tuple-element.49), channel_id=1, source_target_pairs={{0,2},{1,3},{2,0},{3,1},{4,6},{5,7},{6,4},{7,5},{8,10},{9,11},{10,... | collective-permute-start | bytes 86024 | tf_op jit(solution)/shard_map/ppermute | solution.py:396
  128.0 4.9 %collective-permute-start.6 = (bf16[8,56,128]{2,1,0:T(8,128)(2,1)S(1)}, bf16[8,56,128]{2,1,0:T(8,128)(2,1)S(1)}, u32[]{:S(2)}, u32[]{:S(2)}) collective-permute-start(bf16[8,56,128]{2,1,0:T(8,128)(2,1)S(1)} %constant_dynamic-update-slice_fusion.2.refs_1_), channel_id=1, source_target_pairs={{0,192},{64,0},{128,64},{192,128},{1,193},{65,1},{129,65},{193,129... | collective-permute-start | bytes 344072 | tf_op jit(solution)/shard_map/ppermute | solution.py:396
  129.2 6.3 %collective-permute-start.5 = (bf16[8,56,128]{2,1,0:T(8,128)(2,1)S(1)}, bf16[8,56,128]{2,1,0:T(8,128)(2,1)S(1)}, u32[]{:S(2)}, u32[]{:S(2)}) collective-permute-start(bf16[8,56,128]{2,1,0:T(8,128)(2,1)S(1)} %constant_dynamic-update-slice_fusion.2.refs_1_), channel_id=1, source_target_pairs={{0,128},{64,192},{128,0},{192,64},{1,129},{65,193},{129,1},{193,65... | collective-permute-start | bytes 344072 | tf_op jit(solution)/shard_map/ppermute | solution.py:396
  131.0 6.0 %collective-permute-start.4 = (bf16[8,56,128]{2,1,0:T(8,128)(2,1)S(1)}, bf16[8,56,128]{2,1,0:T(8,128)(2,1)S(1)}, u32[]{:S(2)}, u32[]{:S(2)}) collective-permute-start(bf16[8,56,128]{2,1,0:T(8,128)(2,1)S(1)} %constant_dynamic-update-slice_fusion.2.refs_1_), channel_id=1, source_target_pairs={{0,64},{64,128},{128,192},{192,0},{1,65},{65,129},{129,193},{193,1... | collective-permute-start | bytes 344072 | tf_op jit(solution)/shard_map/ppermute | solution.py:396

commit v3 on v2

--- a/solution.py
+++ b/solution.py
@@ -46,20 +46,21 @@
     return lax.broadcasted_iota(jnp.int32, shape, dim)
 
 
-def call(body, outs, *args, scalars=0, scratch=(), flops=0, vmem=40):
+def call(body, outs, *args, scalars=0, hbm=False, hbm_out=False, scratch=(), vmem=40):
     vm = pl.BlockSpec(memory_space=pltpu.VMEM)
     sm = pl.BlockSpec(memory_space=pltpu.SMEM)
+    far = pl.BlockSpec(memory_space=pltpu.HBM)
     single = not isinstance(outs, (list, tuple))
     listed = [outs] if single else list(outs)
     moved = sum(math.prod(a.shape) * a.dtype.itemsize for a in list(args) + listed)
     res = pl.pallas_call(
         body,
         out_shape=listed,
-        in_specs=[sm] * scalars + [vm] * (len(args) - scalars),
-        out_specs=[vm] * len(listed),
+        in_specs=[sm] * scalars + [far if hbm else vm] * (len(args) - scalars),
+        out_specs=[far if hbm_out else vm] * len(listed),
         scratch_shapes=list(scratch),
         compiler_params=pltpu.CompilerParams(vmem_limit_bytes=vmem * 2**20),
-        cost_estimate=pl.CostEstimate(flops=flops, bytes_accessed=moved, transcendentals=0),
+        cost_estimate=pl.CostEstimate(flops=0, bytes_accessed=moved, transcendentals=0),
     )(*args)
     return res[0] if single else res
 
@@ -86,17 +87,26 @@
     return (source == kept).astype(F32).astype(BF16)
 
 
-def pack_kernel(tally, plan, cells, cot, out):
+def pack_kernel(tally_hbm, plan_hbm, cells, cot, out, tally, plan, rows, sent, small_sem, in_sem, out_sem):
+    small = [
+        pltpu.make_async_copy(tally_hbm, tally, small_sem.at[0]),
+        pltpu.make_async_copy(plan_hbm, plan, small_sem.at[1]),
+    ]
+    for copy in small:
+        copy.start()
+    reads = []
+    for j in range(8):
+        at = pl.ds(16 * j, 16)
+        pair = [
+            pltpu.make_async_copy(cells.at[:, at, :], rows.at[j, 0:SIN], in_sem.at[j, 0]),
+            pltpu.make_async_copy(cot.at[:, at, :], rows.at[j, SIN : SIN + SOUT], in_sem.at[j, 1]),
+        ]
+        for copy in pair:
+            copy.start()
+        reads.append(pair)
     order = piece_order(False)
-    for j in range(8):
-        at = 16 * j
-        rows = [cells[s * BLK + at : s * BLK + at + 16, :] for s in range(SIN)]
-        rows += [cot[t * BLK + at : t * BLK + at + 16, :] for t in range(SOUT)]
-        moved = mm(order, jnp.concatenate(rows, axis=0)).astype(BF16)
-        for a in range(4):
-            part = moved[a * SEND : (a + 1) * SEND]
-            out[4 * j + a, 0:SEND, :] = part[:, 0:128]
-            out[4 * j + a, SEND : 2 * SEND, :] = part[:, 128:C]
+    for copy in small:
+        copy.wait()
     block = iota((META, 128), 1) >> 2
     target = jnp.zeros((META, 128), jnp.int32)
     for s in range(SIN):
@@ -104,26 +114,48 @@
     held = jnp.clip(tally[0] - block * BLK, 0, BLK)
     meta = jnp.where(iota((META, 128), 0) < 4, target, held).astype(F32).astype(BF16)
     for j in range(GY):
-        out[j, 2 * SEND : TALL, :] = meta
-
-
-def unpack_kernel(recv, result, cell_grad):
-    order = piece_order(True)
+        sent[j, 2 * SEND : TALL, :] = meta
+    writes = []
     for j in range(8):
-        at = 16 * j
-        rows = jnp.concatenate([recv[4 * j + a] for a in range(4)], axis=0)
-        moved = mm(order, rows).astype(BF16)
-        for s in range(SIN):
-            cell_grad[s * BLK + at : s * BLK + at + 16, :] = moved[s * 16 : s * 16 + 16]
-        for t in range(SOUT):
-            u = SIN + t
-            result[t * BLK + at : t * BLK + at + 16, :] = moved[u * 16 : u * 16 + 16]
+        for copy in reads[j]:
+            copy.wait()
+        moved = mm(order, rows[j].reshape(GROUP, C)).astype(BF16)
+        for a in range(4):
+            part = moved[a * SEND : (a + 1) * SEND]
+            sent[4 * j + a, 0:SEND, :] = part[:, 0:128]
+            sent[4 * j + a, SEND : 2 * SEND, :] = part[:, 128:C]
+        group = pl.ds(4 * j, 4)
+        copy = pltpu.make_async_copy(sent.at[group], out.at[group], out_sem.at[j])
+        copy.start()
+        writes.append(copy)
+    for copy in writes:
+        copy.wait()
+
+
+def weight_kernel(
+    gain, entrance, portion, softness, base, exit_w,
+    entrance_t, exit_t, spread_out, soft_spread_out, gain_out, base_out, soft_out,
+):
+    eye = (iota((C, C), 0) == iota((C, C), 1)).astype(F32).astype(BF16)
+    entrance_t[...] = mm(entrance[...], eye, TN).astype(BF16)
+    exit_t[...] = mm(exit_w[...], eye, TN).astype(BF16)
+    tall = ((iota((C, WIDTH), 0) & 31) == iota((C, WIDTH), 1)).astype(F32).astype(BF16)
+    broad = ((iota((SLICES, 512), 1) & 63) == iota((SLICES, 512), 0)).astype(F32).astype(BF16)
+    spread = mm(mm(tall, portion[...]).astype(BF16), broad)
+    same = (iota((C, 512), 0) >> 5) == (iota((C, 512), 1) >> 6)
+    spread_out[...] = jnp.where(same, spread, 0.0).astype(BF16)
+    soft_row = mm(softness[...], tall, NT)
+    soft_same = (iota((16, C), 1) >> 5) == iota((16, C), 0)
+    soft_spread_out[...] = jnp.where(soft_same, soft_row, 0.0).astype(BF16)
+    gain_out[...] = jnp.broadcast_to(column(gain[...]), (C, 128))
+    base_out[...] = jnp.broadcast_to(column(base[...]), (HEADS, 128))
+    soft_out[...] = jnp.broadcast_to(column(softness[...].astype(F32)), (WIDTH, 128))
 
 
 def forward_kernel(
-    spot, recv, gain, entrance, portion, softness, base, exit_w,
+    spot, recv, entrance_t, exit_w, spread, soft_spread, gain_col, base_col,
     token, pick, xt_out, normed_out, proj_out, prob_out, scaled_out, slice_out,
-    uns_out, cot_out, rows_out, heads_out, spread_out,
+    uns_out, cot_out, rows_out, heads_out,
 ):
     mine = spot[0]
     cells = jnp.concatenate(
@@ -151,14 +183,16 @@
         dest = jnp.where((lane >> 2) == s, found, dest)
     row_in_block = (mine * PIECE + (lane & 3)).astype(F32)
     dest = jnp.where(row_in_block < held, dest, 0.0) - 1.0
-    repeat = ((iota((HOME, GY), 0) >> 5) == iota((HOME, GY), 1)).astype(F32).astype(BF16)
-    wide = mm(repeat, dest.astype(BF16))
-    own = iota((HOME, 128), 1) == (iota((HOME, 128), 0) & 31)
-    dest_col = jnp.sum(jnp.where(own, wide, 0.0), axis=1, keepdims=True)
-    k_col = (iota((HOME, 1), 0) & 3).astype(F32)
-    spot_col = (dest_col * 4.0 + k_col).astype(jnp.int32)
-    pick[...] = (spot_col == iota((HOME, ROWS), 1)).astype(F32).astype(BF16)
-    live = mm(jnp.ones((8, HOME), BF16), pick[...])[0:1, :]
+    flip = (iota((128, 128), 0) == iota((128, 128), 1)).astype(F32).astype(BF16)
+    slots = mm(flip, dest.astype(BF16), NT)[0:32, :]
+    slots = (slots * 4.0 + (iota((32, GY), 0) & 3).astype(F32)).astype(jnp.int32)
+    at_row = iota((32, ROWS), 1)
+    seen = jnp.zeros((32, ROWS), F32)
+    for p in range(GY):
+        match = (slots[:, p : p + 1] == at_row).astype(F32)
+        seen = seen + match
+        pick[p * 32 : (p + 1) * 32, :] = match.astype(BF16)
+    live = jnp.sum(seen, axis=0, keepdims=True)
 
     xt = mm(cells, pick[...], TN)
     xt_out[...] = xt.astype(BF16)
@@ -166,30 +200,20 @@
     centered = xt - mean
     var = jnp.sum(centered * centered, axis=0, keepdims=True) * (1.0 / C)
     inv = lax.rsqrt(var + norm_eps)
-    gain_col = column(gain[...])
-    normed = (centered * inv * gain_col).astype(BF16)
+    normed = (centered * inv * gain_col[:, 0:1]).astype(BF16)
     normed_out[...] = normed
-    proj_out[...] = mm(entrance[...], normed, TN).astype(BF16)
+    proj_out[...] = mm(entrance_t[...], normed).astype(BF16)
     rows_out[0:1, :] = live
     rows_out[1:2, :] = mean
     rows_out[2:3, :] = inv
 
-    tall = ((iota((C, WIDTH), 0) & 31) == iota((C, WIDTH), 1)).astype(F32).astype(BF16)
-    broad = ((iota((SLICES, 512), 1) & 63) == iota((SLICES, 512), 0)).astype(F32).astype(BF16)
-    spread = mm(mm(tall, portion[...]).astype(BF16), broad)
-    same = (iota((C, 512), 0) >> 5) == (iota((C, 512), 1) >> 6)
-    spread_out[...] = jnp.where(same, spread, 0.0).astype(BF16)
-    soft_row = mm(softness[...], tall, NT)
-    soft_same = (iota((HEADS, C), 1) >> 5) == iota((HEADS, C), 0)
-    soft_spread = jnp.where(soft_same, soft_row, 0.0).astype(BF16)
-
     mid = proj_out[C : 2 * C, :]
-    presq = mm(soft_spread, mid)
+    presq = mm(soft_spread[...], mid)[0:HEADS]
     softplus = jnp.maximum(presq, 0.0) + jnp.log1p(jnp.exp(-jnp.abs(presq)))
-    inv_temp = 1.0 / (column(base[...]) + softplus)
+    inv_temp = 1.0 / (base_col[:, 0:1] + softplus)
     heads_out[0:8, :] = inv_temp
     heads_out[8:16, :] = presq
-    scaled_out[...] = mm(spread_out[...], mid, TN)
+    scaled_out[...] = mm(spread[...], mid, TN)
 
     back = mm(exit_w[...], cot, NT) * live
     uns_out[...] = back.astype(BF16)
@@ -270,9 +294,9 @@
 
 
 def backward_kernel(
-    mix, gain, entrance, softness, exit_w,
+    mix, entrance, exit_t, spread, gain_col, soft_col,
     pick, xt_in, normed_in, proj_in, prob_in, scaled_in, slice_in,
-    uns_in, cot_in, rows_in, heads_in, spread_in,
+    uns_in, cot_in, rows_in, heads_in,
     send, grads, weave, stack, gprob, affs, gproj,
 ):
     live = rows_in[0:1, :]
@@ -310,7 +334,7 @@
     deslice = rows[0:C].astype(BF16)
     gproj[0:C, :] = rows[C : 2 * C].astype(BF16)
     gprob[...] = mm(weave[...], stack[...], TN)
-    branch = mm(exit_w[...], deslice, TN)
+    branch = mm(exit_t[...], deslice)
     xt = xt_in[...].astype(F32)
     result = (live * (xt + branch)).astype(BF16)
     eye = (iota((ROWS, ROWS), 0) == iota((ROWS, ROWS), 1)).astype(F32).astype(BF16)
@@ -334,12 +358,11 @@
         affs[at : at + SLICES, :] = (adj * inv_temp).astype(BF16)
         pulled = jnp.sum(adj * scaled_in[at : at + SLICES, :], axis=0, keepdims=True)
         softs.append(-pulled * inv_temp * (1.0 / (1.0 + jnp.exp(-presq))))
-    between = mm(spread_in[...], affs[...])
-    soft_col = column(softness[...].astype(F32))
+    between = mm(spread[...], affs[...])
     slice_grad = jnp.zeros((WIDTH, SLICES), F32)
     for h in range(HEADS):
         at = h * WIDTH
-        part = between[at : at + WIDTH] + soft_col * softs[h]
+        part = between[at : at + WIDTH] + soft_col[:, 0:1] * softs[h]
         gproj[C + at : C + at + WIDTH, :] = part.astype(BF16)
         slice_grad = slice_grad + mm(
             proj_in[C + at : C + at + WIDTH, :], affs[h * SLICES : (h + 1) * SLICES, :], NT
@@ -351,7 +374,7 @@
     grads[6 * C : 6 * C + WIDTH, :] = tail.astype(grads.dtype)
     grads[6 * C + WIDTH :, :] = jnp.zeros((GY * GRAD_ROWS - 6 * C - WIDTH, 128), grads.dtype)
 
-    g_unit = mm(entrance[...], gproj[...]) * column(gain[...])
+    g_unit = mm(entrance[...], gproj[...]) * gain_col[:, 0:1]
     unit = (xt - mean) * inv
     m1 = jnp.sum(g_unit, axis=0, keepdims=True) * (1.0 / C)
     m2 = jnp.sum(g_unit * unit, axis=0, keepdims=True) * (1.0 / C)
@@ -361,7 +384,9 @@
         send[q, 0 : SIN * PIECE, :] = cell_rows[q * 32 : (q + 1) * 32]
 
 
-def weight_kernel(scale, at, r0, r1, r2, r3, grad_in, grad_out, grad_slice, flat):
+def gather_kernel(
+    scale, at, r0, r1, r2, r3, grad_in, grad_out, grad_slice, flat, tail, sem
+):
     y, core, x = at[0], at[1], at[2]
     for dy, recv in enumerate((r0, r1, r2, r3)):
         for dx in range(4):
@@ -369,15 +394,39 @@
                 index = (((y - dy) & 3) * 2 + (core ^ dc)) * 4 + ((x - dx) & 3)
                 start = pl.multiple_of(index * GRAD_ROWS, 8)
                 flat[pl.ds(start, GRAD_ROWS), :] = recv[dx * 2 + dc].astype(F32) * scale
-
-    def part(b):
-        return flat[b * C : (b + 1) * C, :]
-
-    for b in range(4):
-        grad_in[:, b * 128 : (b + 1) * 128] = part(b)
-    for b in range(2):
-        grad_out[:, b * 128 : (b + 1) * 128] = part(4 + b)
-    grad_slice[...] = flat[6 * C : 6 * C + WIDTH, 0:SLICES]
+    tail[...] = flat[6 * C : 6 * C + WIDTH, 0:SLICES]
+    copies = []
+    for b in range(6):
+        out, c = (grad_in, b) if b < 4 else (grad_out, b - 4)
+        target = out.at[:, c * 128 : (c + 1) * 128]
+        copies.append(pltpu.make_async_copy(flat.at[b * C : (b + 1) * C], target, sem.at[b]))
+    copies.append(pltpu.make_async_copy(tail, grad_slice, sem.at[6]))
+    for copy in copies:
+        copy.start()
+    for copy in copies:
+        copy.wait()
+
+
+def unpack_kernel(home, result, cell_grad, cells, rows, sem):
+    copies = []
+    order = piece_order(True)
+    for j in range(8):
+        got = jnp.concatenate([home[4 * j + a] for a in range(4)], axis=0)
+        moved = mm(order, got).astype(BF16)
+        span = pl.ds(16 * j, 16)
+        cells[:, span, :] = moved[0 : SIN * 16].reshape(SIN, 16, C)
+        rows[:, span, :] = moved[SIN * 16 :].reshape(SOUT, 16, C)
+        if j % 2 == 1:
+            both = pl.ds(16 * (j - 1), 32)
+            pair = [
+                pltpu.make_async_copy(cells.at[:, both, :], cell_grad.at[:, both, :], sem.at[j - 1]),
+                pltpu.make_async_copy(rows.at[:, both, :], result.at[:, both, :], sem.at[j]),
+            ]
+            for copy in pair:
+                copy.start()
+            copies += pair
+    for copy in copies:
+        copy.wait()
 
 
 def shards(
@@ -396,7 +445,34 @@
         return lax.ppermute(x, axis, [(i, (i + d) % n) for i in range(n)])
 
     sent = call(
-        pack_kernel, sds((GY, TALL, 128), BF16), tally, plan, cells, cot, scalars=2
+        pack_kernel,
+        sds((GY, TALL, 128), BF16),
+        tally, plan, cells.reshape(SIN, BLK, C), cot.reshape(SOUT, BLK, C),
+        hbm=True,
+        hbm_out=True,
+        vmem=62,
+        scratch=[
+            pltpu.SMEM((1,), jnp.int32),
+            pltpu.SMEM((1, SIN), jnp.int32),
+            pltpu.VMEM((8, SIN + SOUT, 16, C), BF16),
+            pltpu.VMEM((GY, TALL, 128), BF16),
+            pltpu.SemaphoreType.DMA((2,)),
+            pltpu.SemaphoreType.DMA((8, 2)),
+            pltpu.SemaphoreType.DMA((8,)),
+        ],
+    )
+    entrance_t, exit_t, spread, soft_spread, gain_col, base_col, soft_col = call(
+        weight_kernel,
+        [
+            sds((2 * C, C), BF16),
+            sds((C, C), BF16),
+            sds((C, 512), BF16),
+            sds((16, C), BF16),
+            sds((C, 128), F32),
+            sds((HEADS, 128), F32),
+            sds((WIDTH, 128), F32),
+        ],
+        gain, entrance, portion, softness, base, exit_w,
     )
     recv = swap(sent, ("z", "x"))
     spot = (lax.axis_index("z") * 4 + lax.axis_index("x")).astype(jnp.int32).reshape(1)
@@ -415,9 +491,8 @@
             sds((C, ROWS), BF16),
             sds((8, ROWS), F32),
             sds((16, ROWS), F32),
-            sds((C, 512), BF16),
         ],
-        spot, recv, gain, entrance, portion, softness, base, exit_w,
+        spot, recv, entrance_t, exit_w, spread, soft_spread, gain_col, base_col,
         scalars=1,
     )
     token, saved = state[0], state[1:]
@@ -430,7 +505,7 @@
     send, grads = call(
         backward_kernel,
         [sds((GY, SEND, C), BF16), sds((GY * GRAD_ROWS, 128), BF16)],
-        mix, gain, entrance, softness, exit_w, *saved,
+        mix, entrance, exit_t, spread, gain_col, soft_col, *saved,
         scratch=[
             pltpu.VMEM((2 * C + 16, 512), BF16),
             pltpu.VMEM((2 * C + 16, ROWS), BF16),
@@ -449,15 +524,30 @@
     gathered = [grads] + [shifted(grads, "y", 4, d) for d in (1, 2, 3)]
     at = jnp.stack([lax.axis_index(a) for a in ("y", "core", "x")]).astype(jnp.int32)
     result, cell_grad = call(
-        unpack_kernel, [sds((SOUT * BLK, C), BF16), sds((SIN * BLK, C), BF16)], home
+        unpack_kernel,
+        [sds((SOUT, BLK, C), BF16), sds((SIN, BLK, C), BF16)],
+        home,
+        hbm_out=True,
+        scratch=[
+            pltpu.VMEM((SIN, BLK, C), BF16),
+            pltpu.VMEM((SOUT, BLK, C), BF16),
+            pltpu.SemaphoreType.DMA((8,)),
+        ],
     )
     grad_in, grad_out, grad_slice = call(
-        lambda *refs: weight_kernel(scale, *refs),
+        lambda *refs: gather_kernel(scale, *refs),
         [sds((C, 2 * C), F32), sds((C, C), F32), sds((WIDTH, SLICES), F32)],
         at, *gathered,
         scalars=1,
-        scratch=[pltpu.VMEM((GY * GRAD_ROWS, 128), F32)],
-    )
+        hbm_out=True,
+        scratch=[
+            pltpu.VMEM((GY * GRAD_ROWS, 128), F32),
+            pltpu.VMEM((WIDTH, SLICES), F32),
+            pltpu.SemaphoreType.DMA((7,)),
+        ],
+    )
+    result = result.reshape(SOUT * BLK, C)
+    cell_grad = cell_grad.reshape(SIN * BLK, C)
     return result, cell_grad, grad_in, grad_out, grad_slice
 
 

time: 141 us -> 139 us (0.986)
  local copies, waits for them, and re-layouts: 2.72 us -> 0.73 us
    unnamed x27 -> x21, local copies, waits for them, and re-layouts: 2.7 us -> 0.71 us
    pallas_call x9 -> x10, Pallas kernels: 12.5 us -> 13.7 us  [call(): pl.pallas_call(body, out_shape=listed, in_specs=[sm] * scalars + [far if...]
where the time goes in v3:
time: 139 us; the launch traced here: 138 us
  blocking collectives  62.5 us (45%)
  waiting for transfers between devices  35.5 us (26%)
  starting transfers between devices  24.5 us (18%)
  Pallas kernels  13.7 us (10%)
  between operations  1.47 us (1%)
    all_to_all x5, blocking collectives, swap(): return lax.all_to_all(x, axes, 0, 0, tiled=True)  62.5 us
    all_to_all x2, waiting for transfers between devices, swap(): return lax.all_to_all(x, axes, 0, 0, tiled=True)  23.2 us
    all_to_all x2, starting transfers between devices, swap(): return lax.all_to_all(x, axes, 0, 0, tiled=True)  17.2 us
    pallas_call x10, Pallas kernels, call(): pl.pallas_call(body, out_shape=listed, in_specs=[sm] * scalars + [far if...  13.7 us
    ppermute x7, waiting for transfers between devices, shifted(): return lax.ppermute(x, axis, [(i, (i + d) % n) for i in range(n)])  12.3 us
    ppermute x7, starting transfers between devices, shifted(): return lax.ppermute(x, axis, [(i, (i + d) % n) for i in range(n)])  7.29 us
  transfers between devices with their start and end apart: 9, of which 8 were waited for; matrix products, arithmetic and copies ran while one was open for 0% of the time, Pallas kernels for 1%

profile of v3, /device:TPU:2, one launch (start us, length us, event | category | flops | bytes accessed | tf_op | source)
XLA Modules:
  0.0 138.5 jit_solution(6282909979546261682)
XLA Ops:
  1.3 3.3 %shard_map.164 = bf16[32,104,128]{2,1,0:T(8,128)(2,1)} custom-call(s32[1]{0:T(128)S(6)} %copy.23.tally_hbm, s32[1,8]{1,0:T(1,128)} %plan_hbm.1, bf16[8,128,256]{2,1,0:T(8,128)(2,1)} %bitcast.16, bf16[4,128,256]{2,1,0:T(8,128)(2,1)} %bitcast.17), custom_call_target="tpu_custom_call" | custom-call | bytes 1638436 | tf_op jit(solution)/shard_map/pallas_call | solution.py:56
  4.6 0.0 copy-start
  4.6 0.0 copy-start.1
  4.6 0.0 copy-start.8
  4.6 11.8 %all-to-all-start = ((bf16[32,104,128]{2,1,0:T(8,128)(2,1)}), bf16[32,104,128]{2,1,0:T(8,128)(2,1)S(1)}, u32[]{:S(2)}, u32[]{:S(2)}) async-start(bf16[32,104,128]{2,1,0:T(8,128)(2,1)} %shard_map.164), calls=%async_computation | async-start | bytes 1703936 | tf_op jit(solution)/shard_map/all_to_all | solution.py:442
  16.4 0.0 copy-start.5
  16.4 0.0 copy-start.6
  16.4 0.0 copy-start.7
  16.4 0.0 copy-done
  16.4 0.0 copy-done.1
  16.4 0.0 copy-done.8
  16.4 0.6 copy-done.5
  17.1 0.0 copy-done.6
  17.1 0.0 copy-done.7
  17.1 0.5 shard_map.165
  17.5 22.7 %all-to-all-done.recv = bf16[32,104,128]{2,1,0:T(8,128)(2,1)S(1)} async-done(((bf16[32,104,128]{2,1,0:T(8,128)(2,1)}), bf16[32,104,128]{2,1,0:T(8,128)(2,1)S(1)}, u32[]{:S(2)}, u32[]{:S(2)}) %all-to-all-start) | async-done | bytes 852000 | tf_op jit(solution)/shard_map/all_to_all | solution.py:442
  40.2 2.6 %shard_map.166 = (bf16[8,40,128]{2,1,0:T(8,128)(2,1)S(1)}, bf16[1024,512]{1,0:T(8,128)(2,1)S(1)}, bf16[256,512]{1,0:T(8,128)(2,1)S(1)}, bf16[256,512]{1,0:T(8,12...) custom-call(s32[1]{0:T(128)} %bitcast.spot, ...), custom_call_target="tpu_custom_call" | custom-call | bytes 7024644 | tf_op jit(solution)/shard_map/pallas_call | solution.py:56
  42.8 10.0 %all_to_all.35.recv = bf16[8,40,128]{2,1,0:T(8,128)(2,1)S(1)} all-to-all(bf16[8,40,128]{2,1,0:T(8,128)(2,1)S(1)} %get-tuple-element.38), channel_id=1, replica_groups=mesh['y'=4,'core'=2,'z'=8,'x'=4] {'y','core'}, dimensions={0} | all-to-all | bytes 163840 | tf_op jit(solution)/shard_map/all_to_all | solution.py:442
  52.9 0.0 copy-start.2
  52.9 0.0 copy-start.3
  52.9 0.0 copy-start.4
  52.9 18.0 %all_to_all.36.recv = bf16[32,40,128]{2,1,0:T(8,128)(2,1)S(1)} all-to-all(bf16[32,40,128]{2,1,0:T(8,128)(2,1)S(1)} %shard_map.167), channel_id=1, replica_groups=mesh['y'=4,'core'=2,'z'=8,'x'=4] {'z','x'}, dimensions={0} | all-to-all | bytes 655360 | tf_op jit(solution)/shard_map/all_to_all | solution.py:442
  70.9 0.0 copy-done.2
  70.9 0.0 copy-done.3
  70.9 0.0 copy-done.4
  70.9 1.2 shard_map.168
  72.1 8.2 %all_to_all.37.mix = bf16[8,48,128]{2,1,0:T(8,128)(2,1)S(1)} all-to-all(bf16[8,48,128]{2,1,0:T(8,128)(2,1)S(1)} %shard_map.168), channel_id=1, replica_groups=mesh['y'=4,'core'=2,'z'=8,'x'=4] {'y','core'}, dimensions={0} | all-to-all | bytes 196608 | tf_op jit(solution)/shard_map/all_to_all | solution.py:442
  80.2 3.4 %shard_map.169 = (bf16[32,48,256]{2,1,0:T(8,128)(2,1)}, bf16[1792,128]{1,0:T(8,128)(2,1)S(1)}) custom-call(bf16[8,48,128]{2,1,0:T(8,128)(2,1)S(1)} %all_to_all.37.mix, bf16[256,512]{1,0:T(8,128)(2,1)S(1)} %copy-done, bf16[256,256]{1,0:T(8,128)(2,1)S(1)} %get-tuple-element.39.exit_t, bf16[256,512]{1,0:T(8,128)(2,1)S(1)} %get-tuple-element.34.spread, ...), custom_call_target="tpu_custom_call" | custom-call | bytes 7438336 | tf_op jit(solution)/shard_map/pallas_call | solution.py:56
  83.6 14.0 %all_to_all.38.recv = bf16[32,56,128]{2,1,0:T(8,128)(2,1)S(1)} all-to-all(bf16[32,56,128]{2,1,0:T(8,128)(2,1)S(1)} %bitcast.12), channel_id=1, replica_groups=mesh['y'=4,'core'=2,'z'=8,'x'=4] {'y','core','x'}, dimensions={0} | all-to-all | bytes 917504 | tf_op jit(solution)/shard_map/all_to_all | solution.py:442
  97.6 0.1 shard_map.170
  97.7 12.4 %all_to_all.39.recv = bf16[8,56,128]{2,1,0:T(8,128)(2,1)S(1)} all-to-all(bf16[8,56,128]{2,1,0:T(8,128)(2,1)S(1)} %shard_map.170), channel_id=1, replica_groups=mesh['y'=4,'core'=2,'z'=8,'x'=4] {'z'}, dimensions={0} | all-to-all | bytes 229376 | tf_op jit(solution)/shard_map/all_to_all | solution.py:442
  110.1 5.5 %all-to-all-start.6 = ((bf16[32,48,256]{2,1,0:T(8,128)(2,1)}), bf16[32,48,256]{2,1,0:T(8,128)(2,1)S(1)}, u32[]{:S(2)}, u32[]{:S(2)}) async-start(bf16[32,48,256]{2,1,0:T(8,128)(2,1)} %get-tuple-element.54), calls=%async_computation.6 | async-start | bytes 1572864 | tf_op jit(solution)/shard_map/all_to_all | solution.py:442
  115.5 0.1 collective-permute-start
  115.6 1.2 collective-permute-done
  116.8 1.5 %collective-permute-start.1 = (bf16[2,56,128]{2,1,0:T(8,128)(2,1)S(1)}, bf16[2,56,128]{2,1,0:T(8,128)(2,1)S(1)}, u32[]{:S(2)}, u32[]{:S(2)}) collective-permute-start(bf16[2,56,128]{2,1,0:T(8,128)(2,1)S(1)} %get-tuple-element.61), channel_id=1, source_target_pairs={{0,1},{1,2},{2,3},{3,0},{4,5},{5,6},{6,7},{7,4},{8,9},{9,10},{10,1... | collective-permute-start | bytes 86024 | tf_op jit(solution)/shard_map/ppermute | solution.py:445
  118.3 0.6 collective-permute-start.3
  118.9 2.1 %collective-permute-start.2 = (bf16[2,56,128]{2,1,0:T(8,128)(2,1)S(1)}, bf16[2,56,128]{2,1,0:T(8,128)(2,1)S(1)}, u32[]{:S(2)}, u32[]{:S(2)}) collective-permute-start(bf16[2,56,128]{2,1,0:T(8,128)(2,1)S(1)} %get-tuple-element.61), channel_id=1, source_target_pairs={{0,2},{1,3},{2,0},{3,1},{4,6},{5,7},{6,4},{7,5},{8,10},{9,11},{10,... | collective-permute-start | bytes 86024 | tf_op jit(solution)/shard_map/ppermute | solution.py:445
  121.0 0.4 collective-permute-done.1
  121.3 4.8 %collective-permute-done.2 = bf16[2,56,128]{2,1,0:T(8,128)(2,1)S(1)} collective-permute-done((bf16[2,56,128]{2,1,0:T(8,128)(2,1)S(1)}, bf16[2,56,128]{2,1,0:T(8,128)(2,1)S(1)}, u32[]{:S(2)}, u32[]{:S(2)}) %collective-permute-start.2) | collective-permute-done | bytes 28704 | tf_op jit(solution)/shard_map/ppermute | solution.py:445
  126.2 0.0 collective-permute-done.3
  126.2 1.2 collective-permute-start.6
  127.4 1.8 %collective-permute-start.5 = (bf16[8,56,128]{2,1,0:T(8,128)(2,1)S(1)}, bf16[8,56,128]{2,1,0:T(8,128)(2,1)S(1)}, u32[]{:S(2)}, u32[]{:S(2)}) collective-permute-start(bf16[8,56,128]{2,1,0:T(8,128)(2,1)S(1)} %constant_dynamic-update-slice_fusion.2.refs_1_), channel_id=1, source_target_pairs={{0,128},{64,192},{128,0},{192,64},{1,129},{65,193},{129,1},{193,65... | collective-permute-start | bytes 344072 | tf_op jit(solution)/shard_map/ppermute | solution.py:445
  129.2 0.0 collective-permute-start.4
  129.2 0.1 pad_add_fusion.refs_0_
  129.3 1.8 %collective-permute-done.6.refs_4_ = bf16[8,56,128]{2,1,0:T(8,128)(2,1)S(1)} collective-permute-done((bf16[8,56,128]{2,1,0:T(8,128)(2,1)S(1)}, bf16[8,56,128]{2,1,0:T(8,128)(2,1)S(1)}, u32[]{:S(2)}, u32[]{:S(2)}) %collective-permute-start.6) | collective-permute-done | bytes 114720 | tf_op jit(solution)/shard_map/ppermute | solution.py:445
  131.1 2.7 %collective-permute-done.5.refs_3_ = bf16[8,56,128]{2,1,0:T(8,128)(2,1)S(1)} collective-permute-done((bf16[8,56,128]{2,1,0:T(8,128)(2,1)S(1)}, bf16[8,56,128]{2,1,0:T(8,128)(2,1)S(1)}, u32[]{:S(2)}, u32[]{:S(2)}) %collective-permute-start.5) | collective-permute-done | bytes 114720 | tf_op jit(solution)/shard_map/ppermute | solution.py:445
  133.7 1.5 %collective-permute-done.4.refs_2_ = bf16[8,56,128]{2,1,0:T(8,128)(2,1)S(1)} collective-permute-done((bf16[8,56,128]{2,1,0:T(8,128)(2,1)S(1)}, bf16[8,56,128]{2,1,0:T(8,128)(2,1)S(1)}, u32[]{:S(2)}, u32[]{:S(2)}) %collective-permute-start.4) | collective-permute-done | bytes 114720 | tf_op jit(solution)/shard_map/ppermute | solution.py:445
  135.2 1.5 %shard_map.173 = (f32[256,512]{1,0:T(8,128)}, f32[256,256]{1,0:T(8,128)}, f32[32,64]{1,0:T(8,128)}) custom-call(s32[3]{0:T(128)S(1)} %pad_add_fusion.refs_0_, bf16[8,56,128]{2,1,0:T(8,128)(2,1)S(1)} %constant_dynamic-update-slice_fusion.2.refs_1_, bf16[8,56,128]{2,1,0:T(8,128)(2,1)S(1)} %collective-permute-done.4.refs_2_, ...), custom_call_target="tpu_custom_call" | custom-call | bytes 1253388 | tf_op jit(solution)/shard_map/pallas_call | solution.py:56
  136.8 0.6 all-to-all-done.6.home
  137.3 1.1 shard_map.172
  (7 shorter events, 0.1 us)
Async XLA Ops:
  4.6 11.9 %copy-start = (bf16[256,512]{1,0:T(8,128)(2,1)S(1)}, bf16[256,512]{1,0:T(8,128)(2,1)}, u32[]{:S(2)}) copy-start(bf16[256,512]{1,0:T(8,128)(2,1)} %entrance.3) | copy-start | bytes 786436
  4.6 11.8 %copy-start.1 = (bf16[256,256]{1,0:T(8,128)(2,1)S(1)}, bf16[256,256]{1,0:T(8,128)(2,1)}, u32[]{:S(2)}) copy-start(bf16[256,256]{1,0:T(8,128)(2,1)} %exit_w.3) | copy-start | bytes 393220
  4.6 11.8 %copy-start.8 = (f32[8]{0:T(128)S(1)}, f32[8]{0:T(128)}, u32[]{:S(2)}) copy-start(f32[8]{0:T(128)} %param.21) | copy-start | bytes 100
  4.6 35.6 %all-to-all-start = ((bf16[32,104,128]{2,1,0:T(8,128)(2,1)}), bf16[32,104,128]{2,1,0:T(8,128)(2,1)S(1)}, u32[]{:S(2)}, u32[]{:S(2)}) async-start(bf16[32,104,128]{2,1,0:T(8,128)(2,1)} %shard_map.164), calls=%async_computation | async-start | bytes 1703936 | tf_op jit(solution)/shard_map/all_to_all | solution.py:442
  16.4 0.7 copy-start.5
  16.4 0.7 copy-start.6
  16.4 0.7 copy-start.7
  52.9 18.0 %copy-start.2 = (f32[32,32]{1,0:T(8,128)S(1)}, f32[32,32]{1,0:T(8,128)}, u32[]{:S(2)}) copy-start(f32[32,32]{1,0:T(8,128)} %request.1) | copy-start | bytes 12292
  52.9 18.0 %copy-start.3 = (f32[32,32]{1,0:T(8,128)S(1)}, f32[32,32]{1,0:T(8,128)}, u32[]{:S(2)}) copy-start(f32[32,32]{1,0:T(8,128)} %lookup.1) | copy-start | bytes 12292
  52.9 18.0 %copy-start.4 = (f32[32,32]{1,0:T(8,128)S(1)}, f32[32,32]{1,0:T(8,128)}, u32[]{:S(2)}) copy-start(f32[32,32]{1,0:T(8,128)} %content.1) | copy-start | bytes 12292
  110.1 27.3 %all-to-all-start.6 = ((bf16[32,48,256]{2,1,0:T(8,128)(2,1)}), bf16[32,48,256]{2,1,0:T(8,128)(2,1)S(1)}, u32[]{:S(2)}, u32[]{:S(2)}) async-start(bf16[32,48,256]{2,1,0:T(8,128)(2,1)} %get-tuple-element.54), calls=%async_computation.6 | async-start | bytes 1572864 | tf_op jit(solution)/shard_map/all_to_all | solution.py:442
  115.5 1.3 collective-permute-start
  116.8 4.5 %collective-permute-start.1 = (bf16[2,56,128]{2,1,0:T(8,128)(2,1)S(1)}, bf16[2,56,128]{2,1,0:T(8,128)(2,1)S(1)}, u32[]{:S(2)}, u32[]{:S(2)}) collective-permute-start(bf16[2,56,128]{2,1,0:T(8,128)(2,1)S(1)} %get-tuple-element.61), channel_id=1, source_target_pairs={{0,1},{1,2},{2,3},{3,0},{4,5},{5,6},{6,7},{7,4},{8,9},{9,10},{10,1... | collective-permute-start | bytes 86024 | tf_op jit(solution)/shard_map/ppermute | solution.py:445
  118.3 7.8 %collective-permute-start.3 = (bf16[2,56,128]{2,1,0:T(8,128)(2,1)S(1)}, bf16[2,56,128]{2,1,0:T(8,128)(2,1)S(1)}, u32[]{:S(2)}, u32[]{:S(2)}) collective-permute-start(bf16[2,56,128]{2,1,0:T(8,128)(2,1)S(1)} %get-tuple-element.61), channel_id=1, source_target_pairs={{0,3},{1,0},{2,1},{3,2},{4,7},{5,4},{6,5},{7,6},{8,11},{9,8},{10,9... | collective-permute-start | bytes 86024 | tf_op jit(solution)/shard_map/ppermute | solution.py:445
  118.9 7.3 %collective-permute-start.2 = (bf16[2,56,128]{2,1,0:T(8,128)(2,1)S(1)}, bf16[2,56,128]{2,1,0:T(8,128)(2,1)S(1)}, u32[]{:S(2)}, u32[]{:S(2)}) collective-permute-start(bf16[2,56,128]{2,1,0:T(8,128)(2,1)S(1)} %get-tuple-element.61), channel_id=1, source_target_pairs={{0,2},{1,3},{2,0},{3,1},{4,6},{5,7},{6,4},{7,5},{8,10},{9,11},{10,... | collective-permute-start | bytes 86024 | tf_op jit(solution)/shard_map/ppermute | solution.py:445
  126.2 4.9 %collective-permute-start.6 = (bf16[8,56,128]{2,1,0:T(8,128)(2,1)S(1)}, bf16[8,56,128]{2,1,0:T(8,128)(2,1)S(1)}, u32[]{:S(2)}, u32[]{:S(2)}) collective-permute-start(bf16[8,56,128]{2,1,0:T(8,128)(2,1)S(1)} %constant_dynamic-update-slice_fusion.2.refs_1_), channel_id=1, source_target_pairs={{0,192},{64,0},{128,64},{192,128},{1,193},{65,1},{129,65},{193,129... | collective-permute-start | bytes 344072 | tf_op jit(solution)/shard_map/ppermute | solution.py:445
  127.4 6.3 %collective-permute-start.5 = (bf16[8,56,128]{2,1,0:T(8,128)(2,1)S(1)}, bf16[8,56,128]{2,1,0:T(8,128)(2,1)S(1)}, u32[]{:S(2)}, u32[]{:S(2)}) collective-permute-start(bf16[8,56,128]{2,1,0:T(8,128)(2,1)S(1)} %constant_dynamic-update-slice_fusion.2.refs_1_), channel_id=1, source_target_pairs={{0,128},{64,192},{128,0},{192,64},{1,129},{65,193},{129,1},{193,65... | collective-permute-start | bytes 344072 | tf_op jit(solution)/shard_map/ppermute | solution.py:445
  129.2 6.0 %collective-permute-start.4 = (bf16[8,56,128]{2,1,0:T(8,128)(2,1)S(1)}, bf16[8,56,128]{2,1,0:T(8,128)(2,1)S(1)}, u32[]{:S(2)}, u32[]{:S(2)}) collective-permute-start(bf16[8,56,128]{2,1,0:T(8,128)(2,1)S(1)} %constant_dynamic-update-slice_fusion.2.refs_1_), channel_id=1, source_target_pairs={{0,64},{64,128},{128,192},{192,0},{1,65},{65,129},{129,193},{193,1... | collective-permute-start | bytes 344072 | tf_op jit(solution)/shard_map/ppermute | solution.py:445

commit v4 on v3

--- a/solution.py
+++ b/solution.py
@@ -87,26 +87,8 @@
     return (source == kept).astype(F32).astype(BF16)
 
 
-def pack_kernel(tally_hbm, plan_hbm, cells, cot, out, tally, plan, rows, sent, small_sem, in_sem, out_sem):
-    small = [
-        pltpu.make_async_copy(tally_hbm, tally, small_sem.at[0]),
-        pltpu.make_async_copy(plan_hbm, plan, small_sem.at[1]),
-    ]
-    for copy in small:
-        copy.start()
-    reads = []
-    for j in range(8):
-        at = pl.ds(16 * j, 16)
-        pair = [
-            pltpu.make_async_copy(cells.at[:, at, :], rows.at[j, 0:SIN], in_sem.at[j, 0]),
-            pltpu.make_async_copy(cot.at[:, at, :], rows.at[j, SIN : SIN + SOUT], in_sem.at[j, 1]),
-        ]
-        for copy in pair:
-            copy.start()
-        reads.append(pair)
+def pack_kernel(tally, plan, cells, cot, out, sent, out_sem):
     order = piece_order(False)
-    for copy in small:
-        copy.wait()
     block = iota((META, 128), 1) >> 2
     target = jnp.zeros((META, 128), jnp.int32)
     for s in range(SIN):
@@ -117,9 +99,9 @@
         sent[j, 2 * SEND : TALL, :] = meta
     writes = []
     for j in range(8):
-        for copy in reads[j]:
-            copy.wait()
-        moved = mm(order, rows[j].reshape(GROUP, C)).astype(BF16)
+        at = slice(16 * j, 16 * j + 16)
+        rows = [cells[:, at, :].reshape(16 * SIN, C), cot[:, at, :].reshape(16 * SOUT, C)]
+        moved = mm(order, jnp.concatenate(rows, axis=0)).astype(BF16)
         for a in range(4):
             part = moved[a * SEND : (a + 1) * SEND]
             sent[4 * j + a, 0:SEND, :] = part[:, 0:128]
@@ -294,14 +276,11 @@
 
 
 def backward_kernel(
-    mix, entrance, exit_t, spread, gain_col, soft_col,
-    pick, xt_in, normed_in, proj_in, prob_in, scaled_in, slice_in,
+    mix, spread, soft_col, normed_in, proj_in, prob_in, scaled_in, slice_in,
     uns_in, cot_in, rows_in, heads_in,
-    send, grads, weave, stack, gprob, affs, gproj,
+    grads, gproj, deslice_out, weave, stack, gprob, affs,
 ):
     live = rows_in[0:1, :]
-    mean = rows_in[1:2, :]
-    inv = rows_in[2:3, :]
     weave[...] = jnp.zeros_like(weave)
     lane = iota((WIDTH, 128), 1)
     lane16 = iota((16, 128), 1)
@@ -334,13 +313,7 @@
     deslice = rows[0:C].astype(BF16)
     gproj[0:C, :] = rows[C : 2 * C].astype(BF16)
     gprob[...] = mm(weave[...], stack[...], TN)
-    branch = mm(exit_t[...], deslice)
-    xt = xt_in[...].astype(F32)
-    result = (live * (xt + branch)).astype(BF16)
-    eye = (iota((ROWS, ROWS), 0) == iota((ROWS, ROWS), 1)).astype(F32).astype(BF16)
-    result_rows = mm(eye, result, NT).astype(BF16)
-    for q in range(GY):
-        send[q, SIN * PIECE : SEND, :] = result_rows[q * 16 : (q + 1) * 16]
+    deslice_out[...] = deslice
     out_grad = mm(deslice, cot_in[...], NT)
     for b in range(2):
         grads[(4 + b) * C : (5 + b) * C, :] = out_grad[:, b * 128 : (b + 1) * 128].astype(
@@ -374,6 +347,19 @@
     grads[6 * C : 6 * C + WIDTH, :] = tail.astype(grads.dtype)
     grads[6 * C + WIDTH :, :] = jnp.zeros((GY * GRAD_ROWS - 6 * C - WIDTH, 128), grads.dtype)
 
+
+def home_kernel(
+    entrance, exit_t, gain_col, pick, xt_in, cot_in, rows_in, gproj, deslice, send
+):
+    live = rows_in[0:1, :]
+    mean = rows_in[1:2, :]
+    inv = rows_in[2:3, :]
+    xt = xt_in[...].astype(F32)
+    result = (live * (xt + mm(exit_t[...], deslice[...]))).astype(BF16)
+    eye = (iota((ROWS, ROWS), 0) == iota((ROWS, ROWS), 1)).astype(F32).astype(BF16)
+    result_rows = mm(eye, result, NT).astype(BF16)
+    for q in range(GY):
+        send[q, SIN * PIECE : SEND, :] = result_rows[q * 16 : (q + 1) * 16]
     g_unit = mm(entrance[...], gproj[...]) * gain_col[:, 0:1]
     unit = (xt - mean) * inv
     m1 = jnp.sum(g_unit, axis=0, keepdims=True) * (1.0 / C)
@@ -385,15 +371,15 @@
 
 
 def gather_kernel(
-    scale, at, r0, r1, r2, r3, grad_in, grad_out, grad_slice, flat, tail, sem
+    scale, at, r0, r1, grad_in, grad_out, grad_slice, flat, tail, sem
 ):
     y, core, x = at[0], at[1], at[2]
-    for dy, recv in enumerate((r0, r1, r2, r3)):
-        for dx in range(4):
-            for dc in range(2):
+    for dc, recv in enumerate((r0, r1)):
+        for dy in range(4):
+            for dx in range(4):
                 index = (((y - dy) & 3) * 2 + (core ^ dc)) * 4 + ((x - dx) & 3)
                 start = pl.multiple_of(index * GRAD_ROWS, 8)
-                flat[pl.ds(start, GRAD_ROWS), :] = recv[dx * 2 + dc].astype(F32) * scale
+                flat[pl.ds(start, GRAD_ROWS), :] = recv[dy * 4 + dx].astype(F32) * scale
     tail[...] = flat[6 * C : 6 * C + WIDTH, 0:SLICES]
     copies = []
     for b in range(6):
@@ -448,16 +434,11 @@
         pack_kernel,
         sds((GY, TALL, 128), BF16),
         tally, plan, cells.reshape(SIN, BLK, C), cot.reshape(SOUT, BLK, C),
-        hbm=True,
+        scalars=2,
         hbm_out=True,
         vmem=62,
         scratch=[
-            pltpu.SMEM((1,), jnp.int32),
-            pltpu.SMEM((1, SIN), jnp.int32),
-            pltpu.VMEM((8, SIN + SOUT, 16, C), BF16),
             pltpu.VMEM((GY, TALL, 128), BF16),
-            pltpu.SemaphoreType.DMA((2,)),
-            pltpu.SemaphoreType.DMA((8, 2)),
             pltpu.SemaphoreType.DMA((8,)),
         ],
     )
@@ -495,33 +476,41 @@
         spot, recv, entrance_t, exit_w, spread, soft_spread, gain_col, base_col,
         scalars=1,
     )
-    token, saved = state[0], state[1:]
+    token, pick, xt, normed, proj, prob, scaled, slices, uns, cot_t, rows, heads = state
     token = swap(token, ("y", "core"))
     token = swap(spread_sum(token, GY, BF16), ("z", "x"))
     mix = call(
         token_kernel, sds((GX, MIX_ROWS, 128), BF16), token, request, lookup, content
     )
     mix = swap(mix, ("y", "core"))
-    send, grads = call(
+    grads, gproj, deslice = call(
         backward_kernel,
-        [sds((GY, SEND, C), BF16), sds((GY * GRAD_ROWS, 128), BF16)],
-        mix, entrance, exit_t, spread, gain_col, soft_col, *saved,
+        [
+            sds((GY * GRAD_ROWS, 128), BF16),
+            sds((2 * C, ROWS), BF16),
+            sds((C, ROWS), BF16),
+        ],
+        mix, spread, soft_col, normed, proj, prob, scaled, slices, uns, cot_t, rows, heads,
         scratch=[
             pltpu.VMEM((2 * C + 16, 512), BF16),
             pltpu.VMEM((2 * C + 16, ROWS), BF16),
             pltpu.VMEM((512, ROWS), F32),
             pltpu.VMEM((512, ROWS), BF16),
-            pltpu.VMEM((2 * C, ROWS), BF16),
-        ],
+        ],
+    )
+    send = call(
+        home_kernel,
+        sds((GY, SEND, C), BF16),
+        entrance, exit_t, gain_col, pick, xt, cot_t, rows, gproj, deslice,
     )
     grads = swap(grads.reshape(GY, GRAD_ROWS, 128), ("y", "core", "x"))
     grads = swap(spread_sum(grads, 8, BF16), ("z",))
     grads = spread_sum(grads, 1, BF16)
     send, grads = lax.optimization_barrier((send, grads))
     home = swap(send, ("z", "x"))
-    grads = jnp.concatenate([grads, shifted(grads, "core", 2, 1)], axis=0)
-    grads = jnp.concatenate([grads] + [shifted(grads, "x", 4, d) for d in (1, 2, 3)], axis=0)
-    gathered = [grads] + [shifted(grads, "y", 4, d) for d in (1, 2, 3)]
+    for axis in ("x", "y"):
+        grads = jnp.concatenate([grads] + [shifted(grads, axis, 4, d) for d in (1, 2, 3)], axis=0)
+    gathered = [grads, shifted(grads, "core", 2, 1)]
     at = jnp.stack([lax.axis_index(a) for a in ("y", "core", "x")]).astype(jnp.int32)
     result, cell_grad = call(
         unpack_kernel,

time: 139 us -> 138 us (level)
  blocking collectives: 62.5 us -> 50.1 us
  waiting for transfers between devices: 35.5 us -> 41.5 us
  starting transfers between devices: 24.5 us -> 29.2 us
    all_to_all x5 -> x4, blocking collectives: 62.5 us -> 50.1 us  [swap(): return lax.all_to_all(x, axes, 0, 0, tiled=True)]
    all_to_all x2 -> x3, waiting for transfers between devices: 23.2 us -> 32.8 us  [swap(): return lax.all_to_all(x, axes, 0, 0, tiled=True)]
    ppermute x7, waiting for transfers between devices: 12.3 us -> 8.74 us  [shifted(): return lax.ppermute(x, axis, [(i, (i + d) % n) for i in range(n)])]
    all_to_all x2 -> x3, starting transfers between devices: 17.2 us -> 20.7 us  [swap(): return lax.all_to_all(x, axes, 0, 0, tiled=True)]
    pallas_call x10 -> x11, Pallas kernels: 13.7 us -> 13.5 us  [call(): pl.pallas_call(body, out_shape=listed, in_specs=[sm] * scalars + [far if...]
  transfers between devices with their start and end apart: 9 -> 10, of which waited for: 8 -> 7; matrix products, arithmetic and copies ran while one was open for 0% -> 0% of each run, Pallas kernels for 1% -> 3%
where the time goes in v4:
time: 138 us; the launch traced here: 137 us
  blocking collectives  50.1 us (36%)
  waiting for transfers between devices  41.5 us (30%)
  starting transfers between devices  29.2 us (21%)
  Pallas kernels  13.5 us (10%)
  between operations  1.53 us (1%)
  local copies, waits for them, and re-layouts  1.42 us (1%)
    all_to_all x4, blocking collectives, swap(): return lax.all_to_all(x, axes, 0, 0, tiled=True)  50.1 us
    all_to_all x3, waiting for transfers between devices, swap(): return lax.all_to_all(x, axes, 0, 0, tiled=True)  32.8 us
    all_to_all x3, starting transfers between devices, swap(): return lax.all_to_all(x, axes, 0, 0, tiled=True)  20.7 us
    pallas_call x11, Pallas kernels, call(): pl.pallas_call(body, out_shape=listed, in_specs=[sm] * scalars + [far if...  13.5 us
    ppermute x7, waiting for transfers between devices, shifted(): return lax.ppermute(x, axis, [(i, (i + d) % n) for i in range(n)])  8.74 us
    ppermute x7, starting transfers between devices, shifted(): return lax.ppermute(x, axis, [(i, (i + d) % n) for i in range(n)])  8.51 us
  transfers between devices with their start and end apart: 10, of which 7 were waited for; matrix products, arithmetic and copies ran while one was open for 0% of the time, Pallas kernels for 3%

profile of v4, /device:TPU:2, one launch (start us, length us, event | category | flops | bytes accessed | tf_op | source)
XLA Modules:
  0.0 137.4 jit_solution(16362109587097322331)
XLA Ops:
  1.3 2.3 %shard_map.165 = bf16[32,104,128]{2,1,0:T(8,128)(2,1)} custom-call(s32[1]{0:T(128)S(6)} %copy.27.tally, s32[1,8]{1,0:T(1,128)} %plan.1, bf16[8,128,256]{2,1,0:T(8,128)(2,1)} %bitcast.16, bf16[4,128,256]{2,1,0:T(8,128)(2,1)} %bitcast.17), custom_call_target="tpu_custom_call" | custom-call | bytes 1638436 | tf_op jit(solution)/shard_map/pallas_call | solution.py:56
  3.6 0.0 copy-start
  3.6 0.0 copy-start.1
  3.6 0.0 copy-start.10
  3.6 11.8 %all-to-all-start = ((bf16[32,104,128]{2,1,0:T(8,128)(2,1)}), bf16[32,104,128]{2,1,0:T(8,128)(2,1)S(1)}, u32[]{:S(2)}, u32[]{:S(2)}) async-start(bf16[32,104,128]{2,1,0:T(8,128)(2,1)} %shard_map.165), calls=%async_computation | async-start | bytes 1703936 | tf_op jit(solution)/shard_map/all_to_all | solution.py:428
  15.4 0.0 copy-start.7
  15.4 0.0 copy-start.8
  15.4 0.0 copy-start.9
  15.4 0.0 copy-done
  15.5 0.0 copy-done.1
  15.5 0.0 copy-done.10
  15.5 0.6 copy-done.7
  16.1 0.0 copy-done.8
  16.1 0.0 copy-done.9
  16.1 0.5 shard_map.164
  16.6 0.0 copy-start.2
  16.6 0.6 copy-done.2
  17.2 22.0 %all-to-all-done.recv = bf16[32,104,128]{2,1,0:T(8,128)(2,1)S(1)} async-done(((bf16[32,104,128]{2,1,0:T(8,128)(2,1)}), bf16[32,104,128]{2,1,0:T(8,128)(2,1)S(1)}, u32[]{:S(2)}, u32[]{:S(2)}) %all-to-all-start) | async-done | bytes 852000 | tf_op jit(solution)/shard_map/all_to_all | solution.py:428
  39.3 2.6 %shard_map.166 = (bf16[8,40,128]{2,1,0:T(8,128)(2,1)S(1)}, bf16[1024,512]{1,0:T(8,128)(2,1)S(1)}, bf16[256,512]{1,0:T(8,128)(2,1)S(1)}, bf16[256,512]{1,0:T(8,12...) custom-call(s32[1]{0:T(128)} %bitcast.3.spot, ...), custom_call_target="tpu_custom_call" | custom-call | bytes 7024644 | tf_op jit(solution)/shard_map/pallas_call | solution.py:56
  41.9 10.0 %all_to_all.35.recv = bf16[8,40,128]{2,1,0:T(8,128)(2,1)S(1)} all-to-all(bf16[8,40,128]{2,1,0:T(8,128)(2,1)S(1)} %get-tuple-element.44), channel_id=1, replica_groups=mesh['y'=4,'core'=2,'z'=8,'x'=4] {'y','core'}, dimensions={0} | all-to-all | bytes 163840 | tf_op jit(solution)/shard_map/all_to_all | solution.py:428
  51.9 0.0 copy-start.4
  51.9 0.0 copy-start.5
  51.9 0.0 copy-start.6
  51.9 18.0 %all_to_all.36.recv = bf16[32,40,128]{2,1,0:T(8,128)(2,1)S(1)} all-to-all(bf16[32,40,128]{2,1,0:T(8,128)(2,1)S(1)} %shard_map.167), channel_id=1, replica_groups=mesh['y'=4,'core'=2,'z'=8,'x'=4] {'z','x'}, dimensions={0} | all-to-all | bytes 655360 | tf_op jit(solution)/shard_map/all_to_all | solution.py:428
  69.9 0.0 copy-done.4
  69.9 0.0 copy-done.5
  69.9 0.0 copy-done.6
  69.9 1.2 shard_map.168
  71.1 8.2 %all_to_all.37.mix = bf16[8,48,128]{2,1,0:T(8,128)(2,1)S(1)} all-to-all(bf16[8,48,128]{2,1,0:T(8,128)(2,1)S(1)} %shard_map.168), channel_id=1, replica_groups=mesh['y'=4,'core'=2,'z'=8,'x'=4] {'y','core'}, dimensions={0} | all-to-all | bytes 196608 | tf_op jit(solution)/shard_map/all_to_all | solution.py:428
  79.3 1.6 %shard_map.169 = (bf16[1792,128]{1,0:T(8,128)(2,1)S(1)}, bf16[512,512]{1,0:T(8,128)(2,1)S(1)}, bf16[256,512]{1,0:T(8,128)(2,1)S(1)}) custom-call(bf16[8,48,128]{2,1,0:T(8,128)(2,1)S(1)} %all_to_all.37.mix, bf16[256,512]{1,0:T(8,128)(2,1)S(1)} %get-tuple-element.37.spread, f32[32,128]{1,0:T(8,128)S(1)} %get-tuple-element.45.soft_col, ...), custom_call_target="tpu_custom_call" | custom-call | bytes 5603328 | tf_op jit(solution)/shard_map/pallas_call | solution.py:56
  80.9 14.0 %all_to_all.38.recv = bf16[32,56,128]{2,1,0:T(8,128)(2,1)S(1)} all-to-all(bf16[32,56,128]{2,1,0:T(8,128)(2,1)S(1)} %bitcast.12), channel_id=1, replica_groups=mesh['y'=4,'core'=2,'z'=8,'x'=4] {'y','core','x'}, dimensions={0} | all-to-all | bytes 917504 | tf_op jit(solution)/shard_map/all_to_all | solution.py:428
  94.8 0.7 shard_map.171
  95.6 0.0 copy-start.3
  95.6 3.5 %all-to-all-start.5 = ((bf16[8,56,128]{2,1,0:T(8,128)(2,1)}), bf16[8,56,128]{2,1,0:T(8,128)(2,1)S(1)}, u32[]{:S(2)}, u32[]{:S(2)}) async-start(bf16[8,56,128]{2,1,0:T(8,128)(2,1)} %shard_map.171), calls=%async_computation.5 | async-start | bytes 229376 | tf_op jit(solution)/shard_map/all_to_all | solution.py:428
  99.1 0.0 copy-done.3
  99.1 1.9 %shard_map.170 = bf16[32,48,256]{2,1,0:T(8,128)(2,1)} custom-call(bf16[256,512]{1,0:T(8,128)(2,1)S(1)} %copy-done, bf16[256,256]{1,0:T(8,128)(2,1)S(1)} %copy-done.3, f32[256,128]{1,0:T(8,128)S(1)} %get-tuple-element.35.gain_col, bf16[1024,512]{1,0:T(8,128)(2,1)S(1)} %get-tuple-element.40.pick, bf16[256,512]{1,0:T(8,128)(2,1)S(1)} %get-tuple-element.41.xt_in, ...), custom_call_target="tpu_custom_call" | custom-call | bytes 3686400 | tf_op jit(solution)/shard_map/pallas_call | solution.py:56
  101.0 8.0 %all-to-all-done.5.recv = bf16[8,56,128]{2,1,0:T(8,128)(2,1)S(1)} async-done(((bf16[8,56,128]{2,1,0:T(8,128)(2,1)}), bf16[8,56,128]{2,1,0:T(8,128)(2,1)S(1)}, u32[]{:S(2)}, u32[]{:S(2)}) %all-to-all-start.5) | async-done | bytes 114720 | tf_op jit(solution)/shard_map/all_to_all | solution.py:428
  109.0 5.4 %all-to-all-start.6 = ((bf16[32,48,256]{2,1,0:T(8,128)(2,1)}), bf16[32,48,256]{2,1,0:T(8,128)(2,1)S(1)}, u32[]{:S(2)}, u32[]{:S(2)}) async-start(bf16[32,48,256]{2,1,0:T(8,128)(2,1)} %shard_map.170), calls=%async_computation.6 | async-start | bytes 1572864 | tf_op jit(solution)/shard_map/all_to_all | solution.py:428
  114.5 0.4 collective-permute-start.2
  114.9 2.6 %collective-permute-start.1 = (bf16[1,56,128]{2,1,0:T(8,128)(2,1)S(1)}, bf16[1,56,128]{2,1,0:T(8,128)(2,1)S(1)}, u32[]{:S(2)}, u32[]{:S(2)}) collective-permute-start(bf16[1,56,128]{2,1,0:T(8,128)(2,1)S(1)} %shard_map.172), channel_id=1, source_target_pairs={{0,2},{1,3},{2,0},{3,1},{4,6},{5,7},{6,4},{7,5},{8,10},{9,11},{10,... | collective-permute-start | bytes 43016 | tf_op jit(solution)/shard_map/ppermute | solution.py:431
  117.5 1.8 %collective-permute-start = (bf16[1,56,128]{2,1,0:T(8,128)(2,1)S(1)}, bf16[1,56,128]{2,1,0:T(8,128)(2,1)S(1)}, u32[]{:S(2)}, u32[]{:S(2)}) collective-permute-start(bf16[1,56,128]{2,1,0:T(8,128)(2,1)S(1)} %shard_map.172), channel_id=1, source_target_pairs={{0,1},{1,2},{2,3},{3,0},{4,5},{5,6},{6,7},{7,4},{8,9},{9,10},{10,1... | collective-permute-start | bytes 43016 | tf_op jit(solution)/shard_map/ppermute | solution.py:431
  119.3 2.0 %collective-permute-done = bf16[1,56,128]{2,1,0:T(8,128)(2,1)S(1)} collective-permute-done((bf16[1,56,128]{2,1,0:T(8,128)(2,1)S(1)}, bf16[1,56,128]{2,1,0:T(8,128)(2,1)S(1)}, u32[]{:S(2)}, u32[]{:S(2)}) %collective-permute-start) | collective-permute-done | bytes 14368 | tf_op jit(solution)/shard_map/ppermute | solution.py:431
  121.2 0.0 collective-permute-done.1
  121.3 0.0 collective-permute-done.2
  121.3 0.7 collective-permute-start.3
  122.0 2.6 %collective-permute-start.5 = (bf16[4,56,128]{2,1,0:T(8,128)(2,1)S(1)}, bf16[4,56,128]{2,1,0:T(8,128)(2,1)S(1)}, u32[]{:S(2)}, u32[]{:S(2)}) collective-permute-start(bf16[4,56,128]{2,1,0:T(8,128)(2,1)S(1)} %get-tuple-element.63), channel_id=1, source_target_pairs={{0,192},{64,0},{128,64},{192,128},{1,193},{65,1},{129,65},{193,129... | collective-permute-start | bytes 172040 | tf_op jit(solution)/shard_map/ppermute | solution.py:431
  124.6 0.3 collective-permute-start.4
  124.9 1.9 %collective-permute-done.3 = bf16[4,56,128]{2,1,0:T(8,128)(2,1)S(1)} collective-permute-done((bf16[4,56,128]{2,1,0:T(8,128)(2,1)S(1)}, bf16[4,56,128]{2,1,0:T(8,128)(2,1)S(1)}, u32[]{:S(2)}, u32[]{:S(2)}) %collective-permute-start.3) | collective-permute-done | bytes 57376 | tf_op jit(solution)/shard_map/ppermute | solution.py:431
  126.8 3.5 %collective-permute-done.4 = bf16[4,56,128]{2,1,0:T(8,128)(2,1)S(1)} collective-permute-done((bf16[4,56,128]{2,1,0:T(8,128)(2,1)S(1)}, bf16[4,56,128]{2,1,0:T(8,128)(2,1)S(1)}, u32[]{:S(2)}, u32[]{:S(2)}) %collective-permute-start.4) | collective-permute-done | bytes 57376 | tf_op jit(solution)/shard_map/ppermute | solution.py:431
  130.3 0.0 collective-permute-done.5
  130.3 0.1 collective-permute-start.6
  130.4 0.1 pad_add_fusion.refs_0_
  130.5 1.4 %collective-permute-done.6.refs_2_ = bf16[16,56,128]{2,1,0:T(8,128)(2,1)S(1)} collective-permute-done((bf16[16,56,128]{2,1,0:T(8,128)(2,1)S(1)}, bf16[16,56,128]{2,1,0:T(8,128)(2,1)S(1)}, u32[]{:S(2)}, u32[]{:S(2)}) %collective-permute-start.6) | collective-permute-done | bytes 229408 | tf_op jit(solution)/shard_map/ppermute | solution.py:431
  131.9 1.5 %shard_map.174 = (f32[256,512]{1,0:T(8,128)}, f32[256,256]{1,0:T(8,128)}, f32[32,64]{1,0:T(8,128)}) custom-call(s32[3]{0:T(128)S(1)} %pad_add_fusion.refs_0_, bf16[16,56,128]{2,1,0:T(8,128)(2,1)S(1)} %constant_dynamic-update-slice_fusion.4.refs_1_, bf16[16,56,128]{2,1,0:T(8,128)(2,1)S(1)} %collective-permute-done.6.refs_2_), custom_call_target="tpu_custom_call" | custom-call | bytes 1253388 | tf_op jit(solution)/shard_map/pallas_call | solution.py:56
  133.5 2.8 %all-to-all-done.6.home = bf16[32,48,256]{2,1,0:T(8,128)(2,1)S(1)} async-done(((bf16[32,48,256]{2,1,0:T(8,128)(2,1)}), bf16[32,48,256]{2,1,0:T(8,128)(2,1)S(1)}, u32[]{:S(2)}, u32[]{:S(2)}) %all-to-all-start.6) | async-done | bytes 786464 | tf_op jit(solution)/shard_map/all_to_all | solution.py:428
  136.2 1.1 shard_map.173
  (9 shorter events, 0.1 us)
Async XLA Ops:
  3.6 11.8 %copy-start = (bf16[256,512]{1,0:T(8,128)(2,1)S(1)}, bf16[256,512]{1,0:T(8,128)(2,1)}, u32[]{:S(2)}) copy-start(bf16[256,512]{1,0:T(8,128)(2,1)} %entrance.3) | copy-start | bytes 786436
  3.6 11.8 %copy-start.1 = (bf16[256,256]{1,0:T(8,128)(2,1)S(1)}, bf16[256,256]{1,0:T(8,128)(2,1)}, u32[]{:S(2)}) copy-start(bf16[256,256]{1,0:T(8,128)(2,1)} %exit_w.3) | copy-start | bytes 393220
  3.6 11.8 %copy-start.10 = (f32[8]{0:T(128)S(1)}, f32[8]{0:T(128)}, u32[]{:S(2)}) copy-start(f32[8]{0:T(128)} %param.21) | copy-start | bytes 100
  3.6 35.6 %all-to-all-start = ((bf16[32,104,128]{2,1,0:T(8,128)(2,1)}), bf16[32,104,128]{2,1,0:T(8,128)(2,1)S(1)}, u32[]{:S(2)}, u32[]{:S(2)}) async-start(bf16[32,104,128]{2,1,0:T(8,128)(2,1)} %shard_map.165), calls=%async_computation | async-start | bytes 1703936 | tf_op jit(solution)/shard_map/all_to_all | solution.py:428
  15.4 0.7 copy-start.7
  15.4 0.7 copy-start.8
  15.4 0.7 copy-start.9
  16.6 0.7 copy-start.2
  51.9 18.0 %copy-start.4 = (f32[32,32]{1,0:T(8,128)S(1)}, f32[32,32]{1,0:T(8,128)}, u32[]{:S(2)}) copy-start(f32[32,32]{1,0:T(8,128)} %request.1) | copy-start | bytes 12292
  51.9 18.0 %copy-start.5 = (f32[32,32]{1,0:T(8,128)S(1)}, f32[32,32]{1,0:T(8,128)}, u32[]{:S(2)}) copy-start(f32[32,32]{1,0:T(8,128)} %lookup.1) | copy-start | bytes 12292
  51.9 18.0 %copy-start.6 = (f32[32,32]{1,0:T(8,128)S(1)}, f32[32,32]{1,0:T(8,128)}, u32[]{:S(2)}) copy-start(f32[32,32]{1,0:T(8,128)} %content.1) | copy-start | bytes 12292
  95.6 3.5 %copy-start.3 = (bf16[256,256]{1,0:T(8,128)(2,1)S(1)}, bf16[256,256]{1,0:T(8,128)(2,1)}, u32[]{:S(2)}) copy-start(bf16[256,256]{1,0:T(8,128)(2,1)} %copy-done.2) | copy-start | bytes 393220
  95.6 13.4 %all-to-all-start.5 = ((bf16[8,56,128]{2,1,0:T(8,128)(2,1)}), bf16[8,56,128]{2,1,0:T(8,128)(2,1)S(1)}, u32[]{:S(2)}, u32[]{:S(2)}) async-start(bf16[8,56,128]{2,1,0:T(8,128)(2,1)} %shard_map.171), calls=%async_computation.5 | async-start | bytes 229376 | tf_op jit(solution)/shard_map/all_to_all | solution.py:428
  109.0 27.2 %all-to-all-start.6 = ((bf16[32,48,256]{2,1,0:T(8,128)(2,1)}), bf16[32,48,256]{2,1,0:T(8,128)(2,1)S(1)}, u32[]{:S(2)}, u32[]{:S(2)}) async-start(bf16[32,48,256]{2,1,0:T(8,128)(2,1)} %shard_map.170), calls=%async_computation.6 | async-start | bytes 1572864 | tf_op jit(solution)/shard_map/all_to_all | solution.py:428
  114.5 6.8 %collective-permute-start.2 = (bf16[1,56,128]{2,1,0:T(8,128)(2,1)S(1)}, bf16[1,56,128]{2,1,0:T(8,128)(2,1)S(1)}, u32[]{:S(2)}, u32[]{:S(2)}) collective-permute-start(bf16[1,56,128]{2,1,0:T(8,128)(2,1)S(1)} %shard_map.172), channel_id=1, source_target_pairs={{0,3},{1,0},{2,1},{3,2},{4,7},{5,4},{6,5},{7,6},{8,11},{9,8},{10,9... | collective-permute-start | bytes 43016 | tf_op jit(solution)/shard_map/ppermute | solution.py:431
  114.9 6.4 %collective-permute-start.1 = (bf16[1,56,128]{2,1,0:T(8,128)(2,1)S(1)}, bf16[1,56,128]{2,1,0:T(8,128)(2,1)S(1)}, u32[]{:S(2)}, u32[]{:S(2)}) collective-permute-start(bf16[1,56,128]{2,1,0:T(8,128)(2,1)S(1)} %shard_map.172), channel_id=1, source_target_pairs={{0,2},{1,3},{2,0},{3,1},{4,6},{5,7},{6,4},{7,5},{8,10},{9,11},{10,... | collective-permute-start | bytes 43016 | tf_op jit(solution)/shard_map/ppermute | solution.py:431
  117.5 3.8 %collective-permute-start = (bf16[1,56,128]{2,1,0:T(8,128)(2,1)S(1)}, bf16[1,56,128]{2,1,0:T(8,128)(2,1)S(1)}, u32[]{:S(2)}, u32[]{:S(2)}) collective-permute-start(bf16[1,56,128]{2,1,0:T(8,128)(2,1)S(1)} %shard_map.172), channel_id=1, source_target_pairs={{0,1},{1,2},{2,3},{3,0},{4,5},{5,6},{6,7},{7,4},{8,9},{9,10},{10,1... | collective-permute-start | bytes 43016 | tf_op jit(solution)/shard_map/ppermute | solution.py:431
  121.3 5.5 %collective-permute-start.3 = (bf16[4,56,128]{2,1,0:T(8,128)(2,1)S(1)}, bf16[4,56,128]{2,1,0:T(8,128)(2,1)S(1)}, u32[]{:S(2)}, u32[]{:S(2)}) collective-permute-start(bf16[4,56,128]{2,1,0:T(8,128)(2,1)S(1)} %get-tuple-element.63), channel_id=1, source_target_pairs={{0,64},{64,128},{128,192},{192,0},{1,65},{65,129},{129,193},{193,1... | collective-permute-start | bytes 172040 | tf_op jit(solution)/shard_map/ppermute | solution.py:431
  122.0 8.3 %collective-permute-start.5 = (bf16[4,56,128]{2,1,0:T(8,128)(2,1)S(1)}, bf16[4,56,128]{2,1,0:T(8,128)(2,1)S(1)}, u32[]{:S(2)}, u32[]{:S(2)}) collective-permute-start(bf16[4,56,128]{2,1,0:T(8,128)(2,1)S(1)} %get-tuple-element.63), channel_id=1, source_target_pairs={{0,192},{64,0},{128,64},{192,128},{1,193},{65,1},{129,65},{193,129... | collective-permute-start | bytes 172040 | tf_op jit(solution)/shard_map/ppermute | solution.py:431
  124.6 5.7 %collective-permute-start.4 = (bf16[4,56,128]{2,1,0:T(8,128)(2,1)S(1)}, bf16[4,56,128]{2,1,0:T(8,128)(2,1)S(1)}, u32[]{:S(2)}, u32[]{:S(2)}) collective-permute-start(bf16[4,56,128]{2,1,0:T(8,128)(2,1)S(1)} %get-tuple-element.63), channel_id=1, source_target_pairs={{0,128},{64,192},{128,0},{192,64},{1,129},{65,193},{129,1},{193,65... | collective-permute-start | bytes 172040 | tf_op jit(solution)/shard_map/ppermute | solution.py:431
  130.3 1.6 %collective-permute-start.6 = (bf16[16,56,128]{2,1,0:T(8,128)(2,1)S(1)}, bf16[16,56,128]{2,1,0:T(8,128)(2,1)S(1)}, u32[]{:S(2)}, u32[]{:S(2)}) collective-permute-start(bf16[16,56,128]{2,1,0:T(8,128)(2,1)S(1)} %constant_dynamic-update-slice_fusion.4.refs_1_), channel_id=1, source_target_pairs={{0,32},{32,0},{1,33},{33,1},{2,34},{34,2},{3,35},{35,3},{4,36},{36... | collective-permute-start | bytes 688136 | tf_op jit(solution)/shard_map/ppermute | solution.py:431

commit v5 on v4

--- a/solution.py
+++ b/solution.py
@@ -504,7 +504,9 @@
         entrance, exit_t, gain_col, pick, xt, cot_t, rows, gproj, deslice,
     )
     grads = swap(grads.reshape(GY, GRAD_ROWS, 128), ("y", "core", "x"))
-    grads = swap(spread_sum(grads, 8, BF16), ("z",))
+    grads = spread_sum(grads, 8, BF16)
+    send, grads = lax.optimization_barrier((send, grads))
+    grads = swap(grads, ("z",))
     grads = spread_sum(grads, 1, BF16)
     send, grads = lax.optimization_barrier((send, grads))
     home = swap(send, ("z", "x"))

time: 138 us -> 138 us (level)
  starting transfers between devices: 29.2 us -> 31.4 us
  blocking collectives: 50.1 us -> 48.5 us
    all_to_all x3, starting transfers between devices: 20.7 us -> 22.9 us  [swap(): return lax.all_to_all(x, axes, 0, 0, tiled=True)]
    all_to_all x4, blocking collectives: 50.1 us -> 48.5 us  [swap(): return lax.all_to_all(x, axes, 0, 0, tiled=True)]
where the time goes in v5:
time: 138 us; the launch traced here: 137 us
  blocking collectives  48.5 us (35%)
  waiting for transfers between devices  40.2 us (29%)
  starting transfers between devices  31.4 us (23%)
  Pallas kernels  13.7 us (10%)
  between operations  1.52 us (1%)
  local copies, waits for them, and re-layouts  1.42 us (1%)
    all_to_all x4, blocking collectives, swap(): return lax.all_to_all(x, axes, 0, 0, tiled=True)  48.5 us
    all_to_all x3, waiting for transfers between devices, swap(): return lax.all_to_all(x, axes, 0, 0, tiled=True)  31.5 us
    all_to_all x3, starting transfers between devices, swap(): return lax.all_to_all(x, axes, 0, 0, tiled=True)  22.9 us
    pallas_call x11, Pallas kernels, call(): pl.pallas_call(body, out_shape=listed, in_specs=[sm] * scalars + [far if...  13.7 us
    ppermute x7, waiting for transfers between devices, shifted(): return lax.ppermute(x, axis, [(i, (i + d) % n) for i in range(n)])  8.76 us
    ppermute x7, starting transfers between devices, shifted(): return lax.ppermute(x, axis, [(i, (i + d) % n) for i in range(n)])  8.5 us
  transfers between devices with their start and end apart: 10, of which 7 were waited for; matrix products, arithmetic and copies ran while one was open for 0% of the time, Pallas kernels for 3%

profile of v5, /device:TPU:2, one launch (start us, length us, event | category | flops | bytes accessed | tf_op | source)
XLA Modules:
  0.0 136.8 jit_solution(7769029406725080258)
XLA Ops:
  1.3 2.3 %shard_map.165 = bf16[32,104,128]{2,1,0:T(8,128)(2,1)} custom-call(s32[1]{0:T(128)S(6)} %copy.27.tally, s32[1,8]{1,0:T(1,128)} %plan.1, bf16[8,128,256]{2,1,0:T(8,128)(2,1)} %bitcast.15, bf16[4,128,256]{2,1,0:T(8,128)(2,1)} %bitcast.16), custom_call_target="tpu_custom_call" | custom-call | bytes 1638436 | tf_op jit(solution)/shard_map/pallas_call | solution.py:56
  3.6 0.0 copy-start
  3.6 0.0 copy-start.1
  3.6 0.0 copy-start.10
  3.6 11.8 %all-to-all-start = ((bf16[32,104,128]{2,1,0:T(8,128)(2,1)}), bf16[32,104,128]{2,1,0:T(8,128)(2,1)S(1)}, u32[]{:S(2)}, u32[]{:S(2)}) async-start(bf16[32,104,128]{2,1,0:T(8,128)(2,1)} %shard_map.165), calls=%async_computation | async-start | bytes 1703936 | tf_op jit(solution)/shard_map/all_to_all | solution.py:428
  15.4 0.0 copy-start.7
  15.4 0.0 copy-start.8
  15.4 0.0 copy-start.9
  15.4 0.0 copy-done
  15.5 0.0 copy-done.1
  15.5 0.0 copy-done.10
  15.5 0.6 copy-done.7
  16.1 0.0 copy-done.8
  16.1 0.0 copy-done.9
  16.1 0.5 shard_map.164
  16.6 0.0 copy-start.2
  16.6 0.6 copy-done.2
  17.2 22.0 %all-to-all-done.recv = bf16[32,104,128]{2,1,0:T(8,128)(2,1)S(1)} async-done(((bf16[32,104,128]{2,1,0:T(8,128)(2,1)}), bf16[32,104,128]{2,1,0:T(8,128)(2,1)S(1)}, u32[]{:S(2)}, u32[]{:S(2)}) %all-to-all-start) | async-done | bytes 852000 | tf_op jit(solution)/shard_map/all_to_all | solution.py:428
  39.3 2.6 %shard_map.166 = (bf16[8,40,128]{2,1,0:T(8,128)(2,1)S(1)}, bf16[1024,512]{1,0:T(8,128)(2,1)S(1)}, bf16[256,512]{1,0:T(8,128)(2,1)S(1)}, bf16[256,512]{1,0:T(8,12...) custom-call(s32[1]{0:T(128)} %bitcast.3.spot, ...), custom_call_target="tpu_custom_call" | custom-call | bytes 7024644 | tf_op jit(solution)/shard_map/pallas_call | solution.py:56
  41.9 10.0 %all_to_all.35.recv = bf16[8,40,128]{2,1,0:T(8,128)(2,1)S(1)} all-to-all(bf16[8,40,128]{2,1,0:T(8,128)(2,1)S(1)} %get-tuple-element.46), channel_id=1, replica_groups=mesh['y'=4,'core'=2,'z'=8,'x'=4] {'y','core'}, dimensions={0} | all-to-all | bytes 163840 | tf_op jit(solution)/shard_map/all_to_all | solution.py:428
  51.9 0.0 copy-start.4
  51.9 0.0 copy-start.5
  51.9 0.0 copy-start.6
  51.9 18.0 %all_to_all.36.recv = bf16[32,40,128]{2,1,0:T(8,128)(2,1)S(1)} all-to-all(bf16[32,40,128]{2,1,0:T(8,128)(2,1)S(1)} %shard_map.167), channel_id=1, replica_groups=mesh['y'=4,'core'=2,'z'=8,'x'=4] {'z','x'}, dimensions={0} | all-to-all | bytes 655360 | tf_op jit(solution)/shard_map/all_to_all | solution.py:428
  69.9 0.0 copy-done.4
  69.9 0.0 copy-done.5
  69.9 0.0 copy-done.6
  69.9 1.2 shard_map.168
  71.1 8.2 %all_to_all.37.mix = bf16[8,48,128]{2,1,0:T(8,128)(2,1)S(1)} all-to-all(bf16[8,48,128]{2,1,0:T(8,128)(2,1)S(1)} %shard_map.168), channel_id=1, replica_groups=mesh['y'=4,'core'=2,'z'=8,'x'=4] {'y','core'}, dimensions={0} | all-to-all | bytes 196608 | tf_op jit(solution)/shard_map/all_to_all | solution.py:428
  79.3 2.3 %shard_map.169 = (bf16[1792,128]{1,0:T(8,128)(2,1)}, bf16[512,512]{1,0:T(8,128)(2,1)S(1)}, bf16[256,512]{1,0:T(8,128)(2,1)S(1)}) custom-call(bf16[8,48,128]{2,1,0:T(8,128)(2,1)S(1)} %all_to_all.37.mix, bf16[256,512]{1,0:T(8,128)(2,1)S(1)} %get-tuple-element.39.spread, f32[32,128]{1,0:T(8,128)S(1)} %get-tuple-element.47.soft_col, ...), custom_call_target="tpu_custom_call" | custom-call | bytes 5603328 | tf_op jit(solution)/shard_map/pallas_call | solution.py:56
  81.6 0.0 copy-start.3
  81.6 5.7 %all-to-all-start.4 = ((bf16[32,56,128]{2,1,0:T(8,128)(2,1)}), bf16[32,56,128]{2,1,0:T(8,128)(2,1)S(1)}, u32[]{:S(2)}, u32[]{:S(2)}) async-start(bf16[32,56,128]{2,1,0:T(8,128)(2,1)} %bitcast.6), calls=%async_computation.4 | async-start | bytes 917504 | tf_op jit(solution)/shard_map/all_to_all | solution.py:428
  87.3 0.0 copy-done.3
  87.3 1.9 %shard_map.170 = bf16[32,48,256]{2,1,0:T(8,128)(2,1)} custom-call(bf16[256,512]{1,0:T(8,128)(2,1)S(1)} %copy-done, bf16[256,256]{1,0:T(8,128)(2,1)S(1)} %copy-done.3, f32[256,128]{1,0:T(8,128)S(1)} %get-tuple-element.37.gain_col, bf16[1024,512]{1,0:T(8,128)(2,1)S(1)} %get-tuple-element.42.pick, bf16[256,512]{1,0:T(8,128)(2,1)S(1)} %get-tuple-element.43.xt_in, ...), custom_call_target="tpu_custom_call" | custom-call | bytes 3686400 | tf_op jit(solution)/shard_map/pallas_call | solution.py:56
  89.3 6.7 %all-to-all-done.4.recv = bf16[32,56,128]{2,1,0:T(8,128)(2,1)S(1)} async-done(((bf16[32,56,128]{2,1,0:T(8,128)(2,1)}), bf16[32,56,128]{2,1,0:T(8,128)(2,1)S(1)}, u32[]{:S(2)}, u32[]{:S(2)}) %all-to-all-start.4) | async-done | bytes 458784 | tf_op jit(solution)/shard_map/all_to_all | solution.py:428
  95.9 0.1 shard_map.171
  96.0 12.4 %all_to_all.38.recv = bf16[8,56,128]{2,1,0:T(8,128)(2,1)S(1)} all-to-all(bf16[8,56,128]{2,1,0:T(8,128)(2,1)S(1)} %shard_map.171), channel_id=1, replica_groups=mesh['y'=4,'core'=2,'z'=8,'x'=4] {'z'}, dimensions={0} | all-to-all | bytes 229376 | tf_op jit(solution)/shard_map/all_to_all | solution.py:428
  108.4 5.5 %all-to-all-start.6 = ((bf16[32,48,256]{2,1,0:T(8,128)(2,1)}), bf16[32,48,256]{2,1,0:T(8,128)(2,1)S(1)}, u32[]{:S(2)}, u32[]{:S(2)}) async-start(bf16[32,48,256]{2,1,0:T(8,128)(2,1)} %shard_map.170), calls=%async_computation.6 | async-start | bytes 1572864 | tf_op jit(solution)/shard_map/all_to_all | solution.py:428
  113.9 0.4 collective-permute-start.2
  114.3 2.6 %collective-permute-start.1 = (bf16[1,56,128]{2,1,0:T(8,128)(2,1)S(1)}, bf16[1,56,128]{2,1,0:T(8,128)(2,1)S(1)}, u32[]{:S(2)}, u32[]{:S(2)}) collective-permute-start(bf16[1,56,128]{2,1,0:T(8,128)(2,1)S(1)} %shard_map.172), channel_id=1, source_target_pairs={{0,2},{1,3},{2,0},{3,1},{4,6},{5,7},{6,4},{7,5},{8,10},{9,11},{10,... | collective-permute-start | bytes 43016 | tf_op jit(solution)/shard_map/ppermute | solution.py:431
  116.9 1.8 %collective-permute-start = (bf16[1,56,128]{2,1,0:T(8,128)(2,1)S(1)}, bf16[1,56,128]{2,1,0:T(8,128)(2,1)S(1)}, u32[]{:S(2)}, u32[]{:S(2)}) collective-permute-start(bf16[1,56,128]{2,1,0:T(8,128)(2,1)S(1)} %shard_map.172), channel_id=1, source_target_pairs={{0,1},{1,2},{2,3},{3,0},{4,5},{5,6},{6,7},{7,4},{8,9},{9,10},{10,1... | collective-permute-start | bytes 43016 | tf_op jit(solution)/shard_map/ppermute | solution.py:431
  118.7 2.0 %collective-permute-done = bf16[1,56,128]{2,1,0:T(8,128)(2,1)S(1)} collective-permute-done((bf16[1,56,128]{2,1,0:T(8,128)(2,1)S(1)}, bf16[1,56,128]{2,1,0:T(8,128)(2,1)S(1)}, u32[]{:S(2)}, u32[]{:S(2)}) %collective-permute-start) | collective-permute-done | bytes 14368 | tf_op jit(solution)/shard_map/ppermute | solution.py:431
  120.7 0.0 collective-permute-done.1
  120.7 0.0 collective-permute-done.2
  120.7 0.7 collective-permute-start.3
  121.4 2.6 %collective-permute-start.5 = (bf16[4,56,128]{2,1,0:T(8,128)(2,1)S(1)}, bf16[4,56,128]{2,1,0:T(8,128)(2,1)S(1)}, u32[]{:S(2)}, u32[]{:S(2)}) collective-permute-start(bf16[4,56,128]{2,1,0:T(8,128)(2,1)S(1)} %get-tuple-element.67), channel_id=1, source_target_pairs={{0,192},{64,0},{128,64},{192,128},{1,193},{65,1},{129,65},{193,129... | collective-permute-start | bytes 172040 | tf_op jit(solution)/shard_map/ppermute | solution.py:431
  124.0 0.3 collective-permute-start.4
  124.3 1.9 %collective-permute-done.3 = bf16[4,56,128]{2,1,0:T(8,128)(2,1)S(1)} collective-permute-done((bf16[4,56,128]{2,1,0:T(8,128)(2,1)S(1)}, bf16[4,56,128]{2,1,0:T(8,128)(2,1)S(1)}, u32[]{:S(2)}, u32[]{:S(2)}) %collective-permute-start.3) | collective-permute-done | bytes 57376 | tf_op jit(solution)/shard_map/ppermute | solution.py:431
  126.2 3.5 %collective-permute-done.4 = bf16[4,56,128]{2,1,0:T(8,128)(2,1)S(1)} collective-permute-done((bf16[4,56,128]{2,1,0:T(8,128)(2,1)S(1)}, bf16[4,56,128]{2,1,0:T(8,128)(2,1)S(1)}, u32[]{:S(2)}, u32[]{:S(2)}) %collective-permute-start.4) | collective-permute-done | bytes 57376 | tf_op jit(solution)/shard_map/ppermute | solution.py:431
  129.7 0.0 collective-permute-done.5
  129.7 0.1 collective-permute-start.6
  129.9 0.1 pad_add_fusion.refs_0_
  129.9 1.4 %collective-permute-done.6.refs_2_ = bf16[16,56,128]{2,1,0:T(8,128)(2,1)S(1)} collective-permute-done((bf16[16,56,128]{2,1,0:T(8,128)(2,1)S(1)}, bf16[16,56,128]{2,1,0:T(8,128)(2,1)S(1)}, u32[]{:S(2)}, u32[]{:S(2)}) %collective-permute-start.6) | collective-permute-done | bytes 229408 | tf_op jit(solution)/shard_map/ppermute | solution.py:431
  131.3 1.5 %shard_map.174 = (f32[256,512]{1,0:T(8,128)}, f32[256,256]{1,0:T(8,128)}, f32[32,64]{1,0:T(8,128)}) custom-call(s32[3]{0:T(128)S(1)} %pad_add_fusion.refs_0_, bf16[16,56,128]{2,1,0:T(8,128)(2,1)S(1)} %constant_dynamic-update-slice_fusion.4.refs_1_, bf16[16,56,128]{2,1,0:T(8,128)(2,1)S(1)} %collective-permute-done.6.refs_2_), custom_call_target="tpu_custom_call" | custom-call | bytes 1253388 | tf_op jit(solution)/shard_map/pallas_call | solution.py:56
  132.9 2.8 %all-to-all-done.6.home = bf16[32,48,256]{2,1,0:T(8,128)(2,1)S(1)} async-done(((bf16[32,48,256]{2,1,0:T(8,128)(2,1)}), bf16[32,48,256]{2,1,0:T(8,128)(2,1)S(1)}, u32[]{:S(2)}, u32[]{:S(2)}) %all-to-all-start.6) | async-done | bytes 786464 | tf_op jit(solution)/shard_map/all_to_all | solution.py:428
  135.7 1.1 shard_map.173
  (9 shorter events, 0.1 us)
Async XLA Ops:
  3.6 11.8 %copy-start = (bf16[256,512]{1,0:T(8,128)(2,1)S(1)}, bf16[256,512]{1,0:T(8,128)(2,1)}, u32[]{:S(2)}) copy-start(bf16[256,512]{1,0:T(8,128)(2,1)} %entrance.3) | copy-start | bytes 786436
  3.6 11.8 %copy-start.1 = (bf16[256,256]{1,0:T(8,128)(2,1)S(1)}, bf16[256,256]{1,0:T(8,128)(2,1)}, u32[]{:S(2)}) copy-start(bf16[256,256]{1,0:T(8,128)(2,1)} %exit_w.3) | copy-start | bytes 393220
  3.6 11.8 %copy-start.10 = (f32[8]{0:T(128)S(1)}, f32[8]{0:T(128)}, u32[]{:S(2)}) copy-start(f32[8]{0:T(128)} %param.21) | copy-start | bytes 100
  3.6 35.6 %all-to-all-start = ((bf16[32,104,128]{2,1,0:T(8,128)(2,1)}), bf16[32,104,128]{2,1,0:T(8,128)(2,1)S(1)}, u32[]{:S(2)}, u32[]{:S(2)}) async-start(bf16[32,104,128]{2,1,0:T(8,128)(2,1)} %shard_map.165), calls=%async_computation | async-start | bytes 1703936 | tf_op jit(solution)/shard_map/all_to_all | solution.py:428
  15.4 0.7 copy-start.7
  15.4 0.7 copy-start.8
  15.4 0.7 copy-start.9
  16.6 0.7 copy-start.2
  51.9 18.0 %copy-start.4 = (f32[32,32]{1,0:T(8,128)S(1)}, f32[32,32]{1,0:T(8,128)}, u32[]{:S(2)}) copy-start(f32[32,32]{1,0:T(8,128)} %request.1) | copy-start | bytes 12292
  51.9 18.0 %copy-start.5 = (f32[32,32]{1,0:T(8,128)S(1)}, f32[32,32]{1,0:T(8,128)}, u32[]{:S(2)}) copy-start(f32[32,32]{1,0:T(8,128)} %lookup.1) | copy-start | bytes 12292
  51.9 18.0 %copy-start.6 = (f32[32,32]{1,0:T(8,128)S(1)}, f32[32,32]{1,0:T(8,128)}, u32[]{:S(2)}) copy-start(f32[32,32]{1,0:T(8,128)} %content.1) | copy-start | bytes 12292
  81.6 5.7 %copy-start.3 = (bf16[256,256]{1,0:T(8,128)(2,1)S(1)}, bf16[256,256]{1,0:T(8,128)(2,1)}, u32[]{:S(2)}) copy-start(bf16[256,256]{1,0:T(8,128)(2,1)} %copy-done.2) | copy-start | bytes 393220
  81.6 14.3 %all-to-all-start.4 = ((bf16[32,56,128]{2,1,0:T(8,128)(2,1)}), bf16[32,56,128]{2,1,0:T(8,128)(2,1)S(1)}, u32[]{:S(2)}, u32[]{:S(2)}) async-start(bf16[32,56,128]{2,1,0:T(8,128)(2,1)} %bitcast.6), calls=%async_computation.4 | async-start | bytes 917504 | tf_op jit(solution)/shard_map/all_to_all | solution.py:428
  108.4 27.3 %all-to-all-start.6 = ((bf16[32,48,256]{2,1,0:T(8,128)(2,1)}), bf16[32,48,256]{2,1,0:T(8,128)(2,1)S(1)}, u32[]{:S(2)}, u32[]{:S(2)}) async-start(bf16[32,48,256]{2,1,0:T(8,128)(2,1)} %shard_map.170), calls=%async_computation.6 | async-start | bytes 1572864 | tf_op jit(solution)/shard_map/all_to_all | solution.py:428
  113.9 6.8 %collective-permute-start.2 = (bf16[1,56,128]{2,1,0:T(8,128)(2,1)S(1)}, bf16[1,56,128]{2,1,0:T(8,128)(2,1)S(1)}, u32[]{:S(2)}, u32[]{:S(2)}) collective-permute-start(bf16[1,56,128]{2,1,0:T(8,128)(2,1)S(1)} %shard_map.172), channel_id=1, source_target_pairs={{0,3},{1,0},{2,1},{3,2},{4,7},{5,4},{6,5},{7,6},{8,11},{9,8},{10,9... | collective-permute-start | bytes 43016 | tf_op jit(solution)/shard_map/ppermute | solution.py:431
  114.3 6.4 %collective-permute-start.1 = (bf16[1,56,128]{2,1,0:T(8,128)(2,1)S(1)}, bf16[1,56,128]{2,1,0:T(8,128)(2,1)S(1)}, u32[]{:S(2)}, u32[]{:S(2)}) collective-permute-start(bf16[1,56,128]{2,1,0:T(8,128)(2,1)S(1)} %shard_map.172), channel_id=1, source_target_pairs={{0,2},{1,3},{2,0},{3,1},{4,6},{5,7},{6,4},{7,5},{8,10},{9,11},{10,... | collective-permute-start | bytes 43016 | tf_op jit(solution)/shard_map/ppermute | solution.py:431
  116.9 3.8 %collective-permute-start = (bf16[1,56,128]{2,1,0:T(8,128)(2,1)S(1)}, bf16[1,56,128]{2,1,0:T(8,128)(2,1)S(1)}, u32[]{:S(2)}, u32[]{:S(2)}) collective-permute-start(bf16[1,56,128]{2,1,0:T(8,128)(2,1)S(1)} %shard_map.172), channel_id=1, source_target_pairs={{0,1},{1,2},{2,3},{3,0},{4,5},{5,6},{6,7},{7,4},{8,9},{9,10},{10,1... | collective-permute-start | bytes 43016 | tf_op jit(solution)/shard_map/ppermute | solution.py:431
  120.7 5.5 %collective-permute-start.3 = (bf16[4,56,128]{2,1,0:T(8,128)(2,1)S(1)}, bf16[4,56,128]{2,1,0:T(8,128)(2,1)S(1)}, u32[]{:S(2)}, u32[]{:S(2)}) collective-permute-start(bf16[4,56,128]{2,1,0:T(8,128)(2,1)S(1)} %get-tuple-element.67), channel_id=1, source_target_pairs={{0,64},{64,128},{128,192},{192,0},{1,65},{65,129},{129,193},{193,1... | collective-permute-start | bytes 172040 | tf_op jit(solution)/shard_map/ppermute | solution.py:431
  121.4 8.3 %collective-permute-start.5 = (bf16[4,56,128]{2,1,0:T(8,128)(2,1)S(1)}, bf16[4,56,128]{2,1,0:T(8,128)(2,1)S(1)}, u32[]{:S(2)}, u32[]{:S(2)}) collective-permute-start(bf16[4,56,128]{2,1,0:T(8,128)(2,1)S(1)} %get-tuple-element.67), channel_id=1, source_target_pairs={{0,192},{64,0},{128,64},{192,128},{1,193},{65,1},{129,65},{193,129... | collective-permute-start | bytes 172040 | tf_op jit(solution)/shard_map/ppermute | solution.py:431
  124.0 5.7 %collective-permute-start.4 = (bf16[4,56,128]{2,1,0:T(8,128)(2,1)S(1)}, bf16[4,56,128]{2,1,0:T(8,128)(2,1)S(1)}, u32[]{:S(2)}, u32[]{:S(2)}) collective-permute-start(bf16[4,56,128]{2,1,0:T(8,128)(2,1)S(1)} %get-tuple-element.67), channel_id=1, source_target_pairs={{0,128},{64,192},{128,0},{192,64},{1,129},{65,193},{129,1},{193,65... | collective-permute-start | bytes 172040 | tf_op jit(solution)/shard_map/ppermute | solution.py:431
  129.7 1.6 %collective-permute-start.6 = (bf16[16,56,128]{2,1,0:T(8,128)(2,1)S(1)}, bf16[16,56,128]{2,1,0:T(8,128)(2,1)S(1)}, u32[]{:S(2)}, u32[]{:S(2)}) collective-permute-start(bf16[16,56,128]{2,1,0:T(8,128)(2,1)S(1)} %constant_dynamic-update-slice_fusion.4.refs_1_), channel_id=1, source_target_pairs={{0,32},{32,0},{1,33},{33,1},{2,34},{34,2},{3,35},{35,3},{4,36},{36... | collective-permute-start | bytes 688136 | tf_op jit(solution)/shard_map/ppermute | solution.py:431

commit v6 on v5

--- a/solution.py
+++ b/solution.py
@@ -46,7 +46,7 @@
     return lax.broadcasted_iota(jnp.int32, shape, dim)
 
 
-def call(body, outs, *args, scalars=0, hbm=False, hbm_out=False, scratch=(), vmem=40):
+def call(body, outs, *args, scalars=0, hbm=False, hbm_out=(), scratch=(), vmem=40):
     vm = pl.BlockSpec(memory_space=pltpu.VMEM)
     sm = pl.BlockSpec(memory_space=pltpu.SMEM)
     far = pl.BlockSpec(memory_space=pltpu.HBM)
@@ -57,7 +57,7 @@
         body,
         out_shape=listed,
         in_specs=[sm] * scalars + [far if hbm else vm] * (len(args) - scalars),
-        out_specs=[far if hbm_out else vm] * len(listed),
+        out_specs=[far if hbm_out is True or i in hbm_out else vm for i in range(len(listed))],
         scratch_shapes=list(scratch),
         compiler_params=pltpu.CompilerParams(vmem_limit_bytes=vmem * 2**20),
         cost_estimate=pl.CostEstimate(flops=0, bytes_accessed=moved, transcendentals=0),
@@ -248,9 +248,9 @@
     tok = total[0:WIDTH, 0:SLICES] * inverse
     cot = total[0:WIDTH, SLICES:128]
     scale = WIDTH ** (-0.5)
-    q = mm(request[...], tok, TN, HI)
-    k = mm(lookup[...], tok, TN, HI)
-    v = mm(content[...], tok, TN, HI)
+    joined = jnp.concatenate([request[...], lookup[...], content[...]], axis=1)
+    qkv = mm(joined, tok, TN, HI)
+    q, k, v = (qkv[i * WIDTH : (i + 1) * WIDTH] for i in range(3))
     scores = mm(k, q, TN, HI) * scale
     e = jnp.exp(scores - jnp.max(scores, axis=0, keepdims=True))
     att = e / jnp.sum(e, axis=0, keepdims=True)
@@ -260,9 +260,7 @@
     g_s = att * (g_att - jnp.sum(att * g_att, axis=0, keepdims=True)) * scale
     g_q = mm(k, g_s, NN, HI)
     g_k = mm(q, g_s, NT, HI)
-    g_tok = mm(request[...], g_q, NN, HI)
-    g_tok = g_tok + mm(lookup[...], g_k, NN, HI)
-    g_tok = g_tok + mm(content[...], g_v, NN, HI)
+    g_tok = mm(joined, jnp.concatenate([g_q, g_k, g_v], axis=0), NN, HI)
     g_num = g_tok * inverse
     g_den = -jnp.sum(g_tok * tok, axis=0, keepdims=True) * inverse
     g_den_hi = g_den.astype(BF16).astype(F32)
@@ -278,7 +276,7 @@
 def backward_kernel(
     mix, spread, soft_col, normed_in, proj_in, prob_in, scaled_in, slice_in,
     uns_in, cot_in, rows_in, heads_in,
-    grads, gproj, deslice_out, weave, stack, gprob, affs,
+    grads_out, gproj, deslice_out, weave, stack, gprob, affs, grads, sem,
 ):
     live = rows_in[0:1, :]
     weave[...] = jnp.zeros_like(weave)
@@ -320,6 +318,23 @@
             grads.dtype
         )
 
+    copies = []
+
+    def write(first, last):
+        span = pl.ds(first, last - first)
+        copy = pltpu.make_async_copy(grads.at[span], grads_out.at[span], sem.at[len(copies)])
+        copy.start()
+        copies.append(copy)
+
+    def write_half(half):
+        in_grad = mm(normed_in[...], gproj[half * C : (half + 1) * C, :], NT)
+        for b in range(2):
+            at = (2 * half + b) * C
+            grads[at : at + C, :] = in_grad[:, b * 128 : (b + 1) * 128].astype(grads.dtype)
+        write(2 * half * C, 2 * (half + 1) * C)
+
+    write(4 * C, 6 * C)
+    write_half(0)
     softs = []
     for h in range(HEADS):
         at = h * SLICES
@@ -340,12 +355,13 @@
         slice_grad = slice_grad + mm(
             proj_in[C + at : C + at + WIDTH, :], affs[h * SLICES : (h + 1) * SLICES, :], NT
         )
-    in_grad = mm(normed_in[...], gproj[...], NT)
-    for b in range(4):
-        grads[b * C : (b + 1) * C, :] = in_grad[:, b * 128 : (b + 1) * 128].astype(grads.dtype)
+    write_half(1)
     tail = jnp.concatenate([slice_grad, jnp.zeros((WIDTH, SLICES), F32)], axis=1)
     grads[6 * C : 6 * C + WIDTH, :] = tail.astype(grads.dtype)
     grads[6 * C + WIDTH :, :] = jnp.zeros((GY * GRAD_ROWS - 6 * C - WIDTH, 128), grads.dtype)
+    write(6 * C, GY * GRAD_ROWS)
+    for copy in copies:
+        copy.wait()
 
 
 def home_kernel(
@@ -496,7 +512,10 @@
             pltpu.VMEM((2 * C + 16, ROWS), BF16),
             pltpu.VMEM((512, ROWS), F32),
             pltpu.VMEM((512, ROWS), BF16),
-        ],
+            pltpu.VMEM((GY * GRAD_ROWS, 128), BF16),
+            pltpu.SemaphoreType.DMA((4,)),
+        ],
+        hbm_out=(0,),
     )
     send = call(
         home_kernel,

time: 138 us -> 138 us (level)
  no operation moved by 1% of the time
where the time goes in v6:
time: 138 us; the launch traced here: 137 us
  blocking collectives  48.5 us (35%)
  waiting for transfers between devices  40.2 us (29%)
  starting transfers between devices  31.4 us (23%)
  Pallas kernels  13.6 us (10%)
  between operations  1.53 us (1%)
  local copies, waits for them, and re-layouts  1.42 us (1%)
    all_to_all x4, blocking collectives, swap(): return lax.all_to_all(x, axes, 0, 0, tiled=True)  48.5 us
    all_to_all x3, waiting for transfers between devices, swap(): return lax.all_to_all(x, axes, 0, 0, tiled=True)  31.5 us
    all_to_all x3, starting transfers between devices, swap(): return lax.all_to_all(x, axes, 0, 0, tiled=True)  22.9 us
    pallas_call x11, Pallas kernels, call(): pl.pallas_call(body, out_shape=listed, in_specs=[sm] * scalars + [far if...  13.6 us
    ppermute x7, waiting for transfers between devices, shifted(): return lax.ppermute(x, axis, [(i, (i + d) % n) for i in range(n)])  8.76 us
    ppermute x7, starting transfers between devices, shifted(): return lax.ppermute(x, axis, [(i, (i + d) % n) for i in range(n)])  8.5 us
  transfers between devices with their start and end apart: 10, of which 7 were waited for; matrix products, arithmetic and copies ran while one was open for 0% of the time, Pallas kernels for 3%

profile of v6, /device:TPU:2, one launch (start us, length us, event | category | flops | bytes accessed | tf_op | source)
XLA Modules:
  0.0 136.8 jit_solution(12890308757224786216)
XLA Ops:
  1.3 2.3 %shard_map.165 = bf16[32,104,128]{2,1,0:T(8,128)(2,1)} custom-call(s32[1]{0:T(128)S(6)} %copy.27.tally, s32[1,8]{1,0:T(1,128)} %plan.1, bf16[8,128,256]{2,1,0:T(8,128)(2,1)} %bitcast.15, bf16[4,128,256]{2,1,0:T(8,128)(2,1)} %bitcast.16), custom_call_target="tpu_custom_call" | custom-call | bytes 1638436 | tf_op jit(solution)/shard_map/pallas_call | solution.py:56
  3.6 0.0 copy-start
  3.6 0.0 copy-start.1
  3.6 0.0 copy-start.10
  3.6 11.8 %all-to-all-start = ((bf16[32,104,128]{2,1,0:T(8,128)(2,1)}), bf16[32,104,128]{2,1,0:T(8,128)(2,1)S(1)}, u32[]{:S(2)}, u32[]{:S(2)}) async-start(bf16[32,104,128]{2,1,0:T(8,128)(2,1)} %shard_map.165), calls=%async_computation | async-start | bytes 1703936 | tf_op jit(solution)/shard_map/all_to_all | solution.py:444
  15.4 0.0 copy-start.7
  15.4 0.0 copy-start.8
  15.4 0.0 copy-start.9
  15.4 0.0 copy-done
  15.5 0.0 copy-done.1
  15.5 0.0 copy-done.10
  15.5 0.6 copy-done.7
  16.1 0.0 copy-done.8
  16.1 0.0 copy-done.9
  16.1 0.5 shard_map.164
  16.6 0.0 copy-start.2
  16.6 0.6 copy-done.2
  17.2 22.0 %all-to-all-done.recv = bf16[32,104,128]{2,1,0:T(8,128)(2,1)S(1)} async-done(((bf16[32,104,128]{2,1,0:T(8,128)(2,1)}), bf16[32,104,128]{2,1,0:T(8,128)(2,1)S(1)}, u32[]{:S(2)}, u32[]{:S(2)}) %all-to-all-start) | async-done | bytes 852000 | tf_op jit(solution)/shard_map/all_to_all | solution.py:444
  39.3 2.6 %shard_map.166 = (bf16[8,40,128]{2,1,0:T(8,128)(2,1)S(1)}, bf16[1024,512]{1,0:T(8,128)(2,1)S(1)}, bf16[256,512]{1,0:T(8,128)(2,1)S(1)}, bf16[256,512]{1,0:T(8,12...) custom-call(s32[1]{0:T(128)} %bitcast.3.spot, ...), custom_call_target="tpu_custom_call" | custom-call | bytes 7024644 | tf_op jit(solution)/shard_map/pallas_call | solution.py:56
  41.9 10.0 %all_to_all.35.recv = bf16[8,40,128]{2,1,0:T(8,128)(2,1)S(1)} all-to-all(bf16[8,40,128]{2,1,0:T(8,128)(2,1)S(1)} %get-tuple-element.46), channel_id=1, replica_groups=mesh['y'=4,'core'=2,'z'=8,'x'=4] {'y','core'}, dimensions={0} | all-to-all | bytes 163840 | tf_op jit(solution)/shard_map/all_to_all | solution.py:444
  51.9 0.0 copy-start.4
  51.9 0.0 copy-start.5
  51.9 0.0 copy-start.6
  51.9 18.0 %all_to_all.36.recv = bf16[32,40,128]{2,1,0:T(8,128)(2,1)S(1)} all-to-all(bf16[32,40,128]{2,1,0:T(8,128)(2,1)S(1)} %shard_map.167), channel_id=1, replica_groups=mesh['y'=4,'core'=2,'z'=8,'x'=4] {'z','x'}, dimensions={0} | all-to-all | bytes 655360 | tf_op jit(solution)/shard_map/all_to_all | solution.py:444
  69.9 0.0 copy-done.4
  69.9 0.0 copy-done.5
  69.9 0.0 copy-done.6
  69.9 1.2 shard_map.168
  71.1 8.2 %all_to_all.37.mix = bf16[8,48,128]{2,1,0:T(8,128)(2,1)S(1)} all-to-all(bf16[8,48,128]{2,1,0:T(8,128)(2,1)S(1)} %shard_map.168), channel_id=1, replica_groups=mesh['y'=4,'core'=2,'z'=8,'x'=4] {'y','core'}, dimensions={0} | all-to-all | bytes 196608 | tf_op jit(solution)/shard_map/all_to_all | solution.py:444
  79.3 2.2 %shard_map.169 = (bf16[1792,128]{1,0:T(8,128)(2,1)}, bf16[512,512]{1,0:T(8,128)(2,1)S(1)}, bf16[256,512]{1,0:T(8,128)(2,1)S(1)}) custom-call(bf16[8,48,128]{2,1,0:T(8,128)(2,1)S(1)} %all_to_all.37.mix, bf16[256,512]{1,0:T(8,128)(2,1)S(1)} %get-tuple-element.39.spread, f32[32,128]{1,0:T(8,128)S(1)} %get-tuple-element.47.soft_col, ...), custom_call_target="tpu_custom_call" | custom-call | bytes 5603328 | tf_op jit(solution)/shard_map/pallas_call | solution.py:56
  81.6 0.0 copy-start.3
  81.6 5.7 %all-to-all-start.4 = ((bf16[32,56,128]{2,1,0:T(8,128)(2,1)}), bf16[32,56,128]{2,1,0:T(8,128)(2,1)S(1)}, u32[]{:S(2)}, u32[]{:S(2)}) async-start(bf16[32,56,128]{2,1,0:T(8,128)(2,1)} %bitcast.6), calls=%async_computation.4 | async-start | bytes 917504 | tf_op jit(solution)/shard_map/all_to_all | solution.py:444
  87.3 0.0 copy-done.3
  87.3 1.9 %shard_map.170 = bf16[32,48,256]{2,1,0:T(8,128)(2,1)} custom-call(bf16[256,512]{1,0:T(8,128)(2,1)S(1)} %copy-done, bf16[256,256]{1,0:T(8,128)(2,1)S(1)} %copy-done.3, f32[256,128]{1,0:T(8,128)S(1)} %get-tuple-element.37.gain_col, bf16[1024,512]{1,0:T(8,128)(2,1)S(1)} %get-tuple-element.42.pick, bf16[256,512]{1,0:T(8,128)(2,1)S(1)} %get-tuple-element.43.xt_in, ...), custom_call_target="tpu_custom_call" | custom-call | bytes 3686400 | tf_op jit(solution)/shard_map/pallas_call | solution.py:56
  89.2 6.7 %all-to-all-done.4.recv = bf16[32,56,128]{2,1,0:T(8,128)(2,1)S(1)} async-done(((bf16[32,56,128]{2,1,0:T(8,128)(2,1)}), bf16[32,56,128]{2,1,0:T(8,128)(2,1)S(1)}, u32[]{:S(2)}, u32[]{:S(2)}) %all-to-all-start.4) | async-done | bytes 458784 | tf_op jit(solution)/shard_map/all_to_all | solution.py:444
  95.9 0.1 shard_map.171
  96.0 12.4 %all_to_all.38.recv = bf16[8,56,128]{2,1,0:T(8,128)(2,1)S(1)} all-to-all(bf16[8,56,128]{2,1,0:T(8,128)(2,1)S(1)} %shard_map.171), channel_id=1, replica_groups=mesh['y'=4,'core'=2,'z'=8,'x'=4] {'z'}, dimensions={0} | all-to-all | bytes 229376 | tf_op jit(solution)/shard_map/all_to_all | solution.py:444
  108.4 5.5 %all-to-all-start.6 = ((bf16[32,48,256]{2,1,0:T(8,128)(2,1)}), bf16[32,48,256]{2,1,0:T(8,128)(2,1)S(1)}, u32[]{:S(2)}, u32[]{:S(2)}) async-start(bf16[32,48,256]{2,1,0:T(8,128)(2,1)} %shard_map.170), calls=%async_computation.6 | async-start | bytes 1572864 | tf_op jit(solution)/shard_map/all_to_all | solution.py:444
  113.8 0.4 collective-permute-start.2
  114.3 2.6 %collective-permute-start.1 = (bf16[1,56,128]{2,1,0:T(8,128)(2,1)S(1)}, bf16[1,56,128]{2,1,0:T(8,128)(2,1)S(1)}, u32[]{:S(2)}, u32[]{:S(2)}) collective-permute-start(bf16[1,56,128]{2,1,0:T(8,128)(2,1)S(1)} %shard_map.172), channel_id=1, source_target_pairs={{0,2},{1,3},{2,0},{3,1},{4,6},{5,7},{6,4},{7,5},{8,10},{9,11},{10,... | collective-permute-start | bytes 43016 | tf_op jit(solution)/shard_map/ppermute | solution.py:447
  116.8 1.8 %collective-permute-start = (bf16[1,56,128]{2,1,0:T(8,128)(2,1)S(1)}, bf16[1,56,128]{2,1,0:T(8,128)(2,1)S(1)}, u32[]{:S(2)}, u32[]{:S(2)}) collective-permute-start(bf16[1,56,128]{2,1,0:T(8,128)(2,1)S(1)} %shard_map.172), channel_id=1, source_target_pairs={{0,1},{1,2},{2,3},{3,0},{4,5},{5,6},{6,7},{7,4},{8,9},{9,10},{10,1... | collective-permute-start | bytes 43016 | tf_op jit(solution)/shard_map/ppermute | solution.py:447
  118.6 2.0 %collective-permute-done = bf16[1,56,128]{2,1,0:T(8,128)(2,1)S(1)} collective-permute-done((bf16[1,56,128]{2,1,0:T(8,128)(2,1)S(1)}, bf16[1,56,128]{2,1,0:T(8,128)(2,1)S(1)}, u32[]{:S(2)}, u32[]{:S(2)}) %collective-permute-start) | collective-permute-done | bytes 14368 | tf_op jit(solution)/shard_map/ppermute | solution.py:447
  120.6 0.0 collective-permute-done.1
  120.6 0.0 collective-permute-done.2
  120.7 0.7 collective-permute-start.3
  121.4 2.6 %collective-permute-start.5 = (bf16[4,56,128]{2,1,0:T(8,128)(2,1)S(1)}, bf16[4,56,128]{2,1,0:T(8,128)(2,1)S(1)}, u32[]{:S(2)}, u32[]{:S(2)}) collective-permute-start(bf16[4,56,128]{2,1,0:T(8,128)(2,1)S(1)} %get-tuple-element.67), channel_id=1, source_target_pairs={{0,192},{64,0},{128,64},{192,128},{1,193},{65,1},{129,65},{193,129... | collective-permute-start | bytes 172040 | tf_op jit(solution)/shard_map/ppermute | solution.py:447
  124.0 0.3 collective-permute-start.4
  124.3 1.9 %collective-permute-done.3 = bf16[4,56,128]{2,1,0:T(8,128)(2,1)S(1)} collective-permute-done((bf16[4,56,128]{2,1,0:T(8,128)(2,1)S(1)}, bf16[4,56,128]{2,1,0:T(8,128)(2,1)S(1)}, u32[]{:S(2)}, u32[]{:S(2)}) %collective-permute-start.3) | collective-permute-done | bytes 57376 | tf_op jit(solution)/shard_map/ppermute | solution.py:447
  126.2 3.5 %collective-permute-done.4 = bf16[4,56,128]{2,1,0:T(8,128)(2,1)S(1)} collective-permute-done((bf16[4,56,128]{2,1,0:T(8,128)(2,1)S(1)}, bf16[4,56,128]{2,1,0:T(8,128)(2,1)S(1)}, u32[]{:S(2)}, u32[]{:S(2)}) %collective-permute-start.4) | collective-permute-done | bytes 57376 | tf_op jit(solution)/shard_map/ppermute | solution.py:447
  129.7 0.0 collective-permute-done.5
  129.7 0.1 collective-permute-start.6
  129.8 0.1 pad_add_fusion.refs_0_
  129.9 1.4 %collective-permute-done.6.refs_2_ = bf16[16,56,128]{2,1,0:T(8,128)(2,1)S(1)} collective-permute-done((bf16[16,56,128]{2,1,0:T(8,128)(2,1)S(1)}, bf16[16,56,128]{2,1,0:T(8,128)(2,1)S(1)}, u32[]{:S(2)}, u32[]{:S(2)}) %collective-permute-start.6) | collective-permute-done | bytes 229408 | tf_op jit(solution)/shard_map/ppermute | solution.py:447
  131.3 1.5 %shard_map.174 = (f32[256,512]{1,0:T(8,128)}, f32[256,256]{1,0:T(8,128)}, f32[32,64]{1,0:T(8,128)}) custom-call(s32[3]{0:T(128)S(1)} %pad_add_fusion.refs_0_, bf16[16,56,128]{2,1,0:T(8,128)(2,1)S(1)} %constant_dynamic-update-slice_fusion.4.refs_1_, bf16[16,56,128]{2,1,0:T(8,128)(2,1)S(1)} %collective-permute-done.6.refs_2_), custom_call_target="tpu_custom_call" | custom-call | bytes 1253388 | tf_op jit(solution)/shard_map/pallas_call | solution.py:56
  132.8 2.8 %all-to-all-done.6.home = bf16[32,48,256]{2,1,0:T(8,128)(2,1)S(1)} async-done(((bf16[32,48,256]{2,1,0:T(8,128)(2,1)}), bf16[32,48,256]{2,1,0:T(8,128)(2,1)S(1)}, u32[]{:S(2)}, u32[]{:S(2)}) %all-to-all-start.6) | async-done | bytes 786464 | tf_op jit(solution)/shard_map/all_to_all | solution.py:444
  135.6 1.1 shard_map.173
  (9 shorter events, 0.1 us)
Async XLA Ops:
  3.6 11.8 %copy-start = (bf16[256,512]{1,0:T(8,128)(2,1)S(1)}, bf16[256,512]{1,0:T(8,128)(2,1)}, u32[]{:S(2)}) copy-start(bf16[256,512]{1,0:T(8,128)(2,1)} %entrance.3) | copy-start | bytes 786436
  3.6 11.8 %copy-start.1 = (bf16[256,256]{1,0:T(8,128)(2,1)S(1)}, bf16[256,256]{1,0:T(8,128)(2,1)}, u32[]{:S(2)}) copy-start(bf16[256,256]{1,0:T(8,128)(2,1)} %exit_w.3) | copy-start | bytes 393220
  3.6 11.8 %copy-start.10 = (f32[8]{0:T(128)S(1)}, f32[8]{0:T(128)}, u32[]{:S(2)}) copy-start(f32[8]{0:T(128)} %param.21) | copy-start | bytes 100
  3.6 35.6 %all-to-all-start = ((bf16[32,104,128]{2,1,0:T(8,128)(2,1)}), bf16[32,104,128]{2,1,0:T(8,128)(2,1)S(1)}, u32[]{:S(2)}, u32[]{:S(2)}) async-start(bf16[32,104,128]{2,1,0:T(8,128)(2,1)} %shard_map.165), calls=%async_computation | async-start | bytes 1703936 | tf_op jit(solution)/shard_map/all_to_all | solution.py:444
  15.4 0.7 copy-start.7
  15.4 0.7 copy-start.8
  15.4 0.7 copy-start.9
  16.6 0.7 copy-start.2
  51.9 18.0 %copy-start.4 = (f32[32,32]{1,0:T(8,128)S(1)}, f32[32,32]{1,0:T(8,128)}, u32[]{:S(2)}) copy-start(f32[32,32]{1,0:T(8,128)} %request.1) | copy-start | bytes 12292
  51.9 18.0 %copy-start.5 = (f32[32,32]{1,0:T(8,128)S(1)}, f32[32,32]{1,0:T(8,128)}, u32[]{:S(2)}) copy-start(f32[32,32]{1,0:T(8,128)} %lookup.1) | copy-start | bytes 12292
  51.9 18.0 %copy-start.6 = (f32[32,32]{1,0:T(8,128)S(1)}, f32[32,32]{1,0:T(8,128)}, u32[]{:S(2)}) copy-start(f32[32,32]{1,0:T(8,128)} %content.1) | copy-start | bytes 12292
  81.6 5.7 %copy-start.3 = (bf16[256,256]{1,0:T(8,128)(2,1)S(1)}, bf16[256,256]{1,0:T(8,128)(2,1)}, u32[]{:S(2)}) copy-start(bf16[256,256]{1,0:T(8,128)(2,1)} %copy-done.2) | copy-start | bytes 393220
  81.6 14.3 %all-to-all-start.4 = ((bf16[32,56,128]{2,1,0:T(8,128)(2,1)}), bf16[32,56,128]{2,1,0:T(8,128)(2,1)S(1)}, u32[]{:S(2)}, u32[]{:S(2)}) async-start(bf16[32,56,128]{2,1,0:T(8,128)(2,1)} %bitcast.6), calls=%async_computation.4 | async-start | bytes 917504 | tf_op jit(solution)/shard_map/all_to_all | solution.py:444
  108.4 27.3 %all-to-all-start.6 = ((bf16[32,48,256]{2,1,0:T(8,128)(2,1)}), bf16[32,48,256]{2,1,0:T(8,128)(2,1)S(1)}, u32[]{:S(2)}, u32[]{:S(2)}) async-start(bf16[32,48,256]{2,1,0:T(8,128)(2,1)} %shard_map.170), calls=%async_computation.6 | async-start | bytes 1572864 | tf_op jit(solution)/shard_map/all_to_all | solution.py:444
  113.8 6.8 %collective-permute-start.2 = (bf16[1,56,128]{2,1,0:T(8,128)(2,1)S(1)}, bf16[1,56,128]{2,1,0:T(8,128)(2,1)S(1)}, u32[]{:S(2)}, u32[]{:S(2)}) collective-permute-start(bf16[1,56,128]{2,1,0:T(8,128)(2,1)S(1)} %shard_map.172), channel_id=1, source_target_pairs={{0,3},{1,0},{2,1},{3,2},{4,7},{5,4},{6,5},{7,6},{8,11},{9,8},{10,9... | collective-permute-start | bytes 43016 | tf_op jit(solution)/shard_map/ppermute | solution.py:447
  114.3 6.4 %collective-permute-start.1 = (bf16[1,56,128]{2,1,0:T(8,128)(2,1)S(1)}, bf16[1,56,128]{2,1,0:T(8,128)(2,1)S(1)}, u32[]{:S(2)}, u32[]{:S(2)}) collective-permute-start(bf16[1,56,128]{2,1,0:T(8,128)(2,1)S(1)} %shard_map.172), channel_id=1, source_target_pairs={{0,2},{1,3},{2,0},{3,1},{4,6},{5,7},{6,4},{7,5},{8,10},{9,11},{10,... | collective-permute-start | bytes 43016 | tf_op jit(solution)/shard_map/ppermute | solution.py:447
  116.8 3.8 %collective-permute-start = (bf16[1,56,128]{2,1,0:T(8,128)(2,1)S(1)}, bf16[1,56,128]{2,1,0:T(8,128)(2,1)S(1)}, u32[]{:S(2)}, u32[]{:S(2)}) collective-permute-start(bf16[1,56,128]{2,1,0:T(8,128)(2,1)S(1)} %shard_map.172), channel_id=1, source_target_pairs={{0,1},{1,2},{2,3},{3,0},{4,5},{5,6},{6,7},{7,4},{8,9},{9,10},{10,1... | collective-permute-start | bytes 43016 | tf_op jit(solution)/shard_map/ppermute | solution.py:447
  120.7 5.5 %collective-permute-start.3 = (bf16[4,56,128]{2,1,0:T(8,128)(2,1)S(1)}, bf16[4,56,128]{2,1,0:T(8,128)(2,1)S(1)}, u32[]{:S(2)}, u32[]{:S(2)}) collective-permute-start(bf16[4,56,128]{2,1,0:T(8,128)(2,1)S(1)} %get-tuple-element.67), channel_id=1, source_target_pairs={{0,64},{64,128},{128,192},{192,0},{1,65},{65,129},{129,193},{193,1... | collective-permute-start | bytes 172040 | tf_op jit(solution)/shard_map/ppermute | solution.py:447
  121.4 8.3 %collective-permute-start.5 = (bf16[4,56,128]{2,1,0:T(8,128)(2,1)S(1)}, bf16[4,56,128]{2,1,0:T(8,128)(2,1)S(1)}, u32[]{:S(2)}, u32[]{:S(2)}) collective-permute-start(bf16[4,56,128]{2,1,0:T(8,128)(2,1)S(1)} %get-tuple-element.67), channel_id=1, source_target_pairs={{0,192},{64,0},{128,64},{192,128},{1,193},{65,1},{129,65},{193,129... | collective-permute-start | bytes 172040 | tf_op jit(solution)/shard_map/ppermute | solution.py:447
  124.0 5.7 %collective-permute-start.4 = (bf16[4,56,128]{2,1,0:T(8,128)(2,1)S(1)}, bf16[4,56,128]{2,1,0:T(8,128)(2,1)S(1)}, u32[]{:S(2)}, u32[]{:S(2)}) collective-permute-start(bf16[4,56,128]{2,1,0:T(8,128)(2,1)S(1)} %get-tuple-element.67), channel_id=1, source_target_pairs={{0,128},{64,192},{128,0},{192,64},{1,129},{65,193},{129,1},{193,65... | collective-permute-start | bytes 172040 | tf_op jit(solution)/shard_map/ppermute | solution.py:447
  129.7 1.6 %collective-permute-start.6 = (bf16[16,56,128]{2,1,0:T(8,128)(2,1)S(1)}, bf16[16,56,128]{2,1,0:T(8,128)(2,1)S(1)}, u32[]{:S(2)}, u32[]{:S(2)}) collective-permute-start(bf16[16,56,128]{2,1,0:T(8,128)(2,1)S(1)} %constant_dynamic-update-slice_fusion.4.refs_1_), channel_id=1, source_target_pairs={{0,32},{32,0},{1,33},{33,1},{2,34},{34,2},{3,35},{35,3},{4,36},{36... | collective-permute-start | bytes 688136 | tf_op jit(solution)/shard_map/ppermute | solution.py:447

commit v7 on v3

--- a/solution.py
+++ b/solution.py
@@ -87,26 +87,8 @@
     return (source == kept).astype(F32).astype(BF16)
 
 
-def pack_kernel(tally_hbm, plan_hbm, cells, cot, out, tally, plan, rows, sent, small_sem, in_sem, out_sem):
-    small = [
-        pltpu.make_async_copy(tally_hbm, tally, small_sem.at[0]),
-        pltpu.make_async_copy(plan_hbm, plan, small_sem.at[1]),
-    ]
-    for copy in small:
-        copy.start()
-    reads = []
-    for j in range(8):
-        at = pl.ds(16 * j, 16)
-        pair = [
-            pltpu.make_async_copy(cells.at[:, at, :], rows.at[j, 0:SIN], in_sem.at[j, 0]),
-            pltpu.make_async_copy(cot.at[:, at, :], rows.at[j, SIN : SIN + SOUT], in_sem.at[j, 1]),
-        ]
-        for copy in pair:
-            copy.start()
-        reads.append(pair)
+def pack_kernel(tally, plan, cells, cot, out, sent, out_sem):
     order = piece_order(False)
-    for copy in small:
-        copy.wait()
     block = iota((META, 128), 1) >> 2
     target = jnp.zeros((META, 128), jnp.int32)
     for s in range(SIN):
@@ -117,9 +99,9 @@
         sent[j, 2 * SEND : TALL, :] = meta
     writes = []
     for j in range(8):
-        for copy in reads[j]:
-            copy.wait()
-        moved = mm(order, rows[j].reshape(GROUP, C)).astype(BF16)
+        at = slice(16 * j, 16 * j + 16)
+        rows = [cells[:, at, :].reshape(16 * SIN, C), cot[:, at, :].reshape(16 * SOUT, C)]
+        moved = mm(order, jnp.concatenate(rows, axis=0)).astype(BF16)
         for a in range(4):
             part = moved[a * SEND : (a + 1) * SEND]
             sent[4 * j + a, 0:SEND, :] = part[:, 0:128]
@@ -448,16 +430,11 @@
         pack_kernel,
         sds((GY, TALL, 128), BF16),
         tally, plan, cells.reshape(SIN, BLK, C), cot.reshape(SOUT, BLK, C),
-        hbm=True,
+        scalars=2,
         hbm_out=True,
         vmem=62,
         scratch=[
-            pltpu.SMEM((1,), jnp.int32),
-            pltpu.SMEM((1, SIN), jnp.int32),
-            pltpu.VMEM((8, SIN + SOUT, 16, C), BF16),
             pltpu.VMEM((GY, TALL, 128), BF16),
-            pltpu.SemaphoreType.DMA((2,)),
-            pltpu.SemaphoreType.DMA((8, 2)),
             pltpu.SemaphoreType.DMA((8,)),
         ],
     )

time: 139 us -> 138 us (level)
  no operation moved by 1% of the time
where the time goes in v7:
time: 138 us
  blocking collectives  62.5 us (45%)
  waiting for transfers between devices  35.5 us (26%)
  starting transfers between devices  24.5 us (18%)
  Pallas kernels  12.8 us (9%)
  between operations  1.47 us (1%)
    all_to_all x5, blocking collectives, swap(): return lax.all_to_all(x, axes, 0, 0, tiled=True)  62.5 us
    all_to_all x2, waiting for transfers between devices, swap(): return lax.all_to_all(x, axes, 0, 0, tiled=True)  23.2 us
    all_to_all x2, starting transfers between devices, swap(): return lax.all_to_all(x, axes, 0, 0, tiled=True)  17.2 us
    pallas_call x10, Pallas kernels, call(): pl.pallas_call(body, out_shape=listed, in_specs=[sm] * scalars + [far if...  12.8 us
    ppermute x7, waiting for transfers between devices, shifted(): return lax.ppermute(x, axis, [(i, (i + d) % n) for i in range(n)])  12.3 us
    ppermute x7, starting transfers between devices, shifted(): return lax.ppermute(x, axis, [(i, (i + d) % n) for i in range(n)])  7.29 us
  transfers between devices with their start and end apart: 9, of which 8 were waited for; matrix products, arithmetic and copies ran while one was open for 0% of the time, Pallas kernels for 1%

profile of v7, /device:TPU:2, one launch (start us, length us, event | category | flops | bytes accessed | tf_op | source)
XLA Modules:
  0.0 137.5 jit_solution(16759967486817086637)
XLA Ops:
  1.3 2.3 %shard_map.164 = bf16[32,104,128]{2,1,0:T(8,128)(2,1)} custom-call(s32[1]{0:T(128)S(6)} %copy.23.tally, s32[1,8]{1,0:T(1,128)} %plan.1, bf16[8,128,256]{2,1,0:T(8,128)(2,1)} %bitcast.16, bf16[4,128,256]{2,1,0:T(8,128)(2,1)} %bitcast.17), custom_call_target="tpu_custom_call" | custom-call | bytes 1638436 | tf_op jit(solution)/shard_map/pallas_call | solution.py:56
  3.6 0.0 copy-start
  3.6 0.0 copy-start.1
  3.6 0.0 copy-start.8
  3.6 11.8 %all-to-all-start = ((bf16[32,104,128]{2,1,0:T(8,128)(2,1)}), bf16[32,104,128]{2,1,0:T(8,128)(2,1)S(1)}, u32[]{:S(2)}, u32[]{:S(2)}) async-start(bf16[32,104,128]{2,1,0:T(8,128)(2,1)} %shard_map.164), calls=%async_computation | async-start | bytes 1703936 | tf_op jit(solution)/shard_map/all_to_all | solution.py:424
  15.4 0.0 copy-start.5
  15.4 0.0 copy-start.6
  15.4 0.0 copy-start.7
  15.5 0.0 copy-done
  15.5 0.0 copy-done.1
  15.5 0.0 copy-done.8
  15.5 0.6 copy-done.5
  16.1 0.0 copy-done.6
  16.1 0.0 copy-done.7
  16.1 0.5 shard_map.165
  16.6 22.7 %all-to-all-done.recv = bf16[32,104,128]{2,1,0:T(8,128)(2,1)S(1)} async-done(((bf16[32,104,128]{2,1,0:T(8,128)(2,1)}), bf16[32,104,128]{2,1,0:T(8,128)(2,1)S(1)}, u32[]{:S(2)}, u32[]{:S(2)}) %all-to-all-start) | async-done | bytes 852000 | tf_op jit(solution)/shard_map/all_to_all | solution.py:424
  39.3 2.6 %shard_map.166 = (bf16[8,40,128]{2,1,0:T(8,128)(2,1)S(1)}, bf16[1024,512]{1,0:T(8,128)(2,1)S(1)}, bf16[256,512]{1,0:T(8,128)(2,1)S(1)}, bf16[256,512]{1,0:T(8,12...) custom-call(s32[1]{0:T(128)} %bitcast.spot, ...), custom_call_target="tpu_custom_call" | custom-call | bytes 7024644 | tf_op jit(solution)/shard_map/pallas_call | solution.py:56
  41.9 10.0 %all_to_all.35.recv = bf16[8,40,128]{2,1,0:T(8,128)(2,1)S(1)} all-to-all(bf16[8,40,128]{2,1,0:T(8,128)(2,1)S(1)} %get-tuple-element.38), channel_id=1, replica_groups=mesh['y'=4,'core'=2,'z'=8,'x'=4] {'y','core'}, dimensions={0} | all-to-all | bytes 163840 | tf_op jit(solution)/shard_map/all_to_all | solution.py:424
  51.9 0.0 copy-start.2
  51.9 0.0 copy-start.3
  51.9 0.0 copy-start.4
  52.0 18.0 %all_to_all.36.recv = bf16[32,40,128]{2,1,0:T(8,128)(2,1)S(1)} all-to-all(bf16[32,40,128]{2,1,0:T(8,128)(2,1)S(1)} %shard_map.167), channel_id=1, replica_groups=mesh['y'=4,'core'=2,'z'=8,'x'=4] {'z','x'}, dimensions={0} | all-to-all | bytes 655360 | tf_op jit(solution)/shard_map/all_to_all | solution.py:424
  69.9 0.0 copy-done.2
  70.0 0.0 copy-done.3
  70.0 0.0 copy-done.4
  70.0 1.2 shard_map.168
  71.1 8.2 %all_to_all.37.mix = bf16[8,48,128]{2,1,0:T(8,128)(2,1)S(1)} all-to-all(bf16[8,48,128]{2,1,0:T(8,128)(2,1)S(1)} %shard_map.168), channel_id=1, replica_groups=mesh['y'=4,'core'=2,'z'=8,'x'=4] {'y','core'}, dimensions={0} | all-to-all | bytes 196608 | tf_op jit(solution)/shard_map/all_to_all | solution.py:424
  79.3 3.4 %shard_map.169 = (bf16[32,48,256]{2,1,0:T(8,128)(2,1)}, bf16[1792,128]{1,0:T(8,128)(2,1)S(1)}) custom-call(bf16[8,48,128]{2,1,0:T(8,128)(2,1)S(1)} %all_to_all.37.mix, bf16[256,512]{1,0:T(8,128)(2,1)S(1)} %copy-done, bf16[256,256]{1,0:T(8,128)(2,1)S(1)} %get-tuple-element.39.exit_t, bf16[256,512]{1,0:T(8,128)(2,1)S(1)} %get-tuple-element.34.spread, ...), custom_call_target="tpu_custom_call" | custom-call | bytes 7438336 | tf_op jit(solution)/shard_map/pallas_call | solution.py:56
  82.7 14.0 %all_to_all.38.recv = bf16[32,56,128]{2,1,0:T(8,128)(2,1)S(1)} all-to-all(bf16[32,56,128]{2,1,0:T(8,128)(2,1)S(1)} %bitcast.12), channel_id=1, replica_groups=mesh['y'=4,'core'=2,'z'=8,'x'=4] {'y','core','x'}, dimensions={0} | all-to-all | bytes 917504 | tf_op jit(solution)/shard_map/all_to_all | solution.py:424
  96.6 0.1 shard_map.170
  96.7 12.4 %all_to_all.39.recv = bf16[8,56,128]{2,1,0:T(8,128)(2,1)S(1)} all-to-all(bf16[8,56,128]{2,1,0:T(8,128)(2,1)S(1)} %shard_map.170), channel_id=1, replica_groups=mesh['y'=4,'core'=2,'z'=8,'x'=4] {'z'}, dimensions={0} | all-to-all | bytes 229376 | tf_op jit(solution)/shard_map/all_to_all | solution.py:424
  109.1 5.5 %all-to-all-start.6 = ((bf16[32,48,256]{2,1,0:T(8,128)(2,1)}), bf16[32,48,256]{2,1,0:T(8,128)(2,1)S(1)}, u32[]{:S(2)}, u32[]{:S(2)}) async-start(bf16[32,48,256]{2,1,0:T(8,128)(2,1)} %get-tuple-element.54), calls=%async_computation.6 | async-start | bytes 1572864 | tf_op jit(solution)/shard_map/all_to_all | solution.py:424
  114.6 0.1 collective-permute-start
  114.7 1.2 collective-permute-done
  115.9 1.5 %collective-permute-start.1 = (bf16[2,56,128]{2,1,0:T(8,128)(2,1)S(1)}, bf16[2,56,128]{2,1,0:T(8,128)(2,1)S(1)}, u32[]{:S(2)}, u32[]{:S(2)}) collective-permute-start(bf16[2,56,128]{2,1,0:T(8,128)(2,1)S(1)} %get-tuple-element.61), channel_id=1, source_target_pairs={{0,1},{1,2},{2,3},{3,0},{4,5},{5,6},{6,7},{7,4},{8,9},{9,10},{10,1... | collective-permute-start | bytes 86024 | tf_op jit(solution)/shard_map/ppermute | solution.py:427
  117.4 0.6 collective-permute-start.3
  118.0 2.1 %collective-permute-start.2 = (bf16[2,56,128]{2,1,0:T(8,128)(2,1)S(1)}, bf16[2,56,128]{2,1,0:T(8,128)(2,1)S(1)}, u32[]{:S(2)}, u32[]{:S(2)}) collective-permute-start(bf16[2,56,128]{2,1,0:T(8,128)(2,1)S(1)} %get-tuple-element.61), channel_id=1, source_target_pairs={{0,2},{1,3},{2,0},{3,1},{4,6},{5,7},{6,4},{7,5},{8,10},{9,11},{10,... | collective-permute-start | bytes 86024 | tf_op jit(solution)/shard_map/ppermute | solution.py:427
  120.0 0.4 collective-permute-done.1
  120.4 4.8 %collective-permute-done.2 = bf16[2,56,128]{2,1,0:T(8,128)(2,1)S(1)} collective-permute-done((bf16[2,56,128]{2,1,0:T(8,128)(2,1)S(1)}, bf16[2,56,128]{2,1,0:T(8,128)(2,1)S(1)}, u32[]{:S(2)}, u32[]{:S(2)}) %collective-permute-start.2) | collective-permute-done | bytes 28704 | tf_op jit(solution)/shard_map/ppermute | solution.py:427
  125.2 0.0 collective-permute-done.3
  125.3 1.2 collective-permute-start.6
  126.5 1.8 %collective-permute-start.5 = (bf16[8,56,128]{2,1,0:T(8,128)(2,1)S(1)}, bf16[8,56,128]{2,1,0:T(8,128)(2,1)S(1)}, u32[]{:S(2)}, u32[]{:S(2)}) collective-permute-start(bf16[8,56,128]{2,1,0:T(8,128)(2,1)S(1)} %constant_dynamic-update-slice_fusion.2.refs_1_), channel_id=1, source_target_pairs={{0,128},{64,192},{128,0},{192,64},{1,129},{65,193},{129,1},{193,65... | collective-permute-start | bytes 344072 | tf_op jit(solution)/shard_map/ppermute | solution.py:427
  128.3 0.0 collective-permute-start.4
  128.3 0.1 pad_add_fusion.refs_0_
  128.4 1.8 %collective-permute-done.6.refs_4_ = bf16[8,56,128]{2,1,0:T(8,128)(2,1)S(1)} collective-permute-done((bf16[8,56,128]{2,1,0:T(8,128)(2,1)S(1)}, bf16[8,56,128]{2,1,0:T(8,128)(2,1)S(1)}, u32[]{:S(2)}, u32[]{:S(2)}) %collective-permute-start.6) | collective-permute-done | bytes 114720 | tf_op jit(solution)/shard_map/ppermute | solution.py:427
  130.1 2.7 %collective-permute-done.5.refs_3_ = bf16[8,56,128]{2,1,0:T(8,128)(2,1)S(1)} collective-permute-done((bf16[8,56,128]{2,1,0:T(8,128)(2,1)S(1)}, bf16[8,56,128]{2,1,0:T(8,128)(2,1)S(1)}, u32[]{:S(2)}, u32[]{:S(2)}) %collective-permute-start.5) | collective-permute-done | bytes 114720 | tf_op jit(solution)/shard_map/ppermute | solution.py:427
  132.8 1.5 %collective-permute-done.4.refs_2_ = bf16[8,56,128]{2,1,0:T(8,128)(2,1)S(1)} collective-permute-done((bf16[8,56,128]{2,1,0:T(8,128)(2,1)S(1)}, bf16[8,56,128]{2,1,0:T(8,128)(2,1)S(1)}, u32[]{:S(2)}, u32[]{:S(2)}) %collective-permute-start.4) | collective-permute-done | bytes 114720 | tf_op jit(solution)/shard_map/ppermute | solution.py:427
  134.3 1.5 %shard_map.173 = (f32[256,512]{1,0:T(8,128)}, f32[256,256]{1,0:T(8,128)}, f32[32,64]{1,0:T(8,128)}) custom-call(s32[3]{0:T(128)S(1)} %pad_add_fusion.refs_0_, bf16[8,56,128]{2,1,0:T(8,128)(2,1)S(1)} %constant_dynamic-update-slice_fusion.2.refs_1_, bf16[8,56,128]{2,1,0:T(8,128)(2,1)S(1)} %collective-permute-done.4.refs_2_, ...), custom_call_target="tpu_custom_call" | custom-call | bytes 1253388 | tf_op jit(solution)/shard_map/pallas_call | solution.py:56
  135.8 0.6 all-to-all-done.6.home
  136.4 1.1 shard_map.172
  (7 shorter events, 0.1 us)
Async XLA Ops:
  3.6 11.8 %copy-start = (bf16[256,512]{1,0:T(8,128)(2,1)S(1)}, bf16[256,512]{1,0:T(8,128)(2,1)}, u32[]{:S(2)}) copy-start(bf16[256,512]{1,0:T(8,128)(2,1)} %entrance.3) | copy-start | bytes 786436
  3.6 11.8 %copy-start.1 = (bf16[256,256]{1,0:T(8,128)(2,1)S(1)}, bf16[256,256]{1,0:T(8,128)(2,1)}, u32[]{:S(2)}) copy-start(bf16[256,256]{1,0:T(8,128)(2,1)} %exit_w.3) | copy-start | bytes 393220
  3.6 11.8 %copy-start.8 = (f32[8]{0:T(128)S(1)}, f32[8]{0:T(128)}, u32[]{:S(2)}) copy-start(f32[8]{0:T(128)} %param.21) | copy-start | bytes 100
  3.6 35.6 %all-to-all-start = ((bf16[32,104,128]{2,1,0:T(8,128)(2,1)}), bf16[32,104,128]{2,1,0:T(8,128)(2,1)S(1)}, u32[]{:S(2)}, u32[]{:S(2)}) async-start(bf16[32,104,128]{2,1,0:T(8,128)(2,1)} %shard_map.164), calls=%async_computation | async-start | bytes 1703936 | tf_op jit(solution)/shard_map/all_to_all | solution.py:424
  15.4 0.7 copy-start.5
  15.4 0.7 copy-start.6
  15.4 0.7 copy-start.7
  51.9 18.0 %copy-start.2 = (f32[32,32]{1,0:T(8,128)S(1)}, f32[32,32]{1,0:T(8,128)}, u32[]{:S(2)}) copy-start(f32[32,32]{1,0:T(8,128)} %request.1) | copy-start | bytes 12292
  51.9 18.0 %copy-start.3 = (f32[32,32]{1,0:T(8,128)S(1)}, f32[32,32]{1,0:T(8,128)}, u32[]{:S(2)}) copy-start(f32[32,32]{1,0:T(8,128)} %lookup.1) | copy-start | bytes 12292
  51.9 18.0 %copy-start.4 = (f32[32,32]{1,0:T(8,128)S(1)}, f32[32,32]{1,0:T(8,128)}, u32[]{:S(2)}) copy-start(f32[32,32]{1,0:T(8,128)} %content.1) | copy-start | bytes 12292
  109.1 27.3 %all-to-all-start.6 = ((bf16[32,48,256]{2,1,0:T(8,128)(2,1)}), bf16[32,48,256]{2,1,0:T(8,128)(2,1)S(1)}, u32[]{:S(2)}, u32[]{:S(2)}) async-start(bf16[32,48,256]{2,1,0:T(8,128)(2,1)} %get-tuple-element.54), calls=%async_computation.6 | async-start | bytes 1572864 | tf_op jit(solution)/shard_map/all_to_all | solution.py:424
  114.6 1.3 collective-permute-start
  115.9 4.5 %collective-permute-start.1 = (bf16[2,56,128]{2,1,0:T(8,128)(2,1)S(1)}, bf16[2,56,128]{2,1,0:T(8,128)(2,1)S(1)}, u32[]{:S(2)}, u32[]{:S(2)}) collective-permute-start(bf16[2,56,128]{2,1,0:T(8,128)(2,1)S(1)} %get-tuple-element.61), channel_id=1, source_target_pairs={{0,1},{1,2},{2,3},{3,0},{4,5},{5,6},{6,7},{7,4},{8,9},{9,10},{10,1... | collective-permute-start | bytes 86024 | tf_op jit(solution)/shard_map/ppermute | solution.py:427
  117.4 7.8 %collective-permute-start.3 = (bf16[2,56,128]{2,1,0:T(8,128)(2,1)S(1)}, bf16[2,56,128]{2,1,0:T(8,128)(2,1)S(1)}, u32[]{:S(2)}, u32[]{:S(2)}) collective-permute-start(bf16[2,56,128]{2,1,0:T(8,128)(2,1)S(1)} %get-tuple-element.61), channel_id=1, source_target_pairs={{0,3},{1,0},{2,1},{3,2},{4,7},{5,4},{6,5},{7,6},{8,11},{9,8},{10,9... | collective-permute-start | bytes 86024 | tf_op jit(solution)/shard_map/ppermute | solution.py:427
  118.0 7.3 %collective-permute-start.2 = (bf16[2,56,128]{2,1,0:T(8,128)(2,1)S(1)}, bf16[2,56,128]{2,1,0:T(8,128)(2,1)S(1)}, u32[]{:S(2)}, u32[]{:S(2)}) collective-permute-start(bf16[2,56,128]{2,1,0:T(8,128)(2,1)S(1)} %get-tuple-element.61), channel_id=1, source_target_pairs={{0,2},{1,3},{2,0},{3,1},{4,6},{5,7},{6,4},{7,5},{8,10},{9,11},{10,... | collective-permute-start | bytes 86024 | tf_op jit(solution)/shard_map/ppermute | solution.py:427
  125.3 4.9 %collective-permute-start.6 = (bf16[8,56,128]{2,1,0:T(8,128)(2,1)S(1)}, bf16[8,56,128]{2,1,0:T(8,128)(2,1)S(1)}, u32[]{:S(2)}, u32[]{:S(2)}) collective-permute-start(bf16[8,56,128]{2,1,0:T(8,128)(2,1)S(1)} %constant_dynamic-update-slice_fusion.2.refs_1_), channel_id=1, source_target_pairs={{0,192},{64,0},{128,64},{192,128},{1,193},{65,1},{129,65},{193,129... | collective-permute-start | bytes 344072 | tf_op jit(solution)/shard_map/ppermute | solution.py:427
  126.5 6.3 %collective-permute-start.5 = (bf16[8,56,128]{2,1,0:T(8,128)(2,1)S(1)}, bf16[8,56,128]{2,1,0:T(8,128)(2,1)S(1)}, u32[]{:S(2)}, u32[]{:S(2)}) collective-permute-start(bf16[8,56,128]{2,1,0:T(8,128)(2,1)S(1)} %constant_dynamic-update-slice_fusion.2.refs_1_), channel_id=1, source_target_pairs={{0,128},{64,192},{128,0},{192,64},{1,129},{65,193},{129,1},{193,65... | collective-permute-start | bytes 344072 | tf_op jit(solution)/shard_map/ppermute | solution.py:427
  128.3 6.0 %collective-permute-start.4 = (bf16[8,56,128]{2,1,0:T(8,128)(2,1)S(1)}, bf16[8,56,128]{2,1,0:T(8,128)(2,1)S(1)}, u32[]{:S(2)}, u32[]{:S(2)}) collective-permute-start(bf16[8,56,128]{2,1,0:T(8,128)(2,1)S(1)} %constant_dynamic-update-slice_fusion.2.refs_1_), channel_id=1, source_target_pairs={{0,64},{64,128},{128,192},{192,0},{1,65},{65,129},{129,193},{193,1... | collective-permute-start | bytes 344072 | tf_op jit(solution)/shard_map/ppermute | solution.py:427
